TPU v7x, 128 devices: a whole 4x4x4 slice. The times are simulated.
128 devices in a mesh: slab: 8 (over y_hi, z), view: 16 (over y_lo, x, core).
Axes of the slice: x: 4, y: 4 (y_hi: 2, y_lo: 2; y = y_hi * 2 + y_lo), z: 4, core: 2. Of those that a mesh axis runs over, the one named last changes fastest.
Arguments:
- volume: float32 [512, 65536], P('slab', 'view'), may hold values from 0 to 2
- sino: float32 [16, 128, 2048], P('view', 'slab'), may hold values from -6 to 6
- transaxial: bfloat16 [16, 256, 256, 256], P('view'), may hold values from -0.0625 to 0.0625
- blocks: int32 [16, 256], P('view'), may hold values from 0 to 7
- axial: bfloat16 [16, 512, 32], P('view', 'slab'), may hold values from -0.5 to 0.5
- band_start: int32 [16, 8], P('view', 'slab'), may hold values from 0 to 96, as said below
- band_len: int32 [16, 8], P('view', 'slab'), may hold values from 16 to 32, as said below
- row_weight: float32 [16, 128, 2048], P('view', 'slab'), may hold values from 0.25 to 2
- col_weight: float32 [512, 65536], P('slab', 'view'), may hold values from 0.25 to 1
Outputs:
- updated: float32 [512, 65536], P('slab', 'view')
- residual: float32 [16, 128, 2048], P('view', 'slab')
Inputs may be any that keep to these rules, and one draw needn't show every extreme that they name: (s - 1) * 16 <= band_start[v, s] <= s * 16 for every slab s, band_start[v, 0] = 0, band_start[v, s] + band_len[v, s] <= min((s + 2) * 16, 128). In every view some slab has band_len = 32.
All inputs are finite; a program needn't handle non-finite values.
Results may differ from a plain program's by a relative error of at most 0.0019.
Values may be sent and summed in bfloat16 or wider, within the bound.
No kernel may reach another device: no remote copies, remote signals or barrier semaphores. Data moves between devices by JAX's collectives and lax.ppermute only.
A program may use at most 192 MiB of HBM per device.

v0:
```python
import jax
import jax.numpy as jnp
from jax import lax
from jax.sharding import PartitionSpec as P

HIGH = lax.Precision.HIGHEST


def shifted(x, axis, by):
    size = lax.axis_size(axis)
    pairs = [(i, i + by) for i in range(size) if 0 <= i + by < size]
    return lax.ppermute(x, axis, pairs)


def padded(block, sides, width):
    for axis, dim in sides:
        count = lax.axis_size(axis)
        forward = [(i, i + 1) for i in range(count - 1)]
        backward = [(target, source) for source, target in forward]
        low = lax.ppermute(
            lax.slice_in_dim(block, block.shape[dim] - width, None, axis=dim), axis, forward
        )
        high = lax.ppermute(lax.slice_in_dim(block, 0, width, axis=dim), axis, backward)
        block = jnp.concatenate([low, block, high], axis=dim)
    return block


def per_device(
    volume, sino, transaxial, blocks, axial, band_start, band_len, row_weight, col_weight
):
    planes, pixels = volume.shape
    views_here, tile_total, tile_width, block_width = transaxial.shape
    rows_here = sino.shape[1]
    col_total = sino.shape[2]
    col_blocks = col_total // block_width
    band_rows = axial.shape[2]
    tiles_here = pixels // tile_width
    selector = blocks[:, :, None] == jnp.arange(col_blocks, dtype=jnp.int32)[None, None, :]
    select_float = selector.astype(jnp.float32)
    select_half = selector.astype(jnp.bfloat16)
    packed = volume.astype(jnp.bfloat16).reshape(planes, tiles_here, tile_width)
    weights = transaxial
    per_tile = jnp.einsum(
        "zti,vtik->vtzk",
        lax.all_gather(packed, "view", axis=1, tiled=True),
        weights,
        preferred_element_type=jnp.float32,
    )
    projected = jnp.einsum("vtc,vtzk->vzck", select_float, per_tile, precision=HIGH)
    projected = projected.reshape(views_here, planes, col_total)
    live_rows = (jnp.arange(band_rows, dtype=jnp.int32)[None, :] < band_len).astype(jnp.float32)
    masked = axial.astype(jnp.float32) * live_rows[:, None, :]
    band_proj = jnp.einsum("vzj,vzu->vju", masked, projected, precision=HIGH)
    first_row = band_start[:, 0]
    window_base = (lax.axis_index("slab") - 1) * rows_here
    local_first = first_row - window_base
    placing = (
        local_first[:, None, None] + jnp.arange(band_rows, dtype=jnp.int32)[None, :, None]
        == jnp.arange(3 * rows_here, dtype=jnp.int32)[None, None, :]
    ).astype(jnp.float32)
    spread = jnp.einsum("vjr,vju->vru", placing, band_proj, precision=HIGH)
    from_below = shifted(spread[:, 2 * rows_here :], "slab", 1)
    from_above = shifted(spread[:, :rows_here], "slab", -1)
    forward = spread[:, rows_here : 2 * rows_here] + from_below + from_above
    residual = row_weight * (sino - forward)
    rimmed = padded(residual, (("slab", 1),), rows_here)
    band_res = jnp.einsum("vjr,vru->vju", placing, rimmed, precision=HIGH)
    smeared = jnp.einsum("vzj,vju->vzu", masked, band_res, precision=HIGH).astype(jnp.bfloat16)
    smeared = smeared.reshape(views_here, planes, col_blocks, block_width)
    pulled = jnp.einsum(
        "vtc,vzck->vtzk", select_half, smeared, preferred_element_type=jnp.float32
    ).astype(jnp.bfloat16)
    weights = transaxial
    every_tile = lax.psum(
        jnp.einsum("vtik,vtzk->tzi", weights, pulled, preferred_element_type=jnp.float32), "view"
    )
    own_tiles = lax.dynamic_slice_in_dim(
        every_tile, lax.axis_index("view") * tiles_here, tiles_here, 0
    )
    back = jnp.transpose(own_tiles, (1, 0, 2)).reshape(planes, pixels)
    updated = jnp.maximum(volume + col_weight * back, 0.0)
    return (updated, residual)


def solution(mesh):
    in_specs = (
        P("slab", "view"),
        P("view", "slab", None),
        P("view", None, None, None),
        P("view", None),
        P("view", "slab", None),
        P("view", "slab"),
        P("view", "slab"),
        P("view", "slab", None),
        P("slab", "view"),
    )
    out_specs = (P("slab", "view"), P("view", "slab", None))
    return jax.shard_map(
        per_device, mesh=mesh, in_specs=in_specs, out_specs=out_specs, check_vma=False
    )
```

profile of v0, /device:TPU:22, one launch (start us, length us, event | category | flops | bytes accessed | tf_op | source)
XLA Modules:
  0.0 370.1 jit_solution(13149563044447049132)
XLA Ops:
  7.2 1.3 convert_element_type.28
  8.5 0.8 copy.28
  10.8 53.4 %all-gather.2.cloned.1.call-done = bf16[64,256,256]{2,0,1:T(8,128)(2,1)} async-done(((bf16[64,16,256]{2,0,1:T(8,128)(2,1)}), bf16[64,256,256]{2,0,1:T(8,128)(2,1)}) %all-gather.2.cloned.1.call-update) | async-done | bytes 8388624 | tf_op jit(solution)/shard_map/all_gather | solution.py:45
  64.2 21.6 %fusion.6 = f32[256,64,256]{2,1,0:T(8,128)} fusion(bf16[64,256,256]{2,0,1:T(8,128)(2,1)} %all-gather.2.cloned.1.call-done, bf16[1,256,256,256]{3,2,1,0:T(8,128)(2,1)} %param.11), kind=kOutput, calls=%fused_computation.6 | convolution fusion | flops 2147483648 | bytes 58720256 | tf_op jit(solution)/shard_map/zti,vtik->vtzk/dot_general | solution.py:43
  85.7 19.9 %fusion.4 = f32[64,256,8]{1,2,0:T(8,128)S(1)} fusion(f32[256,64,256]{2,1,0:T(8,128)} %fusion.6, s32[256]{0:T(256)S(1)} %bitcast.67), kind=kOutput, calls=%fused_computation.4 | convolution fusion | flops 402655232 | bytes 17302528 | tf_op jit(solution)/shard_map/vtc,vtzk->vzck/dot_general | solution.py:49
  105.6 0.2 copy.21
  105.8 0.4 fusion.19
  106.2 0.4 convolution_bitcast_fusion
  106.7 3.5 collective-permute-start
  110.2 6.0 %collective-permute-start.1 = (f32[1,16,2048]{2,1,0:T(8,128)S(1)}, f32[1,16,2048]{2,1,0:T(8,128)S(1)}, u32[]{:S(2)}, u32[]{:S(2)}) collective-permute-start(f32[1,16,2048]{2,1,0:T(8,128)S(1)} %get-tuple-element.3), channel_id=1, source_target_pairs={{16,0},{32,16},{48,32},{64,48},{80,64},{96,80},{112,96},{17,1},{33... | collective-permute-start | bytes 393224 | tf_op jit(solution)/shard_map/ppermute | solution.py:12
  116.2 1.7 collective-permute-done
  117.8 1.2 collective-permute-done.1
  119.1 8.0 %collective-permute-start.3 = (f32[1,16,2048]{2,1,0:T(8,128)S(1)}, f32[1,16,2048]{2,1,0:T(8,128)S(1)}, u32[]{:S(2)}, u32[]{:S(2)}) collective-permute-start(f32[1,16,2048]{2,1,0:T(8,128)S(1)} %fusion.17), channel_id=1, source_target_pairs={{16,0},{32,16},{48,32},{64,48},{80,64},{96,80},{112,96},{17,1},{33... | collective-permute-start | bytes 393224 | tf_op jit(solution)/shard_map/ppermute | solution.py:23
  127.1 2.1 collective-permute-start.2
  129.2 0.4 collective-permute-done.3
  129.6 8.0 %collective-permute-done.2 = f32[1,16,2048]{2,1,0:T(8,128)S(1)} collective-permute-done((f32[1,16,2048]{2,1,0:T(8,128)S(1)}, f32[1,16,2048]{2,1,0:T(8,128)S(1)}, u32[]{:S(2)}, u32[]{:S(2)}) %collective-permute-start.2) | collective-permute-done | bytes 131104 | tf_op jit(solution)/shard_map/ppermute | solution.py:20
  137.6 0.3 fusion.10
  137.9 0.7 convolution_convert_fusion.1
  138.6 5.6 %convolution_convert_fusion = bf16[256,64,256]{2,0,1:T(8,128)(2,1)} fusion(bf16[64,8,256]{2,1,0:T(8,128)(2,1)S(1)} %bitcast.65, s32[256]{0:T(256)S(1)} %bitcast.68), kind=kOutput, calls=%fused_computation.8 | convolution fusion | flops 71305216 | bytes 8651776 | tf_op jit(solution)/shard_map/vtc,vzck->vtzk/dot_general | solution.py:70
  144.2 24.7 %fusion = f32[256,64,256]{2,1,0:T(8,128)} fusion(bf16[1,256,256,256]{3,2,1,0:T(8,128)(2,1)} %param.11, bf16[256,64,256]{2,0,1:T(8,128)(2,1)} %convolution_convert_fusion), kind=kOutput, calls=%fused_computation | convolution fusion | flops 2147483648 | bytes 58720256 | tf_op jit(solution)/shard_map/vtik,vtzk->tzi/dot_general | solution.py:75
  169.0 191.7 %all-reduce.2.cloned.1.call-done = f32[256,64,256]{2,1,0:T(8,128)} async-done(((f32[256,64,256]{2,1,0:T(8,128)}), f32[256,64,256]{2,1,0:T(8,128)}) %all-reduce.2.cloned.1.call-update) | async-done | bytes 16777232 | tf_op jit(solution)/shard_map/psum | solution.py:74
  360.7 1.3 dynamic-slice_bitcast_fusion
  362.0 0.1 copy.20
  362.1 1.2 add_maximum_fusion
  (23 shorter events, 0.3 us)
Async XLA Ops:
  7.2 57.0 %all-gather.2.cloned.1.call-start = ((), (), s32[]{:S(2)}) async-start(), calls=%async_computation | async-start | bytes 8912896 | tf_op jit(solution)/shard_map/all_gather | solution.py:45
  9.4 351.3 %all-reduce.2.cloned.1.call-start = ((), (), s32[]{:S(2)}) async-start(), calls=%async_computation.1 | async-start | bytes 33554432 | tf_op jit(solution)/shard_map/psum | solution.py:74
  10.7 75.0 %copy-start.6 = (s32[1,256]{1,0:T(1,128)S(1)}, s32[1,256]{1,0:T(1,128)}, u32[]{:S(2)}) copy-start(s32[1,256]{1,0:T(1,128)} %param.12) | copy-start | bytes 3076
  85.7 20.1 %copy-start.5 = (bf16[1,64,32]{1,2,0:T(8,128)(2,1)S(1)}, bf16[1,64,32]{1,2,0:T(8,128)(2,1)}, u32[]{:S(2)}) copy-start(bf16[1,64,32]{1,2,0:T(8,128)(2,1)} %param.13) | copy-start | bytes 12292
  85.7 33.3 %copy-start.3 = (f32[1,16,2048]{2,1,0:T(8,128)S(1)}, f32[1,16,2048]{2,1,0:T(8,128)}, u32[]{:S(2)}) copy-start(f32[1,16,2048]{2,1,0:T(8,128)} %param.16) | copy-start | bytes 393220
  85.7 33.3 %copy-start.4 = (f32[1,16,2048]{2,1,0:T(8,128)S(1)}, f32[1,16,2048]{2,1,0:T(8,128)}, u32[]{:S(2)}) copy-start(f32[1,16,2048]{2,1,0:T(8,128)} %param.10) | copy-start | bytes 393220
  106.7 11.1 %collective-permute-start = (f32[1,16,2048]{2,1,0:T(8,128)S(1)}, f32[1,16,2048]{2,1,0:T(8,128)S(1)}, u32[]{:S(2)}, u32[]{:S(2)}) collective-permute-start(f32[1,16,2048]{2,1,0:T(8,128)S(1)} %get-tuple-element.2), channel_id=1, source_target_pairs={{0,16},{16,32},{32,48},{48,64},{64,80},{80,96},{96,112},{1,17},{17... | collective-permute-start | bytes 393224 | tf_op jit(solution)/shard_map/ppermute | solution.py:12
  110.2 8.9 %collective-permute-start.1 = (f32[1,16,2048]{2,1,0:T(8,128)S(1)}, f32[1,16,2048]{2,1,0:T(8,128)S(1)}, u32[]{:S(2)}, u32[]{:S(2)}) collective-permute-start(f32[1,16,2048]{2,1,0:T(8,128)S(1)} %get-tuple-element.3), channel_id=1, source_target_pairs={{16,0},{32,16},{48,32},{64,48},{80,64},{96,80},{112,96},{17,1},{33... | collective-permute-start | bytes 393224 | tf_op jit(solution)/shard_map/ppermute | solution.py:12
  119.1 49.9 %copy-start.2 = (f32[1,16,2048]{2,1,0:T(8,128)}, f32[1,16,2048]{2,1,0:T(8,128)S(1)}, u32[]{:S(2)}) copy-start(f32[1,16,2048]{2,1,0:T(8,128)S(1)} %fusion.17) | copy-start | bytes 393220
  119.1 10.5 %collective-permute-start.3 = (f32[1,16,2048]{2,1,0:T(8,128)S(1)}, f32[1,16,2048]{2,1,0:T(8,128)S(1)}, u32[]{:S(2)}, u32[]{:S(2)}) collective-permute-start(f32[1,16,2048]{2,1,0:T(8,128)S(1)} %fusion.17), channel_id=1, source_target_pairs={{16,0},{32,16},{48,32},{64,48},{80,64},{96,80},{112,96},{17,1},{33... | collective-permute-start | bytes 393224 | tf_op jit(solution)/shard_map/ppermute | solution.py:23
  127.1 10.5 %collective-permute-start.2 = (f32[1,16,2048]{2,1,0:T(8,128)S(1)}, f32[1,16,2048]{2,1,0:T(8,128)S(1)}, u32[]{:S(2)}, u32[]{:S(2)}) collective-permute-start(f32[1,16,2048]{2,1,0:T(8,128)S(1)} %fusion.17), channel_id=1, source_target_pairs={{0,16},{16,32},{32,48},{48,64},{64,80},{80,96},{96,112},{1,17},{17... | collective-permute-start | bytes 393224 | tf_op jit(solution)/shard_map/ppermute | solution.py:20
  169.0 193.1 %copy-start = (f32[64,4096]{1,0:T(8,128)S(1)}, f32[64,4096]{1,0:T(8,128)}, u32[]{:S(2)}) copy-start(f32[64,4096]{1,0:T(8,128)} %param.9) | copy-start | bytes 3145732
  169.0 193.2 %copy-start.1 = (f32[64,4096]{1,0:T(8,128)S(1)}, f32[64,4096]{1,0:T(8,128)}, u32[]{:S(2)}) copy-start(f32[64,4096]{1,0:T(8,128)} %param.17) | copy-start | bytes 3145732
Sparse Core Ops, SparseCore 0:
  10.3 53.8 all-gather.1
  169.1 191.5 all-reduce.1
where the time goes:
time: 374 us; the launch traced here: 370 us
  waiting for transfers between devices  256 us (68%)
  matrix products  73.6 us (20%)
  starting transfers between devices  19.6 us (5%)
  between operations  15.5 us (4%)
    psum x1, waiting for transfers between devices, per_device(): lax.psum(jnp.einsum('vtik,vtzk->tzi', weights, pulled, preferred_element_...  192 us
    all_gather x1, waiting for transfers between devices, per_device(): lax.all_gather(packed, 'view', axis=1, tiled=True)  53.4 us
    dot_general x1, matrix products, per_device(): jnp.einsum('vtik,vtzk->tzi', weights, pulled, preferred_element_type=jnp....  24.7 us
    dot_general x1, matrix products, per_device(): jnp.einsum('zti,vtik->vtzk', lax.all_gather(packed, 'view', axis=1, tiled...  21.6 us
    dot_general x1, matrix products, per_device(): jnp.einsum('vtc,vtzk->vzck', select_float, per_tile, precision=HIGH)  19.9 us
    ppermute x2, starting transfers between devices, shifted(): return lax.ppermute(x, axis, pairs)  9.46 us
    ppermute x1, starting transfers between devices, padded(): lax.ppermute(lax.slice_in_dim(block, 0, width, axis=dim), axis, backward)  8 us
    ppermute x1, waiting for transfers between devices, padded(): lax.ppermute(lax.slice_in_dim(block, block.shape[dim] - width, None, axis...  7.98 us
  transfers between devices with their start and end apart: 6, of which 6 were waited for; matrix products, arithmetic and copies ran while one was open for 0% of the time, Pallas kernels for 0%

commit v1 on v0

v1 whole, which is shorter than its diff:
```python
import functools
import jax
import jax.numpy as jnp
from jax import lax
from jax.experimental import pallas as pl
from jax.experimental.pallas import tpu as pltpu
from jax.sharding import PartitionSpec as P

F32 = jnp.float32
BF16 = jnp.bfloat16
MIB = 2**20
VM = pl.BlockSpec(memory_space=pltpu.VMEM)
SM = pl.BlockSpec(memory_space=pltpu.SMEM)
ANY = pl.BlockSpec(memory_space=pl.ANY)
HBM = pl.BlockSpec(memory_space=pltpu.HBM)
NT = (((1,), (1,)), ((), ()))
NX = 4


def place(y, x, c):
    return (y % 2) * 2 * NX + (x % NX) * 2 + c


def moves(step):
    return [
        (place(y, x, c), place(*step(y, x, c)))
        for y in range(2)
        for x in range(NX)
        for c in range(2)
    ]


UP = moves(lambda y, x, c: (y, x + 1, c))
DOWN = moves(lambda y, x, c: (y, x - 1, c))
ACROSS = moves(lambda y, x, c: (y + 1, x, c))
CORE = moves(lambda y, x, c: (y, x, 1 - c))


def send(array, pairs):
    return lax.ppermute(array, "view", pairs)


def params(mib):
    return pltpu.CompilerParams(vmem_limit_bytes=mib * MIB)


def split(value):
    high = value.astype(BF16)
    return high, (value - high.astype(F32)).astype(BF16)


def dot(a, b):
    return jnp.dot(a, b, preferred_element_type=F32)


def base_of(info, dx, dy, other, tiles):
    view = info[0]
    y, x, c = view // (2 * NX), (view // 2) % NX, view % 2
    c = 1 - c if other else c
    owner = lax.rem(y + dy, 2) * 2 * NX + lax.rem(x + dx + NX, NX) * 2 + c
    return owner * tiles


def cheap():
    return pl.CostEstimate(flops=1, bytes_accessed=1, transcendentals=0)


def cost(chunks):
    return pl.CostEstimate(
        flops=int(chunks * 3.4e8), bytes_accessed=int(chunks * 6e5), transcendentals=0
    )


def round_volume(volume, info):
    def body(source, about, out):
        out[...] = source[...].astype(BF16)

    return pl.pallas_call(
        body,
        in_specs=[VM, SM],
        out_specs=VM,
        out_shape=jax.ShapeDtypeStruct(volume.shape, BF16),
        compiler_params=params(12),
        cost_estimate=cheap(),
        name="round_volume",
    )(volume, info)


def gate(arrays, after):
    n = len(arrays)

    def body(*refs):
        pass

    return pl.pallas_call(
        body,
        in_specs=[ANY] * (n + 1),
        out_specs=[ANY] * n,
        out_shape=[jax.ShapeDtypeStruct(a.shape, a.dtype) for a in arrays],
        input_output_aliases={i: i for i in range(n)},
        compiler_params=params(12),
        cost_estimate=cheap(),
        name="gate",
    )(*arrays, after)


def cut(array, start, size, after):
    def body(source, earlier, out):
        out[...] = source[:, start : start + size]

    return pl.pallas_call(
        body,
        in_specs=[VM, ANY],
        out_specs=VM,
        out_shape=jax.ShapeDtypeStruct((array.shape[0], size), array.dtype),
        compiler_params=params(12),
        cost_estimate=cheap(),
        name="cut",
    )(array, after)


def join(low, high, after):
    size = low.shape[1]

    def body(a, b, earlier, out):
        out[:, :size] = a[...]
        out[:, size:] = b[...]

    return pl.pallas_call(
        body,
        in_specs=[VM, VM, ANY],
        out_specs=VM,
        out_shape=jax.ShapeDtypeStruct((low.shape[0], 2 * size), low.dtype),
        compiler_params=params(12),
        cost_estimate=cheap(),
        name="join",
    )(low, high, after)


def load_footprints(source, after):
    pieces = 16
    each = source.shape[0] // pieces

    def body(src, earlier, target, sems):
        copies = [
            pltpu.make_async_copy(
                src.at[pl.ds(i * each, each)], target.at[pl.ds(i * each, each)], sems.at[i]
            )
            for i in range(pieces)
        ]
        for copy in copies:
            copy.start()
        for copy in copies:
            copy.wait()

    return pl.pallas_call(
        body,
        in_specs=[HBM, ANY],
        out_specs=VM,
        out_shape=pltpu.VMEM(source.shape, source.dtype),
        scratch_shapes=[pltpu.SemaphoreType.DMA((pieces,))],
        compiler_params=params(12),
        cost_estimate=pl.CostEstimate(flops=1, bytes_accessed=source.size * 2, transcendentals=0),
        name="load_footprints",
    )(source, after)


def placing(info, axial):
    most, planes = axial.shape
    window = 48
    first, length = info[1], info[2]
    live = lax.broadcasted_iota(jnp.int32, (most, planes), 0) < length
    masked = jnp.where(live, axial[...].astype(F32), 0.0).astype(BF16)
    hot = (
        lax.broadcasted_iota(jnp.int32, (window, most), 1) + first
        == lax.broadcasted_iota(jnp.int32, (window, most), 0)
    )
    return dot(jnp.where(hot, 1.0, 0.0).astype(BF16), masked)


def project(weights, blocks, info, places, shards, total=None, axial=None):
    planes, pixels = shards[0].shape
    width, columns = weights.shape[1], weights.shape[2]
    tiles = pixels // width
    detector = 8 * columns
    n = len(shards)
    started = total is not None
    last = axial is not None
    piece = 4
    pieces = tiles // piece

    def body(blk, about, w, *refs):
        refs = list(refs)
        parts = [refs.pop(0) for _ in range(n)]
        before = refs.pop(0) if started else None
        ax = refs.pop(0) if last else None
        outs = [refs.pop(0) for _ in range(3)] if last else None
        acc, slots, sems = refs
        origins = [base_of(about, *places[p], tiles) for p in range(n)]
        copies = [
            pltpu.make_async_copy(
                w.at[pl.ds(origins[p] + q * piece, piece)],
                slots.at[pl.ds(p * tiles + q * piece, piece)],
                sems.at[p * pieces + q],
            )
            for p in range(n)
            for q in range(pieces)
        ]
        for copy in copies:
            copy.start()
        acc[...] = before[...] if started else jnp.zeros(acc.shape, F32)
        for p in range(n):
            for q in range(pieces):
                copies[p * pieces + q].wait()
                for i in range(q * piece, (q + 1) * piece):
                    at = pl.multiple_of(blk[0, origins[p] + i] * columns, columns)
                    row = parts[p][:, i * width : (i + 1) * width]
                    acc[:, pl.ds(at, columns)] += dot(row, slots[p * tiles + i])
        if last:
            placed = placing(about, ax).astype(BF16)
            high, low = split(acc[...])
            spread = dot(placed, high) + dot(placed, low)
            for k in range(3):
                outs[k][...] = spread[16 * k : 16 * k + 16]

    args = [blocks, info, weights, *shards]
    specs = [SM, SM, HBM] + [VM] * n
    if started:
        args.append(total)
        specs.append(VM)
    scratch = [
        pltpu.VMEM((n * tiles, width, columns), BF16),
        pltpu.SemaphoreType.DMA((n * pieces,)),
    ]
    if last:
        args.append(axial)
        specs.append(VM)
        out_shape = [jax.ShapeDtypeStruct((16, detector), F32)] * 3
        out_specs = [VM] * 3
        scratch = [pltpu.VMEM((planes, detector), F32)] + scratch
    else:
        out_shape = jax.ShapeDtypeStruct((planes, detector), F32)
        out_specs = VM
    return pl.pallas_call(
        body,
        in_specs=specs,
        out_specs=out_specs,
        out_shape=out_shape,
        scratch_shapes=scratch,
        compiler_params=params(2 * n + 4),
        cost_estimate=cost(n),
        name="project",
    )(*args)


def weigh(row_weight, sino, mine, low, high):
    def body(rw, measured, a, b, c, out, short):
        value = rw[0] * (measured[0] - (a[...] + b[...] + c[...]))
        out[...] = value
        short[...] = value.astype(BF16)

    return pl.pallas_call(
        body,
        in_specs=[VM] * 5,
        out_specs=[VM, VM],
        out_shape=[
            jax.ShapeDtypeStruct(mine.shape, F32),
            jax.ShapeDtypeStruct(mine.shape, BF16),
        ],
        compiler_params=params(12),
        cost_estimate=cheap(),
        name="weigh",
    )(row_weight, sino, mine, low, high)


def smear(info, axial, rows):
    planes = axial.shape[1]
    detector = rows[0].shape[1]

    def body(about, ax, low_rows, own_rows, high_rows, out):
        placed = placing(about, ax).T.astype(BF16)
        window = jnp.concatenate(
            [low_rows[...].astype(F32), own_rows[...], high_rows[...].astype(F32)], axis=0
        )
        high, low = split(window)
        out[...] = (dot(placed, high) + dot(placed, low)).astype(BF16)

    return pl.pallas_call(
        body,
        in_specs=[SM, VM, VM, VM, VM],
        out_specs=VM,
        out_shape=jax.ShapeDtypeStruct((planes, detector), BF16),
        compiler_params=params(12),
        cost_estimate=cheap(),
        name="smear",
    )(info, axial, *rows)


def pull(weights, blocks, info, places, smeared, adds=None, after=(), out_dtype=F32, joined=False):
    width, columns = weights.shape[1], weights.shape[2]
    planes = smeared.shape[0]
    tiles = weights.shape[0] // (4 * NX)
    pixels = tiles * width
    n = len(places)
    adds = adds or []
    sources = list({id(array): array for array, _ in adds}.values())
    piece = 8
    pieces = tiles // piece

    def body(blk, about, w, sm, *refs):
        given = dict(zip([id(a) for a in sources], refs[: len(sources)]))
        outs = refs[len(sources) + len(after) : -2]
        slots, sems = refs[-2:]
        origins = [base_of(about, *places[p], tiles) for p in range(n)]
        copies = [
            pltpu.make_async_copy(
                w.at[pl.ds(origins[p] + q * piece, piece)],
                slots.at[pl.ds(p * tiles + q * piece, piece)],
                sems.at[p * pieces + q],
            )
            for p in range(n)
            for q in range(pieces)
        ]
        for copy in copies:
            copy.start()
        for p in range(n):
            out, shift = (outs[0], p * pixels) if joined else (outs[p], 0)
            for q in range(pieces):
                copies[p * pieces + q].wait()
                for i in range(q * piece, (q + 1) * piece):
                    at = pl.multiple_of(blk[0, origins[p] + i] * columns, columns)
                    value = lax.dot_general(
                        sm[:, pl.ds(at, columns)],
                        slots[p * tiles + i],
                        NT,
                        preferred_element_type=F32,
                    )
                    if adds:
                        array, first = adds[p]
                        first += i * width
                        value += given[id(array)][:, first : first + width].astype(F32)
                    out[:, shift + i * width : shift + (i + 1) * width] = value.astype(out.dtype)

    shapes = [(planes, n * pixels)] if joined else [(planes, pixels)] * n
    out = pl.pallas_call(
        body,
        in_specs=[SM, SM, HBM, VM] + [VM] * len(sources) + [ANY] * len(after),
        out_specs=[VM] * len(shapes),
        out_shape=[jax.ShapeDtypeStruct(shape, out_dtype) for shape in shapes],
        scratch_shapes=[
            pltpu.VMEM((n * tiles, width, columns), BF16),
            pltpu.SemaphoreType.DMA((n * pieces,)),
        ],
        compiler_params=params(24),
        cost_estimate=cost(n),
        name="pull",
    )(blocks, info, weights, smeared, *sources, *after)
    return out[0] if joined else out


def combine(sums, size, cuts=1, after=()):
    arrays = list({id(term[0]): term[0] for terms in sums for term in terms}.values())
    half = size // 2
    planes = arrays[0].shape[0]

    def body(*refs):
        given = dict(zip([id(a) for a in arrays], refs[: len(arrays)]))
        outs = refs[len(arrays) + len(after) :]
        for s, terms in enumerate(sums):
            for h in range(2):
                value = None
                for array, first, halves in terms:
                    if h in halves:
                        first += h * half
                        more = given[id(array)][:, first : first + half].astype(F32)
                        value = more if value is None else value + more
                if cuts == 2:
                    outs[2 * s + h][...] = value.astype(BF16)
                else:
                    outs[s][:, h * half : (h + 1) * half] = value.astype(BF16)

    return pl.pallas_call(
        body,
        in_specs=[VM] * len(arrays) + [ANY] * len(after),
        out_specs=[VM] * (len(sums) * cuts),
        out_shape=[jax.ShapeDtypeStruct((planes, size // cuts), BF16)] * (len(sums) * cuts),
        compiler_params=params(16),
        cost_estimate=cheap(),
        name="combine",
    )(*arrays, *after)


def update(volume, col_weight, kept, swap, arrived):
    def body(vol, weight, mine, d, a, b, c, out):
        summed = mine[...] + d[...].astype(F32) + a[...].astype(F32) + b[...].astype(F32) + c[...].astype(F32)
        out[...] = jnp.maximum(vol[...] + weight[...] * summed, 0.0)

    planes, pixels = volume.shape
    block = pl.BlockSpec((planes, pixels // 4), lambda i: (0, i))
    return pl.pallas_call(
        body,
        grid=(4,),
        in_specs=[block] * 7,
        out_specs=block,
        out_shape=jax.ShapeDtypeStruct(volume.shape, F32),
        compiler_params=params(12),
        name="update",
    )(
        volume,
        col_weight,
        kept,
        swap,
        *arrived,
    )


def per_device(
    volume, sino, transaxial, blocks, axial, band_start, band_len, row_weight, col_weight
):
    planes, pixels = volume.shape
    rows_here = sino.shape[1]
    half = pixels // 2
    ax = jnp.swapaxes(axial[0], 0, 1)
    slab = lax.axis_index("slab")
    view = lax.axis_index("view")
    first = band_start[0, 0] - (slab - 1) * rows_here
    info = jnp.stack([view, first, band_len[0, 0]]).astype(jnp.int32)

    def whose(dx, dy):
        return [(dx, dy, False), (dx, dy, True)]

    own = round_volume(volume, info)
    left = send(own, UP)
    right = send(own, DOWN)
    over = send(own, ACROSS)
    swapped = send(own, CORE)
    weights = pltpu.with_memory_space_constraint(transaxial[0], pltpu.HBM)
    ahead = functools.partial(project, weights, blocks, info)
    total = ahead(whose(0, 0), [own, swapped])
    left, right, over = gate([left, right, over], total)
    far_low = send(cut(left, 0, half, total), UP)
    far_high = send(cut(right, half, half, total), DOWN)
    left_over = send(over, UP)
    right_over = send(over, DOWN)
    total = ahead(
        whose(-1, 0) + whose(1, 0), [left, send(left, CORE), right, send(right, CORE)], total
    )
    far = join(far_low, far_high, total)
    far_over = send(far, ACROSS)
    t1 = total
    left_over, right_over = gate([left_over, right_over], t1)
    total = ahead(whose(0, 1) + whose(2, 0), [over, send(over, CORE), far, send(far, CORE)], total)
    t2 = total
    total = ahead(
        whose(-1, 1) + whose(1, 1),
        [left_over, send(left_over, CORE), right_over, send(right_over, CORE)],
        total,
    )
    (far_over,) = gate([far_over], t2)
    below, mine, above = ahead(whose(2, 1), [far_over, send(far_over, CORE)], total, ax)

    count = lax.axis_size("slab")
    rise = [(i, i + 1) for i in range(count - 1)]
    fall = [(i + 1, i) for i in range(count - 1)]
    residual, rounded = weigh(
        row_weight, sino, mine, lax.ppermute(above, "slab", rise), lax.ppermute(below, "slab", fall)
    )
    low_rows = lax.ppermute(rounded, "slab", rise)
    high_rows = lax.ppermute(rounded, "slab", fall)
    smeared = smear(info, ax, [low_rows, residual, high_rows])

    back = functools.partial(pull, weights, blocks, info)
    full = (0, 1)

    def others(*offsets):
        return [(dx, dy, True) for dx, dy in offsets]

    def owns(*offsets):
        return [(dx, dy, False) for dx, dy in offsets]

    def rounds(offsets, after):
        parts = back(others(*offsets), smeared, after=after, out_dtype=BF16)
        swaps = [send(part, CORE) for part in parts]
        mine = back(owns(*offsets), smeared, after=[parts[0]])
        return [[(a, 0, full), (b, 0, full)] for a, b in zip(mine, swaps)]

    far_sum, up_sum, down_sum = combine(rounds([(2, 1), (1, 1), (-1, 1)], []), pixels)
    from_over = send(far_sum, ACROSS)
    from_left = send(up_sum, UP)
    from_right = send(down_sum, DOWN)
    to_far, to_over = rounds([(2, 0), (0, 1)], [far_sum])
    half_up, half_down = combine([to_far + [(from_over, 0, full)]], pixels, 2)
    half_left = send(half_up, UP)
    half_right = send(half_down, DOWN)
    (over_sum,) = combine(
        [to_over + [(from_left, 0, full), (from_right, 0, full)]], pixels, after=[half_up]
    )
    over_last = send(over_sum, ACROSS)
    to_up, to_down, here = rounds([(1, 0), (-1, 0), (0, 0)], [over_sum])
    up_sum, down_sum = combine(
        [to_up + [(half_left, 0, (0,))], to_down + [(half_right, -half, (1,))]], pixels
    )
    left_last = send(up_sum, UP)
    right_last = send(down_sum, DOWN)
    updated = update(
        volume, col_weight, here[0][0], here[1][0], [over_last, left_last, right_last]
    )
    return updated, residual[None]


def solution(mesh):
    in_specs = (
        P("slab", "view"),
        P("view", "slab", None),
        P("view", None, None, None),
        P("view", None),
        P("view", "slab", None),
        P("view", "slab"),
        P("view", "slab"),
        P("view", "slab", None),
        P("slab", "view"),
    )
    out_specs = (P("slab", "view"), P("view", "slab", None))
    return jax.shard_map(
        per_device, mesh=mesh, in_specs=in_specs, out_specs=out_specs, check_vma=False
    )
```

time: 374 us -> 150 us (0.40)
  waiting for transfers between devices: 256 us -> 48.8 us
  matrix products: 73.6 us -> 0 us
  Pallas kernels: 0 us -> 53.6 us
  starting transfers between devices: 19.6 us -> 40.7 us
  between operations: 15.5 us -> 2.3 us
    psum x1 -> x0, waiting for transfers between devices: 192 us -> none  [per_device(): lax.psum(jnp.einsum('vtik,vtzk->tzi', weights, pulled, preferred_element_...]
    dot_general x8 -> x0, matrix products: 73.6 us -> none  [the longest x1 24.7 us: per_device(): jnp.einsum('vtik,vtzk->tzi', weights, pulled, preferred_element_type=jnp....]
    pallas_call x0 -> x25, Pallas kernels: none -> 53.6 us  [the longest x6 25.4 us: pull(): pl.pallas_call(body, in_specs=[SM, SM, HBM, VM] + [VM] * len(sources) + [...]
    all_gather x1 -> x0, waiting for transfers between devices: 53.4 us -> none  [per_device(): lax.all_gather(packed, 'view', axis=1, tiled=True)]
    ppermute x4 -> x36, waiting for transfers between devices: 11.2 us -> 48.8 us  [the longest x32 43.8 us: send(): return lax.ppermute(array, 'view', pairs)]
    ppermute x4 -> x36, starting transfers between devices: 19.6 us -> 40.7 us  [the longest x32 21.3 us: send(): return lax.ppermute(array, 'view', pairs)]
  transfers between devices with their start and end apart: 6 -> 36, of which waited for: 6 -> 18; matrix products, arithmetic and copies ran while one was open for 0% -> 0% of each run, Pallas kernels for 0% -> 22%
where the time goes in v1:
time: 150 us; the launch traced here: 148 us
  Pallas kernels  53.6 us (36%)
  waiting for transfers between devices  48.8 us (33%)
  starting transfers between devices  40.7 us (27%)
  local copies, waits for them, and re-layouts  2.84 us (2%)
  between operations  2.3 us (2%)
    ppermute x32, waiting for transfers between devices, send(): return lax.ppermute(array, 'view', pairs)  43.8 us
    pallas_call x6, Pallas kernels, pull(): pl.pallas_call(body, in_specs=[SM, SM, HBM, VM] + [VM] * len(sources) + [...  25.4 us
    pallas_call x5, Pallas kernels, project(): pl.pallas_call(body, in_specs=specs, out_specs=out_specs, out_shape=out_s...  23 us
    ppermute x32, starting transfers between devices, send(): return lax.ppermute(array, 'view', pairs)  21.3 us
    ppermute x1, starting transfers between devices, per_device(): high_rows = lax.ppermute(rounded, 'slab', fall)  7.34 us
    ppermute x1, starting transfers between devices, per_device(): lax.ppermute(below, 'slab', fall)  5.63 us
    ppermute x1, starting transfers between devices, per_device(): lax.ppermute(above, 'slab', rise)  3.82 us
  transfers between devices with their start and end apart: 36, of which 18 were waited for; matrix products, arithmetic and copies ran while one was open for 0% of the time, Pallas kernels for 22%

profile of v1, /device:TPU:22, one launch (start us, length us, event | category | flops | bytes accessed | tf_op | source)
XLA Modules:
  0.0 148.3 jit_solution(5663800935279326394)
XLA Ops:
  8.0 3.4 %project.5.refs_3_.earlier.refs_4_ = f32[64,2048]{1,0:T(8,128)S(1)} custom-call(s32[1,256]{1,0:T(1,128)S(1)} %copy-done.6, s32[3]{0:T(128)S(1)} %pad_add_fusion.about, bf16[256,256,256]{2,1,0:T(8,128)(2,1)} %bitcast.14, bf16[64,4096]{1,0:T(8,128)(2,1)S(1)} %round_volume.1.refs_0_, bf16[64,4096]{1,0:T(8,128)(2,1)S(1)} %collective-permute-done.3.refs_1_), custom_call_target="tpu_custom_call" | custom-call | flops 680000000 | bytes 1200000 | tf_op jit(solution)/shard_map/project/pallas_call | solution.py:244
  11.5 6.8 %collective-permute-done.refs_0_ = bf16[64,4096]{1,0:T(8,128)(2,1)S(1)} collective-permute-done((bf16[64,4096]{1,0:T(8,128)(2,1)S(1)}, bf16[64,4096]{1,0:T(8,128)(2,1)S(1)}, u32[]{:S(2)}, u32[]{:S(2)}) %collective-permute-start) | collective-permute-done | bytes 524320 | tf_op jit(solution)/shard_map/ppermute | solution.py:40
  22.5 2.9 %collective-permute-start.12 = (bf16[64,4096]{1,0:T(8,128)(2,1)S(1)}, bf16[64,4096]{1,0:T(8,128)(2,1)S(1)}, u32[]{:S(2)}, u32[]{:S(2)}) collective-permute-start(bf16[64,4096]{1,0:T(8,128)(2,1)S(1)} %get-tuple-element.37.refs_0_), channel_id=1, source_target_pairs={{0,2},{1,3},{2,4},{3,5},{4,6},{5,7},{6,0},{7,1},{8,10},{9,11},{10,... | collective-permute-start | bytes 1572872 | tf_op jit(solution)/shard_map/ppermute | solution.py:40
  25.4 5.3 %project.6.earlier.refs_4_.refs_2_ = f32[64,2048]{1,0:T(8,128)S(1)} custom-call(s32[1,256]{1,0:T(1,128)S(1)} %copy-done.7, s32[3]{0:T(128)S(1)} %pad_add_fusion.about, bf16[256,256,256]{2,1,0:T(8,128)(2,1)} %bitcast.15, bf16[64,4096]{1,0:T(8,128)(2,1)S(1)} %get-tuple-element.35.source.refs_0_, bf16[64,4096]{1,0:T(8,128)(2,1)S(1)} %collective-permute-done.6.refs_1_, ...), custom_call_target="tpu_custom_call" | custom-call | flops 1360000000 | bytes 2400000 | tf_op jit(solution)/shard_map/project/pallas_call | solution.py:244
  34.1 5.8 %collective-permute-done.12.refs_0_ = bf16[64,4096]{1,0:T(8,128)(2,1)S(1)} collective-permute-done((bf16[64,4096]{1,0:T(8,128)(2,1)S(1)}, bf16[64,4096]{1,0:T(8,128)(2,1)S(1)}, u32[]{:S(2)}, u32[]{:S(2)}) %collective-permute-start.12) | collective-permute-done | bytes 524320 | tf_op jit(solution)/shard_map/ppermute | solution.py:40
  39.8 2.7 %collective-permute-done.13.refs_1_ = bf16[64,4096]{1,0:T(8,128)(2,1)S(1)} collective-permute-done((bf16[64,4096]{1,0:T(8,128)(2,1)S(1)}, bf16[64,4096]{1,0:T(8,128)(2,1)S(1)}, u32[]{:S(2)}, u32[]{:S(2)}) %collective-permute-start.13) | collective-permute-done | bytes 524320 | tf_op jit(solution)/shard_map/ppermute | solution.py:40
  43.0 5.3 %project.7.refs_1_.refs_4_ = f32[64,2048]{1,0:T(8,128)S(1)} custom-call(s32[1,256]{1,0:T(1,128)S(1)} %copy-done.7, s32[3]{0:T(128)S(1)} %pad_add_fusion.about, bf16[256,256,256]{2,1,0:T(8,128)(2,1)} %bitcast.16, bf16[64,4096]{1,0:T(8,128)(2,1)S(1)} %get-tuple-element.37.refs_0_, bf16[64,4096]{1,0:T(8,128)(2,1)S(1)} %collective-permute-done.9.refs_1_, ...), custom_call_target="tpu_custom_call" | custom-call | flops 1360000000 | bytes 2400000 | tf_op jit(solution)/shard_map/project/pallas_call | solution.py:244
  48.6 5.3 %project.8.refs_2_ = f32[64,2048]{1,0:T(8,128)S(1)} custom-call(s32[1,256]{1,0:T(1,128)S(1)} %copy-done.7, s32[3]{0:T(128)S(1)} %pad_add_fusion.about, bf16[256,256,256]{2,1,0:T(8,128)(2,1)} %bitcast.17, bf16[64,4096]{1,0:T(8,128)(2,1)S(1)} %get-tuple-element.38.refs_0_, bf16[64,4096]{1,0:T(8,128)(2,1)S(1)} %collective-permute-done.14.refs_1_, ...), custom_call_target="tpu_custom_call" | custom-call | flops 1360000000 | bytes 2400000 | tf_op jit(solution)/shard_map/project/pallas_call | solution.py:244
  54.0 3.7 %project.9 = (f32[16,2048]{1,0:T(8,128)S(1)}, f32[16,2048]{1,0:T(8,128)S(1)}, f32[16,2048]{1,0:T(8,128)S(1)}) custom-call(s32[1,256]{1,0:T(1,128)S(1)} %copy-done.7, s32[3]{0:T(128)S(1)} %pad_add_fusion.about, bf16[256,256,256]{2,1,0:T(8,128)(2,1)} %bitcast.18, bf16[64,4096]{1,0:T(8,128)(2,1)S(1)} %gate.4.refs_0_, ...), custom_call_target="tpu_custom_call" | custom-call | flops 680000000 | bytes 1200000 | tf_op jit(solution)/shard_map/project/pallas_call | solution.py:244
  57.7 3.8 %collective-permute-start.16 = (f32[16,2048]{1,0:T(8,128)S(1)}, f32[16,2048]{1,0:T(8,128)S(1)}, u32[]{:S(2)}, u32[]{:S(2)}) collective-permute-start(f32[16,2048]{1,0:T(8,128)S(1)} %get-tuple-element.41), channel_id=1, source_target_pairs={{0,16},{16,32},{32,48},{48,64},{64,80},{80,96},{96,112},{1,17},{17... | collective-permute-start | bytes 393224 | tf_op jit(solution)/shard_map/ppermute | solution.py:466
  61.5 5.6 %collective-permute-start.17 = (f32[16,2048]{1,0:T(8,128)S(1)}, f32[16,2048]{1,0:T(8,128)S(1)}, u32[]{:S(2)}, u32[]{:S(2)}) collective-permute-start(f32[16,2048]{1,0:T(8,128)S(1)} %get-tuple-element.42), channel_id=1, source_target_pairs={{16,0},{32,16},{48,32},{64,48},{80,64},{96,80},{112,96},{17,1},{33... | collective-permute-start | bytes 393224 | tf_op jit(solution)/shard_map/ppermute | solution.py:466
  71.0 2.6 %collective-permute-start.18 = (bf16[16,2048]{1,0:T(8,128)(2,1)S(1)}, bf16[16,2048]{1,0:T(8,128)(2,1)S(1)}, u32[]{:S(2)}, u32[]{:S(2)}) collective-permute-start(bf16[16,2048]{1,0:T(8,128)(2,1)S(1)} %get-tuple-element.43), channel_id=1, source_target_pairs={{0,16},{16,32},{32,48},{48,64},{64,80},{80,96},{96,112},{1,17},{17... | collective-permute-start | bytes 196616 | tf_op jit(solution)/shard_map/ppermute | solution.py:468
  73.6 7.3 %collective-permute-start.19 = (bf16[16,2048]{1,0:T(8,128)(2,1)S(1)}, bf16[16,2048]{1,0:T(8,128)(2,1)S(1)}, u32[]{:S(2)}, u32[]{:S(2)}) collective-permute-start(bf16[16,2048]{1,0:T(8,128)(2,1)S(1)} %get-tuple-element.43), channel_id=1, source_target_pairs={{16,0},{32,16},{48,32},{64,48},{80,64},{96,80},{112,96},{17,1},{33... | collective-permute-start | bytes 196616 | tf_op jit(solution)/shard_map/ppermute | solution.py:469
  84.7 4.5 %pull.6 = (bf16[64,4096]{1,0:T(8,128)(2,1)S(1)}, bf16[64,4096]{1,0:T(8,128)(2,1)S(1)}, bf16[64,4096]{1,0:T(8,128)(2,1)S(1)}) custom-call(s32[1,256]{1,0:T(1,128)S(1)} %copy-done.7, s32[3]{0:T(128)S(1)} %pad_add_fusion.about, bf16[256,256,256]{2,1,0:T(8,128)(2,1)} %bitcast.19, bf16[64,2048]{1,0:T(8,128)(2,1)S(1)} %smear.1.sm), custom_call_target="tpu_custom_call" | custom-call | flops 1020000000 | bytes 1800000 | tf_op jit(solution)/shard_map/pull/pallas_call | solution.py:345
  89.9 4.5 %pull.7 = (f32[64,4096]{1,0:T(8,128)S(1)}, f32[64,4096]{1,0:T(8,128)S(1)}, f32[64,4096]{1,0:T(8,128)S(1)}) custom-call(s32[1,256]{1,0:T(1,128)S(1)} %copy-done.7, s32[3]{0:T(128)S(1)} %pad_add_fusion.about, bf16[256,256,256]{2,1,0:T(8,128)(2,1)} %bitcast.20, bf16[64,2048]{1,0:T(8,128)(2,1)S(1)} %smear.1.sm, bf16[64,4096]{1,0:T(8,128)(2,1)S(1)} %get-tuple-element.45.refs_0_), custom_call_target="tpu_custom_call" | custom-call | flops 1020000000 | bytes 1800000 | tf_op jit(solution)/shard_map/pull/pallas_call | solution.py:345
  94.7 3.6 %pull.8 = (bf16[64,4096]{1,0:T(8,128)(2,1)S(1)}, bf16[64,4096]{1,0:T(8,128)(2,1)S(1)}) custom-call(s32[1,256]{1,0:T(1,128)S(1)} %copy-done.7, s32[3]{0:T(128)S(1)} %pad_add_fusion.about, bf16[256,256,256]{2,1,0:T(8,128)(2,1)} %bitcast.21, bf16[64,2048]{1,0:T(8,128)(2,1)S(1)} %smear.1.sm, bf16[64,4096]{1,0:T(8,128)(2,1)S(1)} %get-tuple-element.51.refs_0_), custom_call_target="tpu_custom_call" | custom-call | flops 680000000 | bytes 1200000 | tf_op jit(solution)/shard_map/pull/pallas_call | solution.py:345
  102.3 3.6 %pull.9 = (f32[64,4096]{1,0:T(8,128)S(1)}, f32[64,4096]{1,0:T(8,128)S(1)}) custom-call(s32[1,256]{1,0:T(1,128)S(1)} %copy-done.7, s32[3]{0:T(128)S(1)} %pad_add_fusion.about, bf16[256,256,256]{2,1,0:T(8,128)(2,1)} %bitcast.22, bf16[64,2048]{1,0:T(8,128)(2,1)S(1)} %smear.1.sm, bf16[64,4096]{1,0:T(8,128)(2,1)S(1)} %get-tuple-element.52.refs_0_), custom_call_target="tpu_custom_call" | custom-call | flops 680000000 | bytes 1200000 | tf_op jit(solution)/shard_map/pull/pallas_call | solution.py:345
  105.9 6.8 %collective-permute-done.27.refs_2_ = bf16[64,4096]{1,0:T(8,128)(2,1)S(1)} collective-permute-done((bf16[64,4096]{1,0:T(8,128)(2,1)S(1)}, bf16[64,4096]{1,0:T(8,128)(2,1)S(1)}, u32[]{:S(2)}, u32[]{:S(2)}) %collective-permute-start.27) | collective-permute-done | bytes 524320 | tf_op jit(solution)/shard_map/ppermute | solution.py:40
  115.7 4.6 %pull.10 = (bf16[64,4096]{1,0:T(8,128)(2,1)S(1)}, bf16[64,4096]{1,0:T(8,128)(2,1)S(1)}, bf16[64,4096]{1,0:T(8,128)(2,1)S(1)}) custom-call(s32[1,256]{1,0:T(1,128)S(1)} %copy-done.7, s32[3]{0:T(128)S(1)} %pad_add_fusion.about, bf16[256,256,256]{2,1,0:T(8,128)(2,1)} %bitcast.23, bf16[64,2048]{1,0:T(8,128)(2,1)S(1)} %smear.1.sm, ...), custom_call_target="tpu_custom_call" | custom-call | flops 1020000000 | bytes 1800000 | tf_op jit(solution)/shard_map/pull/pallas_call | solution.py:345
  123.6 4.5 %pull.11 = (f32[64,4096]{1,0:T(8,128)S(1)}, f32[64,4096]{1,0:T(8,128)S(1)}, f32[64,4096]{1,0:T(8,128)S(1)}) custom-call(s32[1,256]{1,0:T(1,128)S(1)} %copy-done.7, s32[3]{0:T(128)S(1)} %pad_add_fusion.about, bf16[256,256,256]{2,1,0:T(8,128)(2,1)} %bitcast.24, bf16[64,2048]{1,0:T(8,128)(2,1)S(1)} %smear.1.sm, bf16[64,4096]{1,0:T(8,128)(2,1)S(1)} %get-tuple-element.59.refs_0_), custom_call_target="tpu_custom_call" | custom-call | flops 1020000000 | bytes 1800000 | tf_op jit(solution)/shard_map/pull/pallas_call | solution.py:345
  132.7 3.5 %collective-permute-done.29.a = bf16[64,4096]{1,0:T(8,128)(2,1)S(1)} collective-permute-done((bf16[64,4096]{1,0:T(8,128)(2,1)S(1)}, bf16[64,4096]{1,0:T(8,128)(2,1)S(1)}, u32[]{:S(2)}, u32[]{:S(2)}) %collective-permute-start.29) | collective-permute-done | bytes 524320 | tf_op jit(solution)/shard_map/ppermute | solution.py:40
  136.2 7.6 %collective-permute-done.34.b = bf16[64,4096]{1,0:T(8,128)(2,1)S(1)} collective-permute-done((bf16[64,4096]{1,0:T(8,128)(2,1)S(1)}, bf16[64,4096]{1,0:T(8,128)(2,1)S(1)}, u32[]{:S(2)}, u32[]{:S(2)}) %collective-permute-start.34) | collective-permute-done | bytes 524320 | tf_op jit(solution)/shard_map/ppermute | solution.py:40
  143.8 2.4 %collective-permute-done.35.c = bf16[64,4096]{1,0:T(8,128)(2,1)S(1)} collective-permute-done((bf16[64,4096]{1,0:T(8,128)(2,1)S(1)}, bf16[64,4096]{1,0:T(8,128)(2,1)S(1)}, u32[]{:S(2)}, u32[]{:S(2)}) %collective-permute-start.35) | collective-permute-done | bytes 524320 | tf_op jit(solution)/shard_map/ppermute | solution.py:40
  146.3 2.0 %update.1 = f32[64,4096]{1,0:T(8,128)} custom-call(f32[64,4096]{1,0:T(8,128)S(1)} %copy-done.1, f32[64,4096]{1,0:T(8,128)S(1)} %copy-done.2, f32[64,4096]{1,0:T(8,128)S(1)} %get-tuple-element.60.mine, bf16[64,4096]{1,0:T(8,128)(2,1)S(1)} %collective-permute-done.28.d, bf16[64,4096]{1,0:T(8,128)(2,1)S(1)} %collective-permute-done.29.a, ...), custom_call_target="tpu_custom_call" | custom-call | tf_op jit(solution)/shard_map/update/pallas_call | solution.py:400
  (92 shorter events, 37.7 us)
Async XLA Ops:
  3.9 14.3 %collective-permute-start = (bf16[64,4096]{1,0:T(8,128)(2,1)S(1)}, bf16[64,4096]{1,0:T(8,128)(2,1)S(1)}, u32[]{:S(2)}, u32[]{:S(2)}) collective-permute-start(bf16[64,4096]{1,0:T(8,128)(2,1)S(1)} %round_volume.1.refs_0_), channel_id=1, source_target_pairs={{0,2},{1,3},{2,4},{3,5},{4,6},{5,7},{6,0},{7,1},{8,10},{9,11},{10,... | collective-permute-start | bytes 1572872 | tf_op jit(solution)/shard_map/ppermute | solution.py:40
  4.5 15.2 %collective-permute-start.1 = (bf16[64,4096]{1,0:T(8,128)(2,1)S(1)}, bf16[64,4096]{1,0:T(8,128)(2,1)S(1)}, u32[]{:S(2)}, u32[]{:S(2)}) collective-permute-start(bf16[64,4096]{1,0:T(8,128)(2,1)S(1)} %round_volume.1.refs_0_), channel_id=1, source_target_pairs={{0,6},{1,7},{2,0},{3,1},{4,2},{5,3},{6,4},{7,5},{8,14},{9,15},{10,... | collective-permute-start | bytes 1572872 | tf_op jit(solution)/shard_map/ppermute | solution.py:40
  6.0 13.7 %collective-permute-start.2 = (bf16[64,4096]{1,0:T(8,128)(2,1)S(1)}, bf16[64,4096]{1,0:T(8,128)(2,1)S(1)}, u32[]{:S(2)}, u32[]{:S(2)}) collective-permute-start(bf16[64,4096]{1,0:T(8,128)(2,1)S(1)} %round_volume.1.refs_0_), channel_id=1, source_target_pairs={{0,8},{1,9},{2,10},{3,11},{4,12},{5,13},{6,14},{7,15},{8,0},{9,1},... | collective-permute-start | bytes 1572872 | tf_op jit(solution)/shard_map/ppermute | solution.py:40
  20.3 10.4 %collective-permute-start.4 = (bf16[64,2048]{1,0:T(8,128)(2,1)S(1)}, bf16[64,2048]{1,0:T(8,128)(2,1)S(1)}, u32[]{:S(2)}, u32[]{:S(2)}) collective-permute-start(bf16[64,2048]{1,0:T(8,128)(2,1)S(1)} %cut.2), channel_id=1, source_target_pairs={{0,2},{1,3},{2,4},{3,5},{4,6},{5,7},{6,0},{7,1},{8,10},{9,11},{10,... | collective-permute-start | bytes 786440 | tf_op jit(solution)/shard_map/ppermute | solution.py:40
  22.1 10.5 %collective-permute-start.5 = (bf16[64,2048]{1,0:T(8,128)(2,1)S(1)}, bf16[64,2048]{1,0:T(8,128)(2,1)S(1)}, u32[]{:S(2)}, u32[]{:S(2)}) collective-permute-start(bf16[64,2048]{1,0:T(8,128)(2,1)S(1)} %cut.3), channel_id=1, source_target_pairs={{0,6},{1,7},{2,0},{3,1},{4,2},{5,3},{6,4},{7,5},{8,14},{9,15},{10,... | collective-permute-start | bytes 786440 | tf_op jit(solution)/shard_map/ppermute | solution.py:40
  22.5 20.6 %collective-permute-start.9 = (bf16[64,4096]{1,0:T(8,128)(2,1)S(1)}, bf16[64,4096]{1,0:T(8,128)(2,1)S(1)}, u32[]{:S(2)}, u32[]{:S(2)}) collective-permute-start(bf16[64,4096]{1,0:T(8,128)(2,1)S(1)} %get-tuple-element.37.refs_0_), channel_id=1, source_target_pairs={{0,1},{1,0},{2,3},{3,2},{4,5},{5,4},{6,7},{7,6},{8,9},{9,8},{10,11... | collective-permute-start | bytes 1572872 | tf_op jit(solution)/shard_map/ppermute | solution.py:40
  22.5 17.3 %collective-permute-start.12 = (bf16[64,4096]{1,0:T(8,128)(2,1)S(1)}, bf16[64,4096]{1,0:T(8,128)(2,1)S(1)}, u32[]{:S(2)}, u32[]{:S(2)}) collective-permute-start(bf16[64,4096]{1,0:T(8,128)(2,1)S(1)} %get-tuple-element.37.refs_0_), channel_id=1, source_target_pairs={{0,2},{1,3},{2,4},{3,5},{4,6},{5,7},{6,0},{7,1},{8,10},{9,11},{10,... | collective-permute-start | bytes 1572872 | tf_op jit(solution)/shard_map/ppermute | solution.py:40
  25.4 17.1 %collective-permute-start.13 = (bf16[64,4096]{1,0:T(8,128)(2,1)S(1)}, bf16[64,4096]{1,0:T(8,128)(2,1)S(1)}, u32[]{:S(2)}, u32[]{:S(2)}) collective-permute-start(bf16[64,4096]{1,0:T(8,128)(2,1)S(1)} %get-tuple-element.37.refs_0_), channel_id=1, source_target_pairs={{0,6},{1,7},{2,0},{3,1},{4,2},{5,3},{6,4},{7,5},{8,14},{9,15},{10,... | collective-permute-start | bytes 1572872 | tf_op jit(solution)/shard_map/ppermute | solution.py:40
  32.6 10.4 %collective-permute-start.10 = (bf16[64,4096]{1,0:T(8,128)(2,1)S(1)}, bf16[64,4096]{1,0:T(8,128)(2,1)S(1)}, u32[]{:S(2)}, u32[]{:S(2)}) collective-permute-start(bf16[64,4096]{1,0:T(8,128)(2,1)S(1)} %join.1.refs_2_), channel_id=1, source_target_pairs={{0,1},{1,0},{2,3},{3,2},{4,5},{5,4},{6,7},{7,6},{8,9},{9,8},{10,11... | collective-permute-start | bytes 1572872 | tf_op jit(solution)/shard_map/ppermute | solution.py:40
  32.7 15.6 %collective-permute-start.8 = (bf16[64,4096]{1,0:T(8,128)(2,1)S(1)}, bf16[64,4096]{1,0:T(8,128)(2,1)S(1)}, u32[]{:S(2)}, u32[]{:S(2)}) collective-permute-start(bf16[64,4096]{1,0:T(8,128)(2,1)S(1)} %join.1.refs_2_), channel_id=1, source_target_pairs={{0,8},{1,9},{2,10},{3,11},{4,12},{5,13},{6,14},{7,15},{8,0},{9,1},... | collective-permute-start | bytes 1572872 | tf_op jit(solution)/shard_map/ppermute | solution.py:40
  57.7 11.4 %collective-permute-start.16 = (f32[16,2048]{1,0:T(8,128)S(1)}, f32[16,2048]{1,0:T(8,128)S(1)}, u32[]{:S(2)}, u32[]{:S(2)}) collective-permute-start(f32[16,2048]{1,0:T(8,128)S(1)} %get-tuple-element.41), channel_id=1, source_target_pairs={{0,16},{16,32},{32,48},{48,64},{64,80},{80,96},{96,112},{1,17},{17... | collective-permute-start | bytes 393224 | tf_op jit(solution)/shard_map/ppermute | solution.py:466
  61.5 8.7 %collective-permute-start.17 = (f32[16,2048]{1,0:T(8,128)S(1)}, f32[16,2048]{1,0:T(8,128)S(1)}, u32[]{:S(2)}, u32[]{:S(2)}) collective-permute-start(f32[16,2048]{1,0:T(8,128)S(1)} %get-tuple-element.42), channel_id=1, source_target_pairs={{16,0},{32,16},{48,32},{64,48},{80,64},{96,80},{112,96},{17,1},{33... | collective-permute-start | bytes 393224 | tf_op jit(solution)/shard_map/ppermute | solution.py:466
  71.0 10.2 %collective-permute-start.18 = (bf16[16,2048]{1,0:T(8,128)(2,1)S(1)}, bf16[16,2048]{1,0:T(8,128)(2,1)S(1)}, u32[]{:S(2)}, u32[]{:S(2)}) collective-permute-start(bf16[16,2048]{1,0:T(8,128)(2,1)S(1)} %get-tuple-element.43), channel_id=1, source_target_pairs={{0,16},{16,32},{32,48},{48,64},{64,80},{80,96},{96,112},{1,17},{17... | collective-permute-start | bytes 196616 | tf_op jit(solution)/shard_map/ppermute | solution.py:468
  73.6 9.2 %collective-permute-start.19 = (bf16[16,2048]{1,0:T(8,128)(2,1)S(1)}, bf16[16,2048]{1,0:T(8,128)(2,1)S(1)}, u32[]{:S(2)}, u32[]{:S(2)}) collective-permute-start(bf16[16,2048]{1,0:T(8,128)(2,1)S(1)} %get-tuple-element.43), channel_id=1, source_target_pairs={{16,0},{32,16},{48,32},{64,48},{80,64},{96,80},{112,96},{17,1},{33... | collective-permute-start | bytes 196616 | tf_op jit(solution)/shard_map/ppermute | solution.py:469
  98.4 14.4 %collective-permute-start.27 = (bf16[64,4096]{1,0:T(8,128)(2,1)S(1)}, bf16[64,4096]{1,0:T(8,128)(2,1)S(1)}, u32[]{:S(2)}, u32[]{:S(2)}) collective-permute-start(bf16[64,4096]{1,0:T(8,128)(2,1)S(1)} %get-tuple-element.51.refs_0_), channel_id=1, source_target_pairs={{0,8},{1,9},{2,10},{3,11},{4,12},{5,13},{6,14},{7,15},{8,0},{9,1},... | collective-permute-start | bytes 1572872 | tf_op jit(solution)/shard_map/ppermute | solution.py:40
  99.9 13.0 %collective-permute-start.23 = (bf16[64,4096]{1,0:T(8,128)(2,1)S(1)}, bf16[64,4096]{1,0:T(8,128)(2,1)S(1)}, u32[]{:S(2)}, u32[]{:S(2)}) collective-permute-start(bf16[64,4096]{1,0:T(8,128)(2,1)S(1)} %get-tuple-element.54), channel_id=1, source_target_pairs={{0,1},{1,0},{2,3},{3,2},{4,5},{5,4},{6,7},{7,6},{8,9},{9,8},{10,11... | collective-permute-start | bytes 1572872 | tf_op jit(solution)/shard_map/ppermute | solution.py:40
  100.2 14.0 %collective-permute-start.24 = (bf16[64,4096]{1,0:T(8,128)(2,1)S(1)}, bf16[64,4096]{1,0:T(8,128)(2,1)S(1)}, u32[]{:S(2)}, u32[]{:S(2)}) collective-permute-start(bf16[64,4096]{1,0:T(8,128)(2,1)S(1)} %get-tuple-element.55), channel_id=1, source_target_pairs={{0,2},{1,3},{2,4},{3,5},{4,6},{5,7},{6,0},{7,1},{8,10},{9,11},{10,... | collective-permute-start | bytes 1572872 | tf_op jit(solution)/shard_map/ppermute | solution.py:40
  100.4 15.0 %collective-permute-start.25 = (bf16[64,4096]{1,0:T(8,128)(2,1)S(1)}, bf16[64,4096]{1,0:T(8,128)(2,1)S(1)}, u32[]{:S(2)}, u32[]{:S(2)}) collective-permute-start(bf16[64,4096]{1,0:T(8,128)(2,1)S(1)} %get-tuple-element.56), channel_id=1, source_target_pairs={{0,6},{1,7},{2,0},{3,1},{4,2},{5,3},{6,4},{7,5},{8,14},{9,15},{10,... | collective-permute-start | bytes 1572872 | tf_op jit(solution)/shard_map/ppermute | solution.py:40
  120.3 10.1 %collective-permute-start.30 = (bf16[64,4096]{1,0:T(8,128)(2,1)S(1)}, bf16[64,4096]{1,0:T(8,128)(2,1)S(1)}, u32[]{:S(2)}, u32[]{:S(2)}) collective-permute-start(bf16[64,4096]{1,0:T(8,128)(2,1)S(1)} %get-tuple-element.59.refs_0_), channel_id=1, source_target_pairs={{0,1},{1,0},{2,3},{3,2},{4,5},{5,4},{6,7},{7,6},{8,9},{9,8},{10,11... | collective-permute-start | bytes 1572872 | tf_op jit(solution)/shard_map/ppermute | solution.py:40
  120.4 10.0 %collective-permute-start.32 = (bf16[64,4096]{1,0:T(8,128)(2,1)S(1)}, bf16[64,4096]{1,0:T(8,128)(2,1)S(1)}, u32[]{:S(2)}, u32[]{:S(2)}) collective-permute-start(bf16[64,4096]{1,0:T(8,128)(2,1)S(1)} %get-tuple-element.64), channel_id=1, source_target_pairs={{0,1},{1,0},{2,3},{3,2},{4,5},{5,4},{6,7},{7,6},{8,9},{9,8},{10,11... | collective-permute-start | bytes 1572872 | tf_op jit(solution)/shard_map/ppermute | solution.py:40
  121.1 9.2 %collective-permute-start.33 = (bf16[64,2048]{1,0:T(8,128)(2,1)S(1)}, bf16[64,2048]{1,0:T(8,128)(2,1)S(1)}, u32[]{:S(2)}, u32[]{:S(2)}) collective-permute-start(bf16[64,2048]{1,0:T(8,128)(2,1)S(1)} %get-tuple-element.65), channel_id=1, source_target_pairs={{0,6},{1,7},{2,0},{3,1},{4,2},{5,3},{6,4},{7,5},{8,14},{9,15},{10,... | collective-permute-start | bytes 786440 | tf_op jit(solution)/shard_map/ppermute | solution.py:40
  122.9 13.4 %collective-permute-start.29 = (bf16[64,4096]{1,0:T(8,128)(2,1)S(1)}, bf16[64,4096]{1,0:T(8,128)(2,1)S(1)}, u32[]{:S(2)}, u32[]{:S(2)}) collective-permute-start(bf16[64,4096]{1,0:T(8,128)(2,1)S(1)} %combine.6.refs_0_), channel_id=1, source_target_pairs={{0,8},{1,9},{2,10},{3,11},{4,12},{5,13},{6,14},{7,15},{8,0},{9,1},... | collective-permute-start | bytes 1572872 | tf_op jit(solution)/shard_map/ppermute | solution.py:40
  130.6 13.2 %collective-permute-start.34 = (bf16[64,4096]{1,0:T(8,128)(2,1)S(1)}, bf16[64,4096]{1,0:T(8,128)(2,1)S(1)}, u32[]{:S(2)}, u32[]{:S(2)}) collective-permute-start(bf16[64,4096]{1,0:T(8,128)(2,1)S(1)} %get-tuple-element.66), channel_id=1, source_target_pairs={{0,2},{1,3},{2,4},{3,5},{4,6},{5,7},{6,0},{7,1},{8,10},{9,11},{10,... | collective-permute-start | bytes 1572872 | tf_op jit(solution)/shard_map/ppermute | solution.py:40
  131.0 15.3 %collective-permute-start.35 = (bf16[64,4096]{1,0:T(8,128)(2,1)S(1)}, bf16[64,4096]{1,0:T(8,128)(2,1)S(1)}, u32[]{:S(2)}, u32[]{:S(2)}) collective-permute-start(bf16[64,4096]{1,0:T(8,128)(2,1)S(1)} %get-tuple-element.67), channel_id=1, source_target_pairs={{0,6},{1,7},{2,0},{3,1},{4,2},{5,3},{6,4},{7,5},{8,14},{9,15},{10,... | collective-permute-start | bytes 1572872 | tf_op jit(solution)/shard_map/ppermute | solution.py:40
  (21 other events, 206.7 us)

commit v2 on v1

--- a/solution.py
+++ b/solution.py
@@ -63,12 +63,6 @@
 
 def cheap():
     return pl.CostEstimate(flops=1, bytes_accessed=1, transcendentals=0)
-
-
-def cost(chunks):
-    return pl.CostEstimate(
-        flops=int(chunks * 3.4e8), bytes_accessed=int(chunks * 6e5), transcendentals=0
-    )
 
 
 def round_volume(volume, info):
@@ -220,8 +214,18 @@
             placed = placing(about, ax).astype(BF16)
             high, low = split(acc[...])
             spread = dot(placed, high) + dot(placed, low)
-            for k in range(3):
-                outs[k][...] = spread[16 * k : 16 * k + 16]
+            outs[1][...] = spread[16:32]
+            odd = lax.rem(about[3], 2)
+
+            @pl.when(odd == 1)
+            def _():
+                outs[0][...] = spread[32:]
+                outs[2][...] = spread[:16]
+
+            @pl.when(odd == 0)
+            def _():
+                outs[0][...] = spread[:16]
+                outs[2][...] = spread[32:]
 
     args = [blocks, info, weights, *shards]
     specs = [SM, SM, HBM] + [VM] * n
@@ -248,23 +252,24 @@
         out_shape=out_shape,
         scratch_shapes=scratch,
         compiler_params=params(2 * n + 4),
-        cost_estimate=cost(n),
+        cost_estimate=cheap(),
         name="project",
     )(*args)
 
 
 def weigh(row_weight, sino, mine, low, high):
-    def body(rw, measured, a, b, c, out, short):
+    def body(rw, measured, a, b, c, out, again, short):
         value = rw[0] * (measured[0] - (a[...] + b[...] + c[...]))
         out[...] = value
+        again[...] = value
         short[...] = value.astype(BF16)
 
     return pl.pallas_call(
         body,
         in_specs=[VM] * 5,
-        out_specs=[VM, VM],
-        out_shape=[
-            jax.ShapeDtypeStruct(mine.shape, F32),
+        out_specs=[VM] * 3,
+        out_shape=[jax.ShapeDtypeStruct(mine.shape, F32)] * 2
+        + [
             jax.ShapeDtypeStruct(mine.shape, BF16),
         ],
         compiler_params=params(12),
@@ -277,11 +282,12 @@
     planes = axial.shape[1]
     detector = rows[0].shape[1]
 
-    def body(about, ax, low_rows, own_rows, high_rows, out):
+    def body(about, ax, first_rows, own_rows, second_rows, out):
         placed = placing(about, ax).T.astype(BF16)
-        window = jnp.concatenate(
-            [low_rows[...].astype(F32), own_rows[...], high_rows[...].astype(F32)], axis=0
-        )
+        odd = lax.rem(about[3], 2) == 1
+        first, second = first_rows[...].astype(F32), second_rows[...].astype(F32)
+        low, high = jnp.where(odd, second, first), jnp.where(odd, first, second)
+        window = jnp.concatenate([low, own_rows[...], high], axis=0)
         high, low = split(window)
         out[...] = (dot(placed, high) + dot(placed, low)).astype(BF16)
 
@@ -352,7 +358,7 @@
             pltpu.SemaphoreType.DMA((n * pieces,)),
         ],
         compiler_params=params(24),
-        cost_estimate=cost(n),
+        cost_estimate=cheap(),
         name="pull",
     )(blocks, info, weights, smeared, *sources, *after)
     return out[0] if joined else out
@@ -424,7 +430,7 @@
     slab = lax.axis_index("slab")
     view = lax.axis_index("view")
     first = band_start[0, 0] - (slab - 1) * rows_here
-    info = jnp.stack([view, first, band_len[0, 0]]).astype(jnp.int32)
+    info = jnp.stack([view, first, band_len[0, 0], slab]).astype(jnp.int32)
 
     def whose(dx, dy):
         return [(dx, dy, False), (dx, dy, True)]
@@ -447,27 +453,33 @@
     )
     far = join(far_low, far_high, total)
     far_over = send(far, ACROSS)
-    t1 = total
-    left_over, right_over = gate([left_over, right_over], t1)
-    total = ahead(whose(0, 1) + whose(2, 0), [over, send(over, CORE), far, send(far, CORE)], total)
-    t2 = total
+    far_swapped = send(far, CORE)
+    total = ahead(whose(0, 1) + [(2, 0, False)], [over, send(over, CORE), far], total)
+    middle = total
+    left_over, right_over = gate([left_over, right_over], total)
     total = ahead(
-        whose(-1, 1) + whose(1, 1),
-        [left_over, send(left_over, CORE), right_over, send(right_over, CORE)],
+        [(2, 0, True)] + whose(-1, 1) + whose(1, 1),
+        [far_swapped, left_over, send(left_over, CORE), right_over, send(right_over, CORE)],
         total,
     )
-    (far_over,) = gate([far_over], t2)
-    below, mine, above = ahead(whose(2, 1), [far_over, send(far_over, CORE)], total, ax)
+    (far_over,) = gate([far_over], middle)
+    to_first, mine, to_second = ahead(whose(2, 1), [far_over, send(far_over, CORE)], total, ax)
 
     count = lax.axis_size("slab")
-    rise = [(i, i + 1) for i in range(count - 1)]
-    fall = [(i + 1, i) for i in range(count - 1)]
-    residual, rounded = weigh(
-        row_weight, sino, mine, lax.ppermute(above, "slab", rise), lax.ppermute(below, "slab", fall)
-    )
-    low_rows = lax.ppermute(rounded, "slab", rise)
-    high_rows = lax.ppermute(rounded, "slab", fall)
-    smeared = smear(info, ax, [low_rows, residual, high_rows])
+    first_swap, second_swap = (
+        [(a, b) for i in range(start, count - 1, 2) for a, b in ((i, i + 1), (i + 1, i))]
+        for start in (1, 0)
+    )
+    residual, own_rows, rounded = weigh(
+        row_weight,
+        sino,
+        mine,
+        lax.ppermute(to_first, "slab", first_swap),
+        lax.ppermute(to_second, "slab", second_swap),
+    )
+    first_rows = lax.ppermute(rounded, "slab", first_swap)
+    second_rows = lax.ppermute(rounded, "slab", second_swap)
+    smeared = smear(info, ax, [first_rows, own_rows, second_rows])
 
     back = functools.partial(pull, weights, blocks, info)
     full = (0, 1)
@@ -481,29 +493,42 @@
     def rounds(offsets, after):
         parts = back(others(*offsets), smeared, after=after, out_dtype=BF16)
         swaps = [send(part, CORE) for part in parts]
-        mine = back(owns(*offsets), smeared, after=[parts[0]])
-        return [[(a, 0, full), (b, 0, full)] for a, b in zip(mine, swaps)]
-
-    far_sum, up_sum, down_sum = combine(rounds([(2, 1), (1, 1), (-1, 1)], []), pixels)
+        return back(owns(*offsets), smeared, after=[parts[0]]), swaps
+
+    def whole(array):
+        return (array, 0, full)
+
+    mine, swaps = rounds([(2, 1), (1, 1), (-1, 1)], [])
+    far_sum, up_sum, down_sum = combine([[whole(a), whole(b)] for a, b in zip(mine, swaps)], pixels)
     from_over = send(far_sum, ACROSS)
     from_left = send(up_sum, UP)
     from_right = send(down_sum, DOWN)
-    to_far, to_over = rounds([(2, 0), (0, 1)], [far_sum])
-    half_up, half_down = combine([to_far + [(from_over, 0, full)]], pixels, 2)
+    mine, swaps = rounds([(2, 0), (0, 1)], [far_sum])
+    from_over, from_left, from_right = gate([from_over, from_left, from_right], mine[0])
+    swaps = gate(swaps, from_over)
+    half_up, half_down = combine([[whole(mine[0]), whole(swaps[0]), whole(from_over)]], pixels, 2)
     half_left = send(half_up, UP)
     half_right = send(half_down, DOWN)
     (over_sum,) = combine(
-        [to_over + [(from_left, 0, full), (from_right, 0, full)]], pixels, after=[half_up]
+        [[whole(mine[1]), whole(swaps[1]), whole(from_left), whole(from_right)]],
+        pixels,
+        after=[half_up],
     )
     over_last = send(over_sum, ACROSS)
-    to_up, to_down, here = rounds([(1, 0), (-1, 0), (0, 0)], [over_sum])
+    mine, swaps = rounds([(1, 0), (-1, 0), (0, 0)], [over_sum])
+    half_left, half_right = gate([half_left, half_right], mine[0])
+    swaps = gate(swaps, half_left)
     up_sum, down_sum = combine(
-        [to_up + [(half_left, 0, (0,))], to_down + [(half_right, -half, (1,))]], pixels
+        [
+            [whole(mine[0]), whole(swaps[0]), (half_left, 0, (0,))],
+            [whole(mine[1]), whole(swaps[1]), (half_right, -half, (1,))],
+        ],
+        pixels,
     )
     left_last = send(up_sum, UP)
     right_last = send(down_sum, DOWN)
     updated = update(
-        volume, col_weight, here[0][0], here[1][0], [over_last, left_last, right_last]
+        volume, col_weight, mine[2], swaps[2], [over_last, left_last, right_last]
     )
     return updated, residual[None]
 

time: 150 us -> 141 us (0.940); the launches traced: 148 us -> 141 us
  starting transfers between devices: 40.7 us -> 36.4 us
  waiting for transfers between devices: 48.8 us -> 46.8 us
    ppermute x4, starting transfers between devices: 19.4 us -> 11.8 us  [the longest x1 6 us: per_device(): lax.ppermute(to_first, 'slab', first_swap)]
    ppermute x32, waiting for transfers between devices: 43.8 us -> 36.9 us  [send(): return lax.ppermute(array, 'view', pairs)]
    ppermute x4, waiting for transfers between devices: 4.99 us -> 9.92 us  [the longest x1 5.28 us: per_device(): lax.ppermute(to_first, 'slab', first_swap)]
    ppermute x32, starting transfers between devices: 21.3 us -> 24.6 us  [send(): return lax.ppermute(array, 'view', pairs)]
  transfers between devices with their start and end apart: 36 -> 36, of which waited for: 18 -> 13; matrix products, arithmetic and copies ran while one was open for 0% -> 0% of each run, Pallas kernels for 22% -> 25%
where the time goes in v2:
time: 141 us
  Pallas kernels  53.7 us (38%)
  waiting for transfers between devices  46.8 us (33%)
  starting transfers between devices  36.4 us (26%)
  between operations  2.35 us (2%)
  local copies, waits for them, and re-layouts  1.94 us (1%)
    ppermute x32, waiting for transfers between devices, send(): return lax.ppermute(array, 'view', pairs)  36.9 us
    pallas_call x6, Pallas kernels, pull(): pl.pallas_call(body, in_specs=[SM, SM, HBM, VM] + [VM] * len(sources) + [...  25.3 us
    ppermute x32, starting transfers between devices, send(): return lax.ppermute(array, 'view', pairs)  24.6 us
    pallas_call x5, Pallas kernels, project(): pl.pallas_call(body, in_specs=specs, out_specs=out_specs, out_shape=out_s...  23 us
    ppermute x1, starting transfers between devices, per_device(): lax.ppermute(to_first, 'slab', first_swap)  6 us
    ppermute x1, starting transfers between devices, per_device(): first_rows = lax.ppermute(rounded, 'slab', first_swap)  5.41 us
    ppermute x1, waiting for transfers between devices, per_device(): lax.ppermute(to_first, 'slab', first_swap)  5.28 us
    ppermute x1, waiting for transfers between devices, per_device(): first_rows = lax.ppermute(rounded, 'slab', first_swap)  4.33 us
  transfers between devices with their start and end apart: 36, of which 13 were waited for; matrix products, arithmetic and copies ran while one was open for 0% of the time, Pallas kernels for 25%

profile of v2, /device:TPU:22, one launch (start us, length us, event | category | flops | bytes accessed | tf_op | source)
XLA Modules:
  0.0 141.2 jit_solution(2155529974259380782)
XLA Ops:
  9.2 3.4 %project.5.refs_3_.earlier.refs_4_ = f32[64,2048]{1,0:T(8,128)S(1)} custom-call(s32[1,256]{1,0:T(1,128)S(1)} %copy-done.5, s32[4]{0:T(128)S(1)} %pad_add_fusion.about, bf16[256,256,256]{2,1,0:T(8,128)(2,1)} %bitcast.14, bf16[64,4096]{1,0:T(8,128)(2,1)S(1)} %round_volume.1.refs_0_, bf16[64,4096]{1,0:T(8,128)(2,1)S(1)} %collective-permute-done.3.refs_1_), custom_call_target="tpu_custom_call" | custom-call | flops 1 | bytes 1 | tf_op jit(solution)/shard_map/project/pallas_call | solution.py:248
  12.7 5.6 %collective-permute-done.2.refs_2_ = bf16[64,4096]{1,0:T(8,128)(2,1)S(1)} collective-permute-done((bf16[64,4096]{1,0:T(8,128)(2,1)S(1)}, bf16[64,4096]{1,0:T(8,128)(2,1)S(1)}, u32[]{:S(2)}, u32[]{:S(2)}) %collective-permute-start.2) | collective-permute-done | bytes 524320 | tf_op jit(solution)/shard_map/ppermute | solution.py:40
  21.1 3.3 %collective-permute-start.4 = (bf16[64,2048]{1,0:T(8,128)(2,1)S(1)}, bf16[64,2048]{1,0:T(8,128)(2,1)S(1)}, u32[]{:S(2)}, u32[]{:S(2)}) collective-permute-start(bf16[64,2048]{1,0:T(8,128)(2,1)S(1)} %cut.2), channel_id=1, source_target_pairs={{0,2},{1,3},{2,4},{3,5},{4,6},{5,7},{6,0},{7,1},{8,10},{9,11},{10,... | collective-permute-start | bytes 786440 | tf_op jit(solution)/shard_map/ppermute | solution.py:40
  24.5 3.2 %collective-permute-start.12 = (bf16[64,4096]{1,0:T(8,128)(2,1)S(1)}, bf16[64,4096]{1,0:T(8,128)(2,1)S(1)}, u32[]{:S(2)}, u32[]{:S(2)}) collective-permute-start(bf16[64,4096]{1,0:T(8,128)(2,1)S(1)} %get-tuple-element.48.refs_0_), channel_id=1, source_target_pairs={{0,2},{1,3},{2,4},{3,5},{4,6},{5,7},{6,0},{7,1},{8,10},{9,11},{10,... | collective-permute-start | bytes 1572872 | tf_op jit(solution)/shard_map/ppermute | solution.py:40
  27.7 5.3 %project.6.earlier.refs_3_ = f32[64,2048]{1,0:T(8,128)S(1)} custom-call(s32[1,256]{1,0:T(1,128)S(1)} %copy-done.6, s32[4]{0:T(128)S(1)} %pad_add_fusion.about, bf16[256,256,256]{2,1,0:T(8,128)(2,1)} %bitcast.15, bf16[64,4096]{1,0:T(8,128)(2,1)S(1)} %get-tuple-element.46.source.refs_0_, bf16[64,4096]{1,0:T(8,128)(2,1)S(1)} %collective-permute-done.6.refs_1_, ...), custom_call_target="tpu_custom_call" | custom-call | flops 1 | bytes 1 | tf_op jit(solution)/shard_map/project/pallas_call | solution.py:248
  33.9 4.4 %project.7.refs_1_.refs_2_.refs_5_ = f32[64,2048]{1,0:T(8,128)S(1)} custom-call(s32[1,256]{1,0:T(1,128)S(1)} %copy-done.6, s32[4]{0:T(128)S(1)} %pad_add_fusion.about, bf16[256,256,256]{2,1,0:T(8,128)(2,1)} %bitcast.16, bf16[64,4096]{1,0:T(8,128)(2,1)S(1)} %get-tuple-element.48.refs_0_, bf16[64,4096]{1,0:T(8,128)(2,1)S(1)} %collective-permute-done.9.refs_1_, ...), custom_call_target="tpu_custom_call" | custom-call | flops 1 | bytes 1 | tf_op jit(solution)/shard_map/project/pallas_call | solution.py:248
  38.3 3.6 %collective-permute-done.13.refs_1_ = bf16[64,4096]{1,0:T(8,128)(2,1)S(1)} collective-permute-done((bf16[64,4096]{1,0:T(8,128)(2,1)S(1)}, bf16[64,4096]{1,0:T(8,128)(2,1)S(1)}, u32[]{:S(2)}, u32[]{:S(2)}) %collective-permute-start.13) | collective-permute-done | bytes 524320 | tf_op jit(solution)/shard_map/ppermute | solution.py:40
  42.4 4.6 %collective-permute-done.8.refs_0_ = bf16[64,4096]{1,0:T(8,128)(2,1)S(1)} collective-permute-done((bf16[64,4096]{1,0:T(8,128)(2,1)S(1)}, bf16[64,4096]{1,0:T(8,128)(2,1)S(1)}, u32[]{:S(2)}, u32[]{:S(2)}) %collective-permute-start.8) | collective-permute-done | bytes 524320 | tf_op jit(solution)/shard_map/ppermute | solution.py:40
  47.0 6.2 %project.8.refs_2_ = f32[64,2048]{1,0:T(8,128)S(1)} custom-call(s32[1,256]{1,0:T(1,128)S(1)} %copy-done.6, s32[4]{0:T(128)S(1)} %pad_add_fusion.about, bf16[256,256,256]{2,1,0:T(8,128)(2,1)} %bitcast.17, bf16[64,4096]{1,0:T(8,128)(2,1)S(1)} %collective-permute-done.11.refs_0_, bf16[64,4096]{1,0:T(8,128)(2,1)S(1)} %get-tuple-element.49.refs_1_, ...), custom_call_target="tpu_custom_call" | custom-call | flops 1 | bytes 1 | tf_op jit(solution)/shard_map/project/pallas_call | solution.py:248
  53.2 3.7 %project.9 = (f32[16,2048]{1,0:T(8,128)S(1)}, f32[16,2048]{1,0:T(8,128)S(1)}, f32[16,2048]{1,0:T(8,128)S(1)}) custom-call(s32[1,256]{1,0:T(1,128)S(1)} %copy-done.6, s32[4]{0:T(128)S(1)} %pad_add_fusion.about, bf16[256,256,256]{2,1,0:T(8,128)(2,1)} %bitcast.18, bf16[64,4096]{1,0:T(8,128)(2,1)S(1)} %gate.8.refs_0_, ...), custom_call_target="tpu_custom_call" | custom-call | flops 1 | bytes 1 | tf_op jit(solution)/shard_map/project/pallas_call | solution.py:248
  56.9 6.0 %collective-permute-start.16 = (f32[16,2048]{1,0:T(8,128)S(1)}, f32[16,2048]{1,0:T(8,128)S(1)}, u32[]{:S(2)}, u32[]{:S(2)}) collective-permute-start(f32[16,2048]{1,0:T(8,128)S(1)} %get-tuple-element.52), channel_id=1, source_target_pairs={{16,32},{32,16},{48,64},{64,48},{80,96},{96,80},{17,33},{33,17},{4... | collective-permute-start | bytes 393224 | tf_op jit(solution)/shard_map/ppermute | solution.py:477
  63.0 5.3 %collective-permute-done.16.b = f32[16,2048]{1,0:T(8,128)S(1)} collective-permute-done((f32[16,2048]{1,0:T(8,128)S(1)}, f32[16,2048]{1,0:T(8,128)S(1)}, u32[]{:S(2)}, u32[]{:S(2)}) %collective-permute-start.16) | collective-permute-done | bytes 131104 | tf_op jit(solution)/shard_map/ppermute | solution.py:477
  69.6 5.4 %collective-permute-start.18 = (bf16[16,2048]{1,0:T(8,128)(2,1)S(1)}, bf16[16,2048]{1,0:T(8,128)(2,1)S(1)}, u32[]{:S(2)}, u32[]{:S(2)}) collective-permute-start(bf16[16,2048]{1,0:T(8,128)(2,1)S(1)} %get-tuple-element.54), channel_id=1, source_target_pairs={{16,32},{32,16},{48,64},{64,48},{80,96},{96,80},{17,33},{33,17},{4... | collective-permute-start | bytes 196616 | tf_op jit(solution)/shard_map/ppermute | solution.py:480
  75.1 4.3 %collective-permute-done.18.first_rows = bf16[16,2048]{1,0:T(8,128)(2,1)S(1)} collective-permute-done((bf16[16,2048]{1,0:T(8,128)(2,1)S(1)}, bf16[16,2048]{1,0:T(8,128)(2,1)S(1)}, u32[]{:S(2)}, u32[]{:S(2)}) %collective-permute-start.18) | collective-permute-done | bytes 65568 | tf_op jit(solution)/shard_map/ppermute | solution.py:480
  80.4 4.5 %pull.6 = (bf16[64,4096]{1,0:T(8,128)(2,1)S(1)}, bf16[64,4096]{1,0:T(8,128)(2,1)S(1)}, bf16[64,4096]{1,0:T(8,128)(2,1)S(1)}) custom-call(s32[1,256]{1,0:T(1,128)S(1)} %copy-done.6, s32[4]{0:T(128)S(1)} %pad_add_fusion.about, bf16[256,256,256]{2,1,0:T(8,128)(2,1)} %bitcast.19, bf16[64,2048]{1,0:T(8,128)(2,1)S(1)} %smear.1.sm), custom_call_target="tpu_custom_call" | custom-call | flops 1 | bytes 1 | tf_op jit(solution)/shard_map/pull/pallas_call | solution.py:351
  85.6 4.5 %pull.7 = (f32[64,4096]{1,0:T(8,128)S(1)}, f32[64,4096]{1,0:T(8,128)S(1)}, f32[64,4096]{1,0:T(8,128)S(1)}) custom-call(s32[1,256]{1,0:T(1,128)S(1)} %copy-done.6, s32[4]{0:T(128)S(1)} %pad_add_fusion.about, bf16[256,256,256]{2,1,0:T(8,128)(2,1)} %bitcast.20, bf16[64,2048]{1,0:T(8,128)(2,1)S(1)} %smear.1.sm, bf16[64,4096]{1,0:T(8,128)(2,1)S(1)} %get-tuple-element.56.refs_0_), custom_call_target="tpu_custom_call" | custom-call | flops 1 | bytes 1 | tf_op jit(solution)/shard_map/pull/pallas_call | solution.py:351
  93.6 3.6 %pull.8 = (bf16[64,4096]{1,0:T(8,128)(2,1)S(1)}, bf16[64,4096]{1,0:T(8,128)(2,1)S(1)}) custom-call(s32[1,256]{1,0:T(1,128)S(1)} %copy-done.6, s32[4]{0:T(128)S(1)} %pad_add_fusion.about, bf16[256,256,256]{2,1,0:T(8,128)(2,1)} %bitcast.21, bf16[64,2048]{1,0:T(8,128)(2,1)S(1)} %smear.1.sm, bf16[64,4096]{1,0:T(8,128)(2,1)S(1)} %get-tuple-element.62.refs_0_), custom_call_target="tpu_custom_call" | custom-call | flops 1 | bytes 1 | tf_op jit(solution)/shard_map/pull/pallas_call | solution.py:351
  97.8 3.6 %pull.9 = (f32[64,4096]{1,0:T(8,128)S(1)}, f32[64,4096]{1,0:T(8,128)S(1)}) custom-call(s32[1,256]{1,0:T(1,128)S(1)} %copy-done.6, s32[4]{0:T(128)S(1)} %pad_add_fusion.about, bf16[256,256,256]{2,1,0:T(8,128)(2,1)} %bitcast.22, bf16[64,2048]{1,0:T(8,128)(2,1)S(1)} %smear.1.sm, bf16[64,4096]{1,0:T(8,128)(2,1)S(1)} %get-tuple-element.63.refs_0_), custom_call_target="tpu_custom_call" | custom-call | flops 1 | bytes 1 | tf_op jit(solution)/shard_map/pull/pallas_call | solution.py:351
  101.4 3.4 %collective-permute-done.26.refs_1_ = bf16[64,4096]{1,0:T(8,128)(2,1)S(1)} collective-permute-done((bf16[64,4096]{1,0:T(8,128)(2,1)S(1)}, bf16[64,4096]{1,0:T(8,128)(2,1)S(1)}, u32[]{:S(2)}, u32[]{:S(2)}) %collective-permute-start.26) | collective-permute-done | bytes 524320 | tf_op jit(solution)/shard_map/ppermute | solution.py:40
  106.7 4.6 %pull.10 = (bf16[64,4096]{1,0:T(8,128)(2,1)S(1)}, bf16[64,4096]{1,0:T(8,128)(2,1)S(1)}, bf16[64,4096]{1,0:T(8,128)(2,1)S(1)}) custom-call(s32[1,256]{1,0:T(1,128)S(1)} %copy-done.6, s32[4]{0:T(128)S(1)} %pad_add_fusion.about, bf16[256,256,256]{2,1,0:T(8,128)(2,1)} %bitcast.23, bf16[64,2048]{1,0:T(8,128)(2,1)S(1)} %smear.1.sm, ...), custom_call_target="tpu_custom_call" | custom-call | flops 1 | bytes 1 | tf_op jit(solution)/shard_map/pull/pallas_call | solution.py:351
  112.2 3.0 %collective-permute-start.31 = (bf16[64,2048]{1,0:T(8,128)(2,1)S(1)}, bf16[64,2048]{1,0:T(8,128)(2,1)S(1)}, u32[]{:S(2)}, u32[]{:S(2)}) collective-permute-start(bf16[64,2048]{1,0:T(8,128)(2,1)S(1)} %get-tuple-element.74.refs_4_), channel_id=1, source_target_pairs={{0,2},{1,3},{2,4},{3,5},{4,6},{5,7},{6,0},{7,1},{8,10},{9,11},{10,... | collective-permute-start | bytes 786440 | tf_op jit(solution)/shard_map/ppermute | solution.py:40
  115.2 4.5 %pull.11 = (f32[64,4096]{1,0:T(8,128)S(1)}, f32[64,4096]{1,0:T(8,128)S(1)}, f32[64,4096]{1,0:T(8,128)S(1)}) custom-call(s32[1,256]{1,0:T(1,128)S(1)} %copy-done.6, s32[4]{0:T(128)S(1)} %pad_add_fusion.about, bf16[256,256,256]{2,1,0:T(8,128)(2,1)} %bitcast.24, bf16[64,2048]{1,0:T(8,128)(2,1)S(1)} %smear.1.sm, bf16[64,4096]{1,0:T(8,128)(2,1)S(1)} %get-tuple-element.75.refs_0_), custom_call_target="tpu_custom_call" | custom-call | flops 1 | bytes 1 | tf_op jit(solution)/shard_map/pull/pallas_call | solution.py:351
  125.2 10.0 %collective-permute-done.33.a = bf16[64,4096]{1,0:T(8,128)(2,1)S(1)} collective-permute-done((bf16[64,4096]{1,0:T(8,128)(2,1)S(1)}, bf16[64,4096]{1,0:T(8,128)(2,1)S(1)}, u32[]{:S(2)}, u32[]{:S(2)}) %collective-permute-start.33) | collective-permute-done | bytes 524320 | tf_op jit(solution)/shard_map/ppermute | solution.py:40
  136.4 2.8 %collective-permute-done.35.c = bf16[64,4096]{1,0:T(8,128)(2,1)S(1)} collective-permute-done((bf16[64,4096]{1,0:T(8,128)(2,1)S(1)}, bf16[64,4096]{1,0:T(8,128)(2,1)S(1)}, u32[]{:S(2)}, u32[]{:S(2)}) %collective-permute-start.35) | collective-permute-done | bytes 524320 | tf_op jit(solution)/shard_map/ppermute | solution.py:40
  (94 shorter events, 30.1 us)
Async XLA Ops:
  3.9 14.3 %collective-permute-start.2 = (bf16[64,4096]{1,0:T(8,128)(2,1)S(1)}, bf16[64,4096]{1,0:T(8,128)(2,1)S(1)}, u32[]{:S(2)}, u32[]{:S(2)}) collective-permute-start(bf16[64,4096]{1,0:T(8,128)(2,1)S(1)} %round_volume.1.refs_0_), channel_id=1, source_target_pairs={{0,8},{1,9},{2,10},{3,11},{4,12},{5,13},{6,14},{7,15},{8,0},{9,1},... | collective-permute-start | bytes 1572872 | tf_op jit(solution)/shard_map/ppermute | solution.py:40
  5.3 15.2 %collective-permute-start.1 = (bf16[64,4096]{1,0:T(8,128)(2,1)S(1)}, bf16[64,4096]{1,0:T(8,128)(2,1)S(1)}, u32[]{:S(2)}, u32[]{:S(2)}) collective-permute-start(bf16[64,4096]{1,0:T(8,128)(2,1)S(1)} %round_volume.1.refs_0_), channel_id=1, source_target_pairs={{0,6},{1,7},{2,0},{3,1},{4,2},{5,3},{6,4},{7,5},{8,14},{9,15},{10,... | collective-permute-start | bytes 1572872 | tf_op jit(solution)/shard_map/ppermute | solution.py:40
  6.1 14.4 %collective-permute-start = (bf16[64,4096]{1,0:T(8,128)(2,1)S(1)}, bf16[64,4096]{1,0:T(8,128)(2,1)S(1)}, u32[]{:S(2)}, u32[]{:S(2)}) collective-permute-start(bf16[64,4096]{1,0:T(8,128)(2,1)S(1)} %round_volume.1.refs_0_), channel_id=1, source_target_pairs={{0,2},{1,3},{2,4},{3,5},{4,6},{5,7},{6,0},{7,1},{8,10},{9,11},{10,... | collective-permute-start | bytes 1572872 | tf_op jit(solution)/shard_map/ppermute | solution.py:40
  21.0 11.9 %collective-permute-start.5 = (bf16[64,2048]{1,0:T(8,128)(2,1)S(1)}, bf16[64,2048]{1,0:T(8,128)(2,1)S(1)}, u32[]{:S(2)}, u32[]{:S(2)}) collective-permute-start(bf16[64,2048]{1,0:T(8,128)(2,1)S(1)} %cut.3), channel_id=1, source_target_pairs={{0,6},{1,7},{2,0},{3,1},{4,2},{5,3},{6,4},{7,5},{8,14},{9,15},{10,... | collective-permute-start | bytes 786440 | tf_op jit(solution)/shard_map/ppermute | solution.py:40
  21.1 11.8 %collective-permute-start.4 = (bf16[64,2048]{1,0:T(8,128)(2,1)S(1)}, bf16[64,2048]{1,0:T(8,128)(2,1)S(1)}, u32[]{:S(2)}, u32[]{:S(2)}) collective-permute-start(bf16[64,2048]{1,0:T(8,128)(2,1)S(1)} %cut.2), channel_id=1, source_target_pairs={{0,2},{1,3},{2,4},{3,5},{4,6},{5,7},{6,0},{7,1},{8,10},{9,11},{10,... | collective-permute-start | bytes 786440 | tf_op jit(solution)/shard_map/ppermute | solution.py:40
  24.4 9.5 %collective-permute-start.9 = (bf16[64,4096]{1,0:T(8,128)(2,1)S(1)}, bf16[64,4096]{1,0:T(8,128)(2,1)S(1)}, u32[]{:S(2)}, u32[]{:S(2)}) collective-permute-start(bf16[64,4096]{1,0:T(8,128)(2,1)S(1)} %get-tuple-element.48.refs_0_), channel_id=1, source_target_pairs={{0,1},{1,0},{2,3},{3,2},{4,5},{5,4},{6,7},{7,6},{8,9},{9,8},{10,11... | collective-permute-start | bytes 1572872 | tf_op jit(solution)/shard_map/ppermute | solution.py:40
  24.4 17.4 %collective-permute-start.13 = (bf16[64,4096]{1,0:T(8,128)(2,1)S(1)}, bf16[64,4096]{1,0:T(8,128)(2,1)S(1)}, u32[]{:S(2)}, u32[]{:S(2)}) collective-permute-start(bf16[64,4096]{1,0:T(8,128)(2,1)S(1)} %get-tuple-element.48.refs_0_), channel_id=1, source_target_pairs={{0,6},{1,7},{2,0},{3,1},{4,2},{5,3},{6,4},{7,5},{8,14},{9,15},{10,... | collective-permute-start | bytes 1572872 | tf_op jit(solution)/shard_map/ppermute | solution.py:40
  24.5 17.4 %collective-permute-start.12 = (bf16[64,4096]{1,0:T(8,128)(2,1)S(1)}, bf16[64,4096]{1,0:T(8,128)(2,1)S(1)}, u32[]{:S(2)}, u32[]{:S(2)}) collective-permute-start(bf16[64,4096]{1,0:T(8,128)(2,1)S(1)} %get-tuple-element.48.refs_0_), channel_id=1, source_target_pairs={{0,2},{1,3},{2,4},{3,5},{4,6},{5,7},{6,0},{7,1},{8,10},{9,11},{10,... | collective-permute-start | bytes 1572872 | tf_op jit(solution)/shard_map/ppermute | solution.py:40
  33.1 13.9 %collective-permute-start.8 = (bf16[64,4096]{1,0:T(8,128)(2,1)S(1)}, bf16[64,4096]{1,0:T(8,128)(2,1)S(1)}, u32[]{:S(2)}, u32[]{:S(2)}) collective-permute-start(bf16[64,4096]{1,0:T(8,128)(2,1)S(1)} %join.1.refs_2_), channel_id=1, source_target_pairs={{0,8},{1,9},{2,10},{3,11},{4,12},{5,13},{6,14},{7,15},{8,0},{9,1},... | collective-permute-start | bytes 1572872 | tf_op jit(solution)/shard_map/ppermute | solution.py:40
  33.9 13.0 %collective-permute-start.11 = (bf16[64,4096]{1,0:T(8,128)(2,1)S(1)}, bf16[64,4096]{1,0:T(8,128)(2,1)S(1)}, u32[]{:S(2)}, u32[]{:S(2)}) collective-permute-start(bf16[64,4096]{1,0:T(8,128)(2,1)S(1)} %join.1.refs_2_), channel_id=1, source_target_pairs={{0,1},{1,0},{2,3},{3,2},{4,5},{5,4},{6,7},{7,6},{8,9},{9,8},{10,11... | collective-permute-start | bytes 1572872 | tf_op jit(solution)/shard_map/ppermute | solution.py:40
  56.9 11.4 %collective-permute-start.16 = (f32[16,2048]{1,0:T(8,128)S(1)}, f32[16,2048]{1,0:T(8,128)S(1)}, u32[]{:S(2)}, u32[]{:S(2)}) collective-permute-start(f32[16,2048]{1,0:T(8,128)S(1)} %get-tuple-element.52), channel_id=1, source_target_pairs={{16,32},{32,16},{48,64},{64,48},{80,96},{96,80},{17,33},{33,17},{4... | collective-permute-start | bytes 393224 | tf_op jit(solution)/shard_map/ppermute | solution.py:477
  69.6 9.8 %collective-permute-start.18 = (bf16[16,2048]{1,0:T(8,128)(2,1)S(1)}, bf16[16,2048]{1,0:T(8,128)(2,1)S(1)}, u32[]{:S(2)}, u32[]{:S(2)}) collective-permute-start(bf16[16,2048]{1,0:T(8,128)(2,1)S(1)} %get-tuple-element.54), channel_id=1, source_target_pairs={{16,32},{32,16},{48,64},{64,48},{80,96},{96,80},{17,33},{33,17},{4... | collective-permute-start | bytes 196616 | tf_op jit(solution)/shard_map/ppermute | solution.py:480
  90.4 14.3 %collective-permute-start.26 = (bf16[64,4096]{1,0:T(8,128)(2,1)S(1)}, bf16[64,4096]{1,0:T(8,128)(2,1)S(1)}, u32[]{:S(2)}, u32[]{:S(2)}) collective-permute-start(bf16[64,4096]{1,0:T(8,128)(2,1)S(1)} %get-tuple-element.66), channel_id=1, source_target_pairs={{0,2},{1,3},{2,4},{3,5},{4,6},{5,7},{6,0},{7,1},{8,10},{9,11},{10,... | collective-permute-start | bytes 1572872 | tf_op jit(solution)/shard_map/ppermute | solution.py:40
  91.1 15.2 %collective-permute-start.27 = (bf16[64,4096]{1,0:T(8,128)(2,1)S(1)}, bf16[64,4096]{1,0:T(8,128)(2,1)S(1)}, u32[]{:S(2)}, u32[]{:S(2)}) collective-permute-start(bf16[64,4096]{1,0:T(8,128)(2,1)S(1)} %get-tuple-element.67), channel_id=1, source_target_pairs={{0,6},{1,7},{2,0},{3,1},{4,2},{5,3},{6,4},{7,5},{8,14},{9,15},{10,... | collective-permute-start | bytes 1572872 | tf_op jit(solution)/shard_map/ppermute | solution.py:40
  92.5 13.7 %collective-permute-start.25 = (bf16[64,4096]{1,0:T(8,128)(2,1)S(1)}, bf16[64,4096]{1,0:T(8,128)(2,1)S(1)}, u32[]{:S(2)}, u32[]{:S(2)}) collective-permute-start(bf16[64,4096]{1,0:T(8,128)(2,1)S(1)} %get-tuple-element.62.refs_0_), channel_id=1, source_target_pairs={{0,8},{1,9},{2,10},{3,11},{4,12},{5,13},{6,14},{7,15},{8,0},{9,1},... | collective-permute-start | bytes 1572872 | tf_op jit(solution)/shard_map/ppermute | solution.py:40
  97.2 9.0 %collective-permute-start.24 = (bf16[64,4096]{1,0:T(8,128)(2,1)S(1)}, bf16[64,4096]{1,0:T(8,128)(2,1)S(1)}, u32[]{:S(2)}, u32[]{:S(2)}) collective-permute-start(bf16[64,4096]{1,0:T(8,128)(2,1)S(1)} %get-tuple-element.65), channel_id=1, source_target_pairs={{0,1},{1,0},{2,3},{3,2},{4,5},{5,4},{6,7},{7,6},{8,9},{9,8},{10,11... | collective-permute-start | bytes 1572872 | tf_op jit(solution)/shard_map/ppermute | solution.py:40
  111.3 11.6 %collective-permute-start.29 = (bf16[64,4096]{1,0:T(8,128)(2,1)S(1)}, bf16[64,4096]{1,0:T(8,128)(2,1)S(1)}, u32[]{:S(2)}, u32[]{:S(2)}) collective-permute-start(bf16[64,4096]{1,0:T(8,128)(2,1)S(1)} %get-tuple-element.77), channel_id=1, source_target_pairs={{0,1},{1,0},{2,3},{3,2},{4,5},{5,4},{6,7},{7,6},{8,9},{9,8},{10,11... | collective-permute-start | bytes 1572872 | tf_op jit(solution)/shard_map/ppermute | solution.py:40
  111.4 11.5 %collective-permute-start.30 = (bf16[64,4096]{1,0:T(8,128)(2,1)S(1)}, bf16[64,4096]{1,0:T(8,128)(2,1)S(1)}, u32[]{:S(2)}, u32[]{:S(2)}) collective-permute-start(bf16[64,4096]{1,0:T(8,128)(2,1)S(1)} %get-tuple-element.78), channel_id=1, source_target_pairs={{0,1},{1,0},{2,3},{3,2},{4,5},{5,4},{6,7},{7,6},{8,9},{9,8},{10,11... | collective-permute-start | bytes 1572872 | tf_op jit(solution)/shard_map/ppermute | solution.py:40
  111.9 11.0 %collective-permute-start.28 = (bf16[64,4096]{1,0:T(8,128)(2,1)S(1)}, bf16[64,4096]{1,0:T(8,128)(2,1)S(1)}, u32[]{:S(2)}, u32[]{:S(2)}) collective-permute-start(bf16[64,4096]{1,0:T(8,128)(2,1)S(1)} %get-tuple-element.75.refs_0_), channel_id=1, source_target_pairs={{0,1},{1,0},{2,3},{3,2},{4,5},{5,4},{6,7},{7,6},{8,9},{9,8},{10,11... | collective-permute-start | bytes 1572872 | tf_op jit(solution)/shard_map/ppermute | solution.py:40
  112.0 9.9 %collective-permute-start.32 = (bf16[64,2048]{1,0:T(8,128)(2,1)S(1)}, bf16[64,2048]{1,0:T(8,128)(2,1)S(1)}, u32[]{:S(2)}, u32[]{:S(2)}) collective-permute-start(bf16[64,2048]{1,0:T(8,128)(2,1)S(1)} %get-tuple-element.79), channel_id=1, source_target_pairs={{0,6},{1,7},{2,0},{3,1},{4,2},{5,3},{6,4},{7,5},{8,14},{9,15},{10,... | collective-permute-start | bytes 786440 | tf_op jit(solution)/shard_map/ppermute | solution.py:40
  112.2 10.6 %collective-permute-start.31 = (bf16[64,2048]{1,0:T(8,128)(2,1)S(1)}, bf16[64,2048]{1,0:T(8,128)(2,1)S(1)}, u32[]{:S(2)}, u32[]{:S(2)}) collective-permute-start(bf16[64,2048]{1,0:T(8,128)(2,1)S(1)} %get-tuple-element.74.refs_4_), channel_id=1, source_target_pairs={{0,2},{1,3},{2,4},{3,5},{4,6},{5,7},{6,0},{7,1},{8,10},{9,11},{10,... | collective-permute-start | bytes 786440 | tf_op jit(solution)/shard_map/ppermute | solution.py:40
  121.8 13.5 %collective-permute-start.33 = (bf16[64,4096]{1,0:T(8,128)(2,1)S(1)}, bf16[64,4096]{1,0:T(8,128)(2,1)S(1)}, u32[]{:S(2)}, u32[]{:S(2)}) collective-permute-start(bf16[64,4096]{1,0:T(8,128)(2,1)S(1)} %combine.6.refs_0_), channel_id=1, source_target_pairs={{0,8},{1,9},{2,10},{3,11},{4,12},{5,13},{6,14},{7,15},{8,0},{9,1},... | collective-permute-start | bytes 1572872 | tf_op jit(solution)/shard_map/ppermute | solution.py:40
  123.1 13.3 %collective-permute-start.34 = (bf16[64,4096]{1,0:T(8,128)(2,1)S(1)}, bf16[64,4096]{1,0:T(8,128)(2,1)S(1)}, u32[]{:S(2)}, u32[]{:S(2)}) collective-permute-start(bf16[64,4096]{1,0:T(8,128)(2,1)S(1)} %get-tuple-element.87), channel_id=1, source_target_pairs={{0,2},{1,3},{2,4},{3,5},{4,6},{5,7},{6,0},{7,1},{8,10},{9,11},{10,... | collective-permute-start | bytes 1572872 | tf_op jit(solution)/shard_map/ppermute | solution.py:40
  125.1 14.1 %collective-permute-start.35 = (bf16[64,4096]{1,0:T(8,128)(2,1)S(1)}, bf16[64,4096]{1,0:T(8,128)(2,1)S(1)}, u32[]{:S(2)}, u32[]{:S(2)}) collective-permute-start(bf16[64,4096]{1,0:T(8,128)(2,1)S(1)} %get-tuple-element.88), channel_id=1, source_target_pairs={{0,6},{1,7},{2,0},{3,1},{4,2},{5,3},{6,4},{7,5},{8,14},{9,15},{10,... | collective-permute-start | bytes 1572872 | tf_op jit(solution)/shard_map/ppermute | solution.py:40
  (20 other events, 221.9 us)

commit v3 on v2

--- a/solution.py
+++ b/solution.py
@@ -278,44 +278,29 @@
     )(row_weight, sino, mine, low, high)
 
 
-def smear(info, axial, rows):
-    planes = axial.shape[1]
-    detector = rows[0].shape[1]
-
-    def body(about, ax, first_rows, own_rows, second_rows, out):
-        placed = placing(about, ax).T.astype(BF16)
-        odd = lax.rem(about[3], 2) == 1
-        first, second = first_rows[...].astype(F32), second_rows[...].astype(F32)
-        low, high = jnp.where(odd, second, first), jnp.where(odd, first, second)
-        window = jnp.concatenate([low, own_rows[...], high], axis=0)
-        high, low = split(window)
-        out[...] = (dot(placed, high) + dot(placed, low)).astype(BF16)
-
-    return pl.pallas_call(
-        body,
-        in_specs=[SM, VM, VM, VM, VM],
-        out_specs=VM,
-        out_shape=jax.ShapeDtypeStruct((planes, detector), BF16),
-        compiler_params=params(12),
-        cost_estimate=cheap(),
-        name="smear",
-    )(info, axial, *rows)
-
-
-def pull(weights, blocks, info, places, smeared, adds=None, after=(), out_dtype=F32, joined=False):
+def smear(about, ax, rows, out):
+    placed = placing(about, ax).T.astype(BF16)
+    odd = lax.rem(about[3], 2) == 1
+    first, second = rows[0][...].astype(F32), rows[2][...].astype(F32)
+    low, high = jnp.where(odd, second, first), jnp.where(odd, first, second)
+    high, low = split(jnp.concatenate([low, rows[1][...], high], axis=0))
+    out[...] = (dot(placed, high) + dot(placed, low)).astype(BF16)
+
+
+def pull(weights, blocks, info, places, smeared, after=(), out_dtype=F32, bands=None):
     width, columns = weights.shape[1], weights.shape[2]
-    planes = smeared.shape[0]
+    own = bands is not None
+    given = list(bands) if own else [smeared]
+    planes = bands[0].shape[1] if own else smeared.shape[0]
     tiles = weights.shape[0] // (4 * NX)
     pixels = tiles * width
     n = len(places)
-    adds = adds or []
-    sources = list({id(array): array for array, _ in adds}.values())
     piece = 8
     pieces = tiles // piece
 
-    def body(blk, about, w, sm, *refs):
-        given = dict(zip([id(a) for a in sources], refs[: len(sources)]))
-        outs = refs[len(sources) + len(after) : -2]
+    def body(blk, about, w, *refs):
+        args = refs[: len(given)]
+        outs = refs[len(given) + len(after) : -2]
         slots, sems = refs[-2:]
         origins = [base_of(about, *places[p], tiles) for p in range(n)]
         copies = [
@@ -329,8 +314,12 @@
         ]
         for copy in copies:
             copy.start()
+        if own:
+            sm = outs[n]
+            smear(about, args[0], args[1:], sm)
+        else:
+            sm = args[0]
         for p in range(n):
-            out, shift = (outs[0], p * pixels) if joined else (outs[p], 0)
             for q in range(pieces):
                 copies[p * pieces + q].wait()
                 for i in range(q * piece, (q + 1) * piece):
@@ -341,18 +330,16 @@
                         NT,
                         preferred_element_type=F32,
                     )
-                    if adds:
-                        array, first = adds[p]
-                        first += i * width
-                        value += given[id(array)][:, first : first + width].astype(F32)
-                    out[:, shift + i * width : shift + (i + 1) * width] = value.astype(out.dtype)
-
-    shapes = [(planes, n * pixels)] if joined else [(planes, pixels)] * n
-    out = pl.pallas_call(
-        body,
-        in_specs=[SM, SM, HBM, VM] + [VM] * len(sources) + [ANY] * len(after),
-        out_specs=[VM] * len(shapes),
-        out_shape=[jax.ShapeDtypeStruct(shape, out_dtype) for shape in shapes],
+                    outs[p][:, i * width : (i + 1) * width] = value.astype(out_dtype)
+
+    out_shape = [jax.ShapeDtypeStruct((planes, pixels), out_dtype)] * n
+    if own:
+        out_shape.append(jax.ShapeDtypeStruct((planes, bands[1].shape[1]), BF16))
+    return pl.pallas_call(
+        body,
+        in_specs=[SM, SM, HBM] + [VM] * len(given) + [ANY] * len(after),
+        out_specs=[VM] * len(out_shape),
+        out_shape=out_shape,
         scratch_shapes=[
             pltpu.VMEM((n * tiles, width, columns), BF16),
             pltpu.SemaphoreType.DMA((n * pieces,)),
@@ -360,8 +347,7 @@
         compiler_params=params(24),
         cost_estimate=cheap(),
         name="pull",
-    )(blocks, info, weights, smeared, *sources, *after)
-    return out[0] if joined else out
+    )(blocks, info, weights, *given, *after)
 
 
 def combine(sums, size, cuts=1, after=()):
@@ -443,7 +429,8 @@
     weights = pltpu.with_memory_space_constraint(transaxial[0], pltpu.HBM)
     ahead = functools.partial(project, weights, blocks, info)
     total = ahead(whose(0, 0), [own, swapped])
-    left, right, over = gate([left, right, over], total)
+    left, right = gate([left, right], total)
+    (over,) = gate([over], left)
     far_low = send(cut(left, 0, half, total), UP)
     far_high = send(cut(right, half, half, total), DOWN)
     left_over = send(over, UP)
@@ -479,7 +466,6 @@
     )
     first_rows = lax.ppermute(rounded, "slab", first_swap)
     second_rows = lax.ppermute(rounded, "slab", second_swap)
-    smeared = smear(info, ax, [first_rows, own_rows, second_rows])
 
     back = functools.partial(pull, weights, blocks, info)
     full = (0, 1)
@@ -490,21 +476,30 @@
     def owns(*offsets):
         return [(dx, dy, False) for dx, dy in offsets]
 
-    def rounds(offsets, after):
+    def swap_parts(offsets, after):
         parts = back(others(*offsets), smeared, after=after, out_dtype=BF16)
-        swaps = [send(part, CORE) for part in parts]
-        return back(owns(*offsets), smeared, after=[parts[0]]), swaps
+        return parts[0], [send(part, CORE) for part in parts]
 
     def whole(array):
         return (array, 0, full)
 
-    mine, swaps = rounds([(2, 1), (1, 1), (-1, 1)], [])
+    offsets = [(2, 1), (1, 1), (-1, 1)]
+    *parts, smeared = back(
+        others(*offsets), None, out_dtype=BF16, bands=[ax, first_rows, own_rows, second_rows]
+    )
+    swaps = [send(part, CORE) for part in parts]
+    part = parts[0]
+    mine = back(owns(*offsets), smeared, after=[part])
     far_sum, up_sum, down_sum = combine([[whole(a), whole(b)] for a, b in zip(mine, swaps)], pixels)
     from_over = send(far_sum, ACROSS)
     from_left = send(up_sum, UP)
     from_right = send(down_sum, DOWN)
-    mine, swaps = rounds([(2, 0), (0, 1)], [far_sum])
-    from_over, from_left, from_right = gate([from_over, from_left, from_right], mine[0])
+    offsets = [(2, 0), (0, 1)]
+    part, swaps = swap_parts(offsets, [far_sum])
+    mine = back(owns(*offsets), smeared, after=[part])
+    offsets = [(1, 0), (-1, 0), (0, 0)]
+    part, last_swaps = swap_parts(offsets, [mine[0]])
+    from_over, from_left, from_right = gate([from_over, from_left, from_right], part)
     swaps = gate(swaps, from_over)
     half_up, half_down = combine([[whole(mine[0]), whole(swaps[0]), whole(from_over)]], pixels, 2)
     half_left = send(half_up, UP)
@@ -515,9 +510,9 @@
         after=[half_up],
     )
     over_last = send(over_sum, ACROSS)
-    mine, swaps = rounds([(1, 0), (-1, 0), (0, 0)], [over_sum])
+    mine = back(owns(*offsets), smeared, after=[over_sum])
     half_left, half_right = gate([half_left, half_right], mine[0])
-    swaps = gate(swaps, half_left)
+    swaps = gate(last_swaps, half_left)
     up_sum, down_sum = combine(
         [
             [whole(mine[0]), whole(swaps[0]), (half_left, 0, (0,))],

time: 141 us -> 136 us (0.965)
  waiting for transfers between devices: 46.8 us -> 39.1 us
  starting transfers between devices: 36.4 us -> 38.8 us
    ppermute x32, waiting for transfers between devices: 36.9 us -> 29.4 us  [send(): return lax.ppermute(array, 'view', pairs)]
    ppermute x32, starting transfers between devices: 24.6 us -> 27.2 us  [send(): return lax.ppermute(array, 'view', pairs)]
    pallas_call x7 -> x6, Pallas kernels: 26.3 us -> 25.5 us  [pull(): pl.pallas_call(body, in_specs=[SM, SM, HBM] + [VM] * len(given) + [ANY] *...]
  transfers between devices with their start and end apart: 36 -> 36, of which waited for: 13 -> 11; matrix products, arithmetic and copies ran while one was open for 0% -> 0% of each run, Pallas kernels for 25% -> 30%
where the time goes in v3:
time: 136 us; the launch traced here: 135 us
  Pallas kernels  52.8 us (39%)
  waiting for transfers between devices  39.1 us (29%)
  starting transfers between devices  38.8 us (29%)
  between operations  2.33 us (2%)
  local copies, waits for them, and re-layouts  1.94 us (1%)
    ppermute x32, waiting for transfers between devices, send(): return lax.ppermute(array, 'view', pairs)  29.4 us
    ppermute x32, starting transfers between devices, send(): return lax.ppermute(array, 'view', pairs)  27.2 us
    pallas_call x6, Pallas kernels, pull(): pl.pallas_call(body, in_specs=[SM, SM, HBM] + [VM] * len(given) + [ANY] *...  25.5 us
    pallas_call x5, Pallas kernels, project(): pl.pallas_call(body, in_specs=specs, out_specs=out_specs, out_shape=out_s...  23 us
    ppermute x1, starting transfers between devices, per_device(): lax.ppermute(to_first, 'slab', first_swap)  5.7 us
    ppermute x1, starting transfers between devices, per_device(): first_rows = lax.ppermute(rounded, 'slab', first_swap)  5.41 us
    ppermute x1, waiting for transfers between devices, per_device(): lax.ppermute(to_first, 'slab', first_swap)  5.4 us
    ppermute x1, waiting for transfers between devices, per_device(): first_rows = lax.ppermute(rounded, 'slab', first_swap)  4.33 us
  transfers between devices with their start and end apart: 36, of which 11 were waited for; matrix products, arithmetic and copies ran while one was open for 0% of the time, Pallas kernels for 30%

profile of v3, /device:TPU:22, one launch (start us, length us, event | category | flops | bytes accessed | tf_op | source)
XLA Modules:
  0.0 135.1 jit_solution(12868241314489547060)
XLA Ops:
  4.8 2.4 %collective-permute-start = (bf16[64,4096]{1,0:T(8,128)(2,1)S(1)}, bf16[64,4096]{1,0:T(8,128)(2,1)S(1)}, u32[]{:S(2)}, u32[]{:S(2)}) collective-permute-start(bf16[64,4096]{1,0:T(8,128)(2,1)S(1)} %round_volume.1.refs_0_), channel_id=1, source_target_pairs={{0,2},{1,3},{2,4},{3,5},{4,6},{5,7},{6,0},{7,1},{8,10},{9,11},{10,... | collective-permute-start | bytes 1572872 | tf_op jit(solution)/shard_map/ppermute | solution.py:40
  9.2 3.4 %project.5.refs_2_.earlier.refs_4_ = f32[64,2048]{1,0:T(8,128)S(1)} custom-call(s32[1,256]{1,0:T(1,128)S(1)} %copy-done.5, s32[4]{0:T(128)S(1)} %pad_add_fusion.about, bf16[256,256,256]{2,1,0:T(8,128)(2,1)} %bitcast.14, bf16[64,4096]{1,0:T(8,128)(2,1)S(1)} %round_volume.1.refs_0_, bf16[64,4096]{1,0:T(8,128)(2,1)S(1)} %collective-permute-done.2.refs_1_), custom_call_target="tpu_custom_call" | custom-call | flops 1 | bytes 1 | tf_op jit(solution)/shard_map/project/pallas_call | solution.py:248
  12.6 6.8 %collective-permute-done.1.refs_1_ = bf16[64,4096]{1,0:T(8,128)(2,1)S(1)} collective-permute-done((bf16[64,4096]{1,0:T(8,128)(2,1)S(1)}, bf16[64,4096]{1,0:T(8,128)(2,1)S(1)}, u32[]{:S(2)}, u32[]{:S(2)}) %collective-permute-start.1) | collective-permute-done | bytes 524320 | tf_op jit(solution)/shard_map/ppermute | solution.py:40
  20.0 3.0 %collective-permute-start.3 = (bf16[64,2048]{1,0:T(8,128)(2,1)S(1)}, bf16[64,2048]{1,0:T(8,128)(2,1)S(1)}, u32[]{:S(2)}, u32[]{:S(2)}) collective-permute-start(bf16[64,2048]{1,0:T(8,128)(2,1)S(1)} %cut.2), channel_id=1, source_target_pairs={{0,2},{1,3},{2,4},{3,5},{4,6},{5,7},{6,0},{7,1},{8,10},{9,11},{10,... | collective-permute-start | bytes 786440 | tf_op jit(solution)/shard_map/ppermute | solution.py:40
  23.4 3.2 %collective-permute-start.12 = (bf16[64,4096]{1,0:T(8,128)(2,1)S(1)}, bf16[64,4096]{1,0:T(8,128)(2,1)S(1)}, u32[]{:S(2)}, u32[]{:S(2)}) collective-permute-start(bf16[64,4096]{1,0:T(8,128)(2,1)S(1)} %gate.9.refs_0_), channel_id=1, source_target_pairs={{0,2},{1,3},{2,4},{3,5},{4,6},{5,7},{6,0},{7,1},{8,10},{9,11},{10,... | collective-permute-start | bytes 1572872 | tf_op jit(solution)/shard_map/ppermute | solution.py:40
  26.6 5.3 %project.6.earlier.refs_3_ = f32[64,2048]{1,0:T(8,128)S(1)} custom-call(s32[1,256]{1,0:T(1,128)S(1)} %copy-done.6, s32[4]{0:T(128)S(1)} %pad_add_fusion.about, bf16[256,256,256]{2,1,0:T(8,128)(2,1)} %bitcast.15, bf16[64,4096]{1,0:T(8,128)(2,1)S(1)} %get-tuple-element.46.source.refs_0_.refs_1_, bf16[64,4096]{1,0:T(8,128)(2,1)S(1)} %collective-permute-done.5.refs_1_, ...), custom_call_target="tpu_custom_call" | custom-call | flops 1 | bytes 1 | tf_op jit(solution)/shard_map/project/pallas_call | solution.py:248
  35.0 4.3 %project.7.refs_1_.refs_2_.refs_5_ = f32[64,2048]{1,0:T(8,128)S(1)} custom-call(s32[1,256]{1,0:T(1,128)S(1)} %copy-done.6, s32[4]{0:T(128)S(1)} %pad_add_fusion.about, bf16[256,256,256]{2,1,0:T(8,128)(2,1)} %bitcast.16, bf16[64,4096]{1,0:T(8,128)(2,1)S(1)} %gate.9.refs_0_, bf16[64,4096]{1,0:T(8,128)(2,1)S(1)} %collective-permute-done.9.refs_1_, ...), custom_call_target="tpu_custom_call" | custom-call | flops 1 | bytes 1 | tf_op jit(solution)/shard_map/project/pallas_call | solution.py:248
  39.3 4.2 %collective-permute-done.13.refs_1_ = bf16[64,4096]{1,0:T(8,128)(2,1)S(1)} collective-permute-done((bf16[64,4096]{1,0:T(8,128)(2,1)S(1)}, bf16[64,4096]{1,0:T(8,128)(2,1)S(1)}, u32[]{:S(2)}, u32[]{:S(2)}) %collective-permute-start.13) | collective-permute-done | bytes 524320 | tf_op jit(solution)/shard_map/ppermute | solution.py:40
  46.2 6.2 %project.8.refs_2_ = f32[64,2048]{1,0:T(8,128)S(1)} custom-call(s32[1,256]{1,0:T(1,128)S(1)} %copy-done.6, s32[4]{0:T(128)S(1)} %pad_add_fusion.about, bf16[256,256,256]{2,1,0:T(8,128)(2,1)} %bitcast.17, bf16[64,4096]{1,0:T(8,128)(2,1)S(1)} %collective-permute-done.11.refs_0_, bf16[64,4096]{1,0:T(8,128)(2,1)S(1)} %get-tuple-element.48.refs_1_, ...), custom_call_target="tpu_custom_call" | custom-call | flops 1 | bytes 1 | tf_op jit(solution)/shard_map/project/pallas_call | solution.py:248
  52.4 3.7 %project.9 = (f32[16,2048]{1,0:T(8,128)S(1)}, f32[16,2048]{1,0:T(8,128)S(1)}, f32[16,2048]{1,0:T(8,128)S(1)}) custom-call(s32[1,256]{1,0:T(1,128)S(1)} %copy-done.6, s32[4]{0:T(128)S(1)} %pad_add_fusion.about, bf16[256,256,256]{2,1,0:T(8,128)(2,1)} %bitcast.18, bf16[64,4096]{1,0:T(8,128)(2,1)S(1)} %gate.10.refs_0_, ...), custom_call_target="tpu_custom_call" | custom-call | flops 1 | bytes 1 | tf_op jit(solution)/shard_map/project/pallas_call | solution.py:248
  56.2 5.7 %collective-permute-start.16 = (f32[16,2048]{1,0:T(8,128)S(1)}, f32[16,2048]{1,0:T(8,128)S(1)}, u32[]{:S(2)}, u32[]{:S(2)}) collective-permute-start(f32[16,2048]{1,0:T(8,128)S(1)} %get-tuple-element.51), channel_id=1, source_target_pairs={{16,32},{32,16},{48,64},{64,48},{80,96},{96,80},{17,33},{33,17},{4... | collective-permute-start | bytes 393224 | tf_op jit(solution)/shard_map/ppermute | solution.py:464
  62.0 5.4 %collective-permute-done.16.b = f32[16,2048]{1,0:T(8,128)S(1)} collective-permute-done((f32[16,2048]{1,0:T(8,128)S(1)}, f32[16,2048]{1,0:T(8,128)S(1)}, u32[]{:S(2)}, u32[]{:S(2)}) %collective-permute-start.16) | collective-permute-done | bytes 131104 | tf_op jit(solution)/shard_map/ppermute | solution.py:464
  68.4 5.4 %collective-permute-start.18 = (bf16[16,2048]{1,0:T(8,128)(2,1)S(1)}, bf16[16,2048]{1,0:T(8,128)(2,1)S(1)}, u32[]{:S(2)}, u32[]{:S(2)}) collective-permute-start(bf16[16,2048]{1,0:T(8,128)(2,1)S(1)} %get-tuple-element.53), channel_id=1, source_target_pairs={{16,32},{32,16},{48,64},{64,48},{80,96},{96,80},{17,33},{33,17},{4... | collective-permute-start | bytes 196616 | tf_op jit(solution)/shard_map/ppermute | solution.py:467
  73.8 4.3 %collective-permute-done.18.refs_1_ = bf16[16,2048]{1,0:T(8,128)(2,1)S(1)} collective-permute-done((bf16[16,2048]{1,0:T(8,128)(2,1)S(1)}, bf16[16,2048]{1,0:T(8,128)(2,1)S(1)}, u32[]{:S(2)}, u32[]{:S(2)}) %collective-permute-start.18) | collective-permute-done | bytes 65568 | tf_op jit(solution)/shard_map/ppermute | solution.py:467
  78.2 4.8 %pull.6 = (bf16[64,4096]{1,0:T(8,128)(2,1)S(1)}, bf16[64,4096]{1,0:T(8,128)(2,1)S(1)}, bf16[64,4096]{1,0:T(8,128)(2,1)S(1)}, bf16[64,2048]{1,0:T(8,128)(2,1)S(1)}) custom-call(s32[1,256]{1,0:T(1,128)S(1)} %copy-done.6, s32[4]{0:T(128)S(1)} %pad_add_fusion.about, bf16[256,256,256]{2,1,0:T(8,128)(2,1)} %bitcast.19, bf16[32,64]{1,0:T(8,128)(2,1)S(1)} %bitcast.13, ...), custom_call_target="tpu_custom_call" | custom-call | flops 1 | bytes 1 | tf_op jit(solution)/shard_map/pull/pallas_call | solution.py:338
  83.6 4.5 %pull.7 = (f32[64,4096]{1,0:T(8,128)S(1)}, f32[64,4096]{1,0:T(8,128)S(1)}, f32[64,4096]{1,0:T(8,128)S(1)}) custom-call(s32[1,256]{1,0:T(1,128)S(1)} %copy-done.6, s32[4]{0:T(128)S(1)} %pad_add_fusion.about, bf16[256,256,256]{2,1,0:T(8,128)(2,1)} %bitcast.20, bf16[64,2048]{1,0:T(8,128)(2,1)S(1)} %get-tuple-element.55.refs_0_, ...), custom_call_target="tpu_custom_call" | custom-call | flops 1 | bytes 1 | tf_op jit(solution)/shard_map/pull/pallas_call | solution.py:338
  90.5 2.2 %collective-permute-start.25 = (bf16[64,4096]{1,0:T(8,128)(2,1)S(1)}, bf16[64,4096]{1,0:T(8,128)(2,1)S(1)}, u32[]{:S(2)}, u32[]{:S(2)}) collective-permute-start(bf16[64,4096]{1,0:T(8,128)(2,1)S(1)} %get-tuple-element.62.refs_1_), channel_id=1, source_target_pairs={{0,8},{1,9},{2,10},{3,11},{4,12},{5,13},{6,14},{7,15},{8,0},{9,1},... | collective-permute-start | bytes 1572872 | tf_op jit(solution)/shard_map/ppermute | solution.py:40
  92.7 3.6 %pull.8 = (bf16[64,4096]{1,0:T(8,128)(2,1)S(1)}, bf16[64,4096]{1,0:T(8,128)(2,1)S(1)}) custom-call(s32[1,256]{1,0:T(1,128)S(1)} %copy-done.6, s32[4]{0:T(128)S(1)} %pad_add_fusion.about, bf16[256,256,256]{2,1,0:T(8,128)(2,1)} %bitcast.21, bf16[64,2048]{1,0:T(8,128)(2,1)S(1)} %get-tuple-element.55.refs_0_, bf16[64,4096]{1,0:T(8,128)(2,1)S(1)} %get-tuple-element.62.refs_1_), custom_call_target="tpu_custom_call" | custom-call | flops 1 | bytes 1 | tf_op jit(solution)/shard_map/pull/pallas_call | solution.py:338
  96.9 3.6 %pull.9 = (f32[64,4096]{1,0:T(8,128)S(1)}, f32[64,4096]{1,0:T(8,128)S(1)}) custom-call(s32[1,256]{1,0:T(1,128)S(1)} %copy-done.6, s32[4]{0:T(128)S(1)} %pad_add_fusion.about, bf16[256,256,256]{2,1,0:T(8,128)(2,1)} %bitcast.22, bf16[64,2048]{1,0:T(8,128)(2,1)S(1)} %get-tuple-element.55.refs_0_, bf16[64,4096]{1,0:T(8,128)(2,1)S(1)} %get-tuple-element.63.refs_1_), custom_call_target="tpu_custom_call" | custom-call | flops 1 | bytes 1 | tf_op jit(solution)/shard_map/pull/pallas_call | solution.py:338
  100.5 4.5 %pull.10 = (bf16[64,4096]{1,0:T(8,128)(2,1)S(1)}, bf16[64,4096]{1,0:T(8,128)(2,1)S(1)}, bf16[64,4096]{1,0:T(8,128)(2,1)S(1)}) custom-call(s32[1,256]{1,0:T(1,128)S(1)} %copy-done.6, s32[4]{0:T(128)S(1)} %pad_add_fusion.about, bf16[256,256,256]{2,1,0:T(8,128)(2,1)} %bitcast.23, bf16[64,2048]{1,0:T(8,128)(2,1)S(1)} %get-tuple-element.55.refs_0_, ...), custom_call_target="tpu_custom_call" | custom-call | flops 1 | bytes 1 | tf_op jit(solution)/shard_map/pull/pallas_call | solution.py:338
  106.3 3.2 %collective-permute-start.31 = (bf16[64,2048]{1,0:T(8,128)(2,1)S(1)}, bf16[64,2048]{1,0:T(8,128)(2,1)S(1)}, u32[]{:S(2)}, u32[]{:S(2)}) collective-permute-start(bf16[64,2048]{1,0:T(8,128)(2,1)S(1)} %get-tuple-element.75.refs_4_), channel_id=1, source_target_pairs={{0,2},{1,3},{2,4},{3,5},{4,6},{5,7},{6,0},{7,1},{8,10},{9,11},{10,... | collective-permute-start | bytes 786440 | tf_op jit(solution)/shard_map/ppermute | solution.py:40
  109.7 4.5 %pull.11 = (f32[64,4096]{1,0:T(8,128)S(1)}, f32[64,4096]{1,0:T(8,128)S(1)}, f32[64,4096]{1,0:T(8,128)S(1)}) custom-call(s32[1,256]{1,0:T(1,128)S(1)} %copy-done.6, s32[4]{0:T(128)S(1)} %pad_add_fusion.about, bf16[256,256,256]{2,1,0:T(8,128)(2,1)} %bitcast.24, bf16[64,2048]{1,0:T(8,128)(2,1)S(1)} %get-tuple-element.55.refs_0_, ...), custom_call_target="tpu_custom_call" | custom-call | flops 1 | bytes 1 | tf_op jit(solution)/shard_map/pull/pallas_call | solution.py:338
  120.1 9.0 %collective-permute-done.33.a = bf16[64,4096]{1,0:T(8,128)(2,1)S(1)} collective-permute-done((bf16[64,4096]{1,0:T(8,128)(2,1)S(1)}, bf16[64,4096]{1,0:T(8,128)(2,1)S(1)}, u32[]{:S(2)}, u32[]{:S(2)}) %collective-permute-start.33) | collective-permute-done | bytes 524320 | tf_op jit(solution)/shard_map/ppermute | solution.py:40
  130.8 2.2 %collective-permute-done.35.c = bf16[64,4096]{1,0:T(8,128)(2,1)S(1)} collective-permute-done((bf16[64,4096]{1,0:T(8,128)(2,1)S(1)}, bf16[64,4096]{1,0:T(8,128)(2,1)S(1)}, u32[]{:S(2)}, u32[]{:S(2)}) %collective-permute-start.35) | collective-permute-done | bytes 524320 | tf_op jit(solution)/shard_map/ppermute | solution.py:40
  (94 shorter events, 27.1 us)
Async XLA Ops:
  3.9 15.6 %collective-permute-start.1 = (bf16[64,4096]{1,0:T(8,128)(2,1)S(1)}, bf16[64,4096]{1,0:T(8,128)(2,1)S(1)}, u32[]{:S(2)}, u32[]{:S(2)}) collective-permute-start(bf16[64,4096]{1,0:T(8,128)(2,1)S(1)} %round_volume.1.refs_0_), channel_id=1, source_target_pairs={{0,6},{1,7},{2,0},{3,1},{4,2},{5,3},{6,4},{7,5},{8,14},{9,15},{10,... | collective-permute-start | bytes 1572872 | tf_op jit(solution)/shard_map/ppermute | solution.py:40
  4.8 14.7 %collective-permute-start = (bf16[64,4096]{1,0:T(8,128)(2,1)S(1)}, bf16[64,4096]{1,0:T(8,128)(2,1)S(1)}, u32[]{:S(2)}, u32[]{:S(2)}) collective-permute-start(bf16[64,4096]{1,0:T(8,128)(2,1)S(1)} %round_volume.1.refs_0_), channel_id=1, source_target_pairs={{0,2},{1,3},{2,4},{3,5},{4,6},{5,7},{6,0},{7,1},{8,10},{9,11},{10,... | collective-permute-start | bytes 1572872 | tf_op jit(solution)/shard_map/ppermute | solution.py:40
  7.2 15.9 %collective-permute-start.8 = (bf16[64,4096]{1,0:T(8,128)(2,1)S(1)}, bf16[64,4096]{1,0:T(8,128)(2,1)S(1)}, u32[]{:S(2)}, u32[]{:S(2)}) collective-permute-start(bf16[64,4096]{1,0:T(8,128)(2,1)S(1)} %round_volume.1.refs_0_), channel_id=1, source_target_pairs={{0,8},{1,9},{2,10},{3,11},{4,12},{5,13},{6,14},{7,15},{8,0},{9,1},... | collective-permute-start | bytes 1572872 | tf_op jit(solution)/shard_map/ppermute | solution.py:40
  20.0 11.9 %collective-permute-start.3 = (bf16[64,2048]{1,0:T(8,128)(2,1)S(1)}, bf16[64,2048]{1,0:T(8,128)(2,1)S(1)}, u32[]{:S(2)}, u32[]{:S(2)}) collective-permute-start(bf16[64,2048]{1,0:T(8,128)(2,1)S(1)} %cut.2), channel_id=1, source_target_pairs={{0,2},{1,3},{2,4},{3,5},{4,6},{5,7},{6,0},{7,1},{8,10},{9,11},{10,... | collective-permute-start | bytes 786440 | tf_op jit(solution)/shard_map/ppermute | solution.py:40
  23.1 10.5 %collective-permute-start.4 = (bf16[64,2048]{1,0:T(8,128)(2,1)S(1)}, bf16[64,2048]{1,0:T(8,128)(2,1)S(1)}, u32[]{:S(2)}, u32[]{:S(2)}) collective-permute-start(bf16[64,2048]{1,0:T(8,128)(2,1)S(1)} %cut.3), channel_id=1, source_target_pairs={{0,6},{1,7},{2,0},{3,1},{4,2},{5,3},{6,4},{7,5},{8,14},{9,15},{10,... | collective-permute-start | bytes 786440 | tf_op jit(solution)/shard_map/ppermute | solution.py:40
  23.2 11.8 %collective-permute-start.9 = (bf16[64,4096]{1,0:T(8,128)(2,1)S(1)}, bf16[64,4096]{1,0:T(8,128)(2,1)S(1)}, u32[]{:S(2)}, u32[]{:S(2)}) collective-permute-start(bf16[64,4096]{1,0:T(8,128)(2,1)S(1)} %gate.9.refs_0_), channel_id=1, source_target_pairs={{0,1},{1,0},{2,3},{3,2},{4,5},{5,4},{6,7},{7,6},{8,9},{9,8},{10,11... | collective-permute-start | bytes 1572872 | tf_op jit(solution)/shard_map/ppermute | solution.py:40
  23.3 20.2 %collective-permute-start.13 = (bf16[64,4096]{1,0:T(8,128)(2,1)S(1)}, bf16[64,4096]{1,0:T(8,128)(2,1)S(1)}, u32[]{:S(2)}, u32[]{:S(2)}) collective-permute-start(bf16[64,4096]{1,0:T(8,128)(2,1)S(1)} %gate.9.refs_0_), channel_id=1, source_target_pairs={{0,6},{1,7},{2,0},{3,1},{4,2},{5,3},{6,4},{7,5},{8,14},{9,15},{10,... | collective-permute-start | bytes 1572872 | tf_op jit(solution)/shard_map/ppermute | solution.py:40
  23.4 20.2 %collective-permute-start.12 = (bf16[64,4096]{1,0:T(8,128)(2,1)S(1)}, bf16[64,4096]{1,0:T(8,128)(2,1)S(1)}, u32[]{:S(2)}, u32[]{:S(2)}) collective-permute-start(bf16[64,4096]{1,0:T(8,128)(2,1)S(1)} %gate.9.refs_0_), channel_id=1, source_target_pairs={{0,2},{1,3},{2,4},{3,5},{4,6},{5,7},{6,0},{7,1},{8,10},{9,11},{10,... | collective-permute-start | bytes 1572872 | tf_op jit(solution)/shard_map/ppermute | solution.py:40
  33.6 12.4 %collective-permute-start.7 = (bf16[64,4096]{1,0:T(8,128)(2,1)S(1)}, bf16[64,4096]{1,0:T(8,128)(2,1)S(1)}, u32[]{:S(2)}, u32[]{:S(2)}) collective-permute-start(bf16[64,4096]{1,0:T(8,128)(2,1)S(1)} %join.1.refs_2_), channel_id=1, source_target_pairs={{0,8},{1,9},{2,10},{3,11},{4,12},{5,13},{6,14},{7,15},{8,0},{9,1},... | collective-permute-start | bytes 1572872 | tf_op jit(solution)/shard_map/ppermute | solution.py:40
  35.0 11.2 %collective-permute-start.11 = (bf16[64,4096]{1,0:T(8,128)(2,1)S(1)}, bf16[64,4096]{1,0:T(8,128)(2,1)S(1)}, u32[]{:S(2)}, u32[]{:S(2)}) collective-permute-start(bf16[64,4096]{1,0:T(8,128)(2,1)S(1)} %join.1.refs_2_), channel_id=1, source_target_pairs={{0,1},{1,0},{2,3},{3,2},{4,5},{5,4},{6,7},{7,6},{8,9},{9,8},{10,11... | collective-permute-start | bytes 1572872 | tf_op jit(solution)/shard_map/ppermute | solution.py:40
  56.2 11.2 %collective-permute-start.16 = (f32[16,2048]{1,0:T(8,128)S(1)}, f32[16,2048]{1,0:T(8,128)S(1)}, u32[]{:S(2)}, u32[]{:S(2)}) collective-permute-start(f32[16,2048]{1,0:T(8,128)S(1)} %get-tuple-element.51), channel_id=1, source_target_pairs={{16,32},{32,16},{48,64},{64,48},{80,96},{96,80},{17,33},{33,17},{4... | collective-permute-start | bytes 393224 | tf_op jit(solution)/shard_map/ppermute | solution.py:464
  68.4 9.8 %collective-permute-start.18 = (bf16[16,2048]{1,0:T(8,128)(2,1)S(1)}, bf16[16,2048]{1,0:T(8,128)(2,1)S(1)}, u32[]{:S(2)}, u32[]{:S(2)}) collective-permute-start(bf16[16,2048]{1,0:T(8,128)(2,1)S(1)} %get-tuple-element.53), channel_id=1, source_target_pairs={{16,32},{32,16},{48,64},{64,48},{80,96},{96,80},{17,33},{33,17},{4... | collective-permute-start | bytes 196616 | tf_op jit(solution)/shard_map/ppermute | solution.py:467
  88.4 16.7 %collective-permute-start.26 = (bf16[64,4096]{1,0:T(8,128)(2,1)S(1)}, bf16[64,4096]{1,0:T(8,128)(2,1)S(1)}, u32[]{:S(2)}, u32[]{:S(2)}) collective-permute-start(bf16[64,4096]{1,0:T(8,128)(2,1)S(1)} %get-tuple-element.66), channel_id=1, source_target_pairs={{0,2},{1,3},{2,4},{3,5},{4,6},{5,7},{6,0},{7,1},{8,10},{9,11},{10,... | collective-permute-start | bytes 1572872 | tf_op jit(solution)/shard_map/ppermute | solution.py:40
  90.2 15.3 %collective-permute-start.27 = (bf16[64,4096]{1,0:T(8,128)(2,1)S(1)}, bf16[64,4096]{1,0:T(8,128)(2,1)S(1)}, u32[]{:S(2)}, u32[]{:S(2)}) collective-permute-start(bf16[64,4096]{1,0:T(8,128)(2,1)S(1)} %get-tuple-element.67), channel_id=1, source_target_pairs={{0,6},{1,7},{2,0},{3,1},{4,2},{5,3},{6,4},{7,5},{8,14},{9,15},{10,... | collective-permute-start | bytes 1572872 | tf_op jit(solution)/shard_map/ppermute | solution.py:40
  90.5 15.2 %collective-permute-start.25 = (bf16[64,4096]{1,0:T(8,128)(2,1)S(1)}, bf16[64,4096]{1,0:T(8,128)(2,1)S(1)}, u32[]{:S(2)}, u32[]{:S(2)}) collective-permute-start(bf16[64,4096]{1,0:T(8,128)(2,1)S(1)} %get-tuple-element.62.refs_1_), channel_id=1, source_target_pairs={{0,8},{1,9},{2,10},{3,11},{4,12},{5,13},{6,14},{7,15},{8,0},{9,1},... | collective-permute-start | bytes 1572872 | tf_op jit(solution)/shard_map/ppermute | solution.py:40
  96.3 9.7 %collective-permute-start.24 = (bf16[64,4096]{1,0:T(8,128)(2,1)S(1)}, bf16[64,4096]{1,0:T(8,128)(2,1)S(1)}, u32[]{:S(2)}, u32[]{:S(2)}) collective-permute-start(bf16[64,4096]{1,0:T(8,128)(2,1)S(1)} %get-tuple-element.65), channel_id=1, source_target_pairs={{0,1},{1,0},{2,3},{3,2},{4,5},{5,4},{6,7},{7,6},{8,9},{9,8},{10,11... | collective-permute-start | bytes 1572872 | tf_op jit(solution)/shard_map/ppermute | solution.py:40
  105.1 12.6 %collective-permute-start.29 = (bf16[64,4096]{1,0:T(8,128)(2,1)S(1)}, bf16[64,4096]{1,0:T(8,128)(2,1)S(1)}, u32[]{:S(2)}, u32[]{:S(2)}) collective-permute-start(bf16[64,4096]{1,0:T(8,128)(2,1)S(1)} %get-tuple-element.77), channel_id=1, source_target_pairs={{0,1},{1,0},{2,3},{3,2},{4,5},{5,4},{6,7},{7,6},{8,9},{9,8},{10,11... | collective-permute-start | bytes 1572872 | tf_op jit(solution)/shard_map/ppermute | solution.py:40
  105.5 12.3 %collective-permute-start.30 = (bf16[64,4096]{1,0:T(8,128)(2,1)S(1)}, bf16[64,4096]{1,0:T(8,128)(2,1)S(1)}, u32[]{:S(2)}, u32[]{:S(2)}) collective-permute-start(bf16[64,4096]{1,0:T(8,128)(2,1)S(1)} %get-tuple-element.78), channel_id=1, source_target_pairs={{0,1},{1,0},{2,3},{3,2},{4,5},{5,4},{6,7},{7,6},{8,9},{9,8},{10,11... | collective-permute-start | bytes 1572872 | tf_op jit(solution)/shard_map/ppermute | solution.py:40
  105.7 12.1 %collective-permute-start.28 = (bf16[64,4096]{1,0:T(8,128)(2,1)S(1)}, bf16[64,4096]{1,0:T(8,128)(2,1)S(1)}, u32[]{:S(2)}, u32[]{:S(2)}) collective-permute-start(bf16[64,4096]{1,0:T(8,128)(2,1)S(1)} %get-tuple-element.69.refs_3_), channel_id=1, source_target_pairs={{0,1},{1,0},{2,3},{3,2},{4,5},{5,4},{6,7},{7,6},{8,9},{9,8},{10,11... | collective-permute-start | bytes 1572872 | tf_op jit(solution)/shard_map/ppermute | solution.py:40
  106.2 9.7 %collective-permute-start.32 = (bf16[64,2048]{1,0:T(8,128)(2,1)S(1)}, bf16[64,2048]{1,0:T(8,128)(2,1)S(1)}, u32[]{:S(2)}, u32[]{:S(2)}) collective-permute-start(bf16[64,2048]{1,0:T(8,128)(2,1)S(1)} %get-tuple-element.79), channel_id=1, source_target_pairs={{0,6},{1,7},{2,0},{3,1},{4,2},{5,3},{6,4},{7,5},{8,14},{9,15},{10,... | collective-permute-start | bytes 786440 | tf_op jit(solution)/shard_map/ppermute | solution.py:40
  106.3 11.5 %collective-permute-start.31 = (bf16[64,2048]{1,0:T(8,128)(2,1)S(1)}, bf16[64,2048]{1,0:T(8,128)(2,1)S(1)}, u32[]{:S(2)}, u32[]{:S(2)}) collective-permute-start(bf16[64,2048]{1,0:T(8,128)(2,1)S(1)} %get-tuple-element.75.refs_4_), channel_id=1, source_target_pairs={{0,2},{1,3},{2,4},{3,5},{4,6},{5,7},{6,0},{7,1},{8,10},{9,11},{10,... | collective-permute-start | bytes 786440 | tf_op jit(solution)/shard_map/ppermute | solution.py:40
  115.9 13.2 %collective-permute-start.33 = (bf16[64,4096]{1,0:T(8,128)(2,1)S(1)}, bf16[64,4096]{1,0:T(8,128)(2,1)S(1)}, u32[]{:S(2)}, u32[]{:S(2)}) collective-permute-start(bf16[64,4096]{1,0:T(8,128)(2,1)S(1)} %combine.6.refs_1_), channel_id=1, source_target_pairs={{0,8},{1,9},{2,10},{3,11},{4,12},{5,13},{6,14},{7,15},{8,0},{9,1},... | collective-permute-start | bytes 1572872 | tf_op jit(solution)/shard_map/ppermute | solution.py:40
  118.0 12.8 %collective-permute-start.34 = (bf16[64,4096]{1,0:T(8,128)(2,1)S(1)}, bf16[64,4096]{1,0:T(8,128)(2,1)S(1)}, u32[]{:S(2)}, u32[]{:S(2)}) collective-permute-start(bf16[64,4096]{1,0:T(8,128)(2,1)S(1)} %get-tuple-element.87), channel_id=1, source_target_pairs={{0,2},{1,3},{2,4},{3,5},{4,6},{5,7},{6,0},{7,1},{8,10},{9,11},{10,... | collective-permute-start | bytes 1572872 | tf_op jit(solution)/shard_map/ppermute | solution.py:40
  119.2 13.8 %collective-permute-start.35 = (bf16[64,4096]{1,0:T(8,128)(2,1)S(1)}, bf16[64,4096]{1,0:T(8,128)(2,1)S(1)}, u32[]{:S(2)}, u32[]{:S(2)}) collective-permute-start(bf16[64,4096]{1,0:T(8,128)(2,1)S(1)} %get-tuple-element.88), channel_id=1, source_target_pairs={{0,6},{1,7},{2,0},{3,1},{4,2},{5,3},{6,4},{7,5},{8,14},{9,15},{10,... | collective-permute-start | bytes 1572872 | tf_op jit(solution)/shard_map/ppermute | solution.py:40
  (20 other events, 205.1 us)

commit v4 on v3

--- a/solution.py
+++ b/solution.py
@@ -180,7 +180,7 @@
     n = len(shards)
     started = total is not None
     last = axial is not None
-    piece = 4
+    piece = 8
     pieces = tiles // piece
 
     def body(blk, about, w, *refs):
@@ -388,10 +388,10 @@
         out[...] = jnp.maximum(vol[...] + weight[...] * summed, 0.0)
 
     planes, pixels = volume.shape
-    block = pl.BlockSpec((planes, pixels // 4), lambda i: (0, i))
-    return pl.pallas_call(
-        body,
-        grid=(4,),
+    block = pl.BlockSpec((planes, pixels // 2), lambda i: (0, i))
+    return pl.pallas_call(
+        body,
+        grid=(2,),
         in_specs=[block] * 7,
         out_specs=block,
         out_shape=jax.ShapeDtypeStruct(volume.shape, F32),
@@ -442,15 +442,20 @@
     far_over = send(far, ACROSS)
     far_swapped = send(far, CORE)
     total = ahead(whose(0, 1) + [(2, 0, False)], [over, send(over, CORE), far], total)
-    middle = total
     left_over, right_over = gate([left_over, right_over], total)
     total = ahead(
-        [(2, 0, True)] + whose(-1, 1) + whose(1, 1),
-        [far_swapped, left_over, send(left_over, CORE), right_over, send(right_over, CORE)],
+        [(2, 0, True), (-1, 1, False), (1, 1, False)],
+        [far_swapped, left_over, right_over],
         total,
     )
-    (far_over,) = gate([far_over], middle)
-    to_first, mine, to_second = ahead(whose(2, 1), [far_over, send(far_over, CORE)], total, ax)
+    left_swapped, right_swapped = send(left_over, CORE), send(right_over, CORE)
+    (far_over,) = gate([far_over], total)
+    to_first, mine, to_second = ahead(
+        [(-1, 1, True), (1, 1, True)] + whose(2, 1),
+        [left_swapped, right_swapped, far_over, send(far_over, CORE)],
+        total,
+        ax,
+    )
 
     count = lax.axis_size("slab")
     first_swap, second_swap = (

time: 136 us -> 133 us (0.978)
  Pallas kernels: 52.8 us -> 49 us
  waiting for transfers between devices: 39.1 us -> 41.5 us
    pallas_call x5, Pallas kernels: 23 us -> 19.6 us  [project(): pl.pallas_call(body, in_specs=specs, out_specs=out_specs, out_shape=out_s...]
    ppermute x32, waiting for transfers between devices: 29.4 us -> 32 us  [send(): return lax.ppermute(array, 'view', pairs)]
  transfers between devices with their start and end apart: 36 -> 36, of which waited for: 11 -> 11; matrix products, arithmetic and copies ran while one was open for 0% -> 0% of each run, Pallas kernels for 30% -> 27%
where the time goes in v4:
time: 133 us
  Pallas kernels  49 us (37%)
  waiting for transfers between devices  41.5 us (31%)
  starting transfers between devices  38 us (29%)
  between operations  2.33 us (2%)
  local copies, waits for them, and re-layouts  1.94 us (1%)
    ppermute x32, waiting for transfers between devices, send(): return lax.ppermute(array, 'view', pairs)  32 us
    ppermute x32, starting transfers between devices, send(): return lax.ppermute(array, 'view', pairs)  26.5 us
    pallas_call x6, Pallas kernels, pull(): pl.pallas_call(body, in_specs=[SM, SM, HBM] + [VM] * len(given) + [ANY] *...  25.5 us
    pallas_call x5, Pallas kernels, project(): pl.pallas_call(body, in_specs=specs, out_specs=out_specs, out_shape=out_s...  19.6 us
    ppermute x1, starting transfers between devices, per_device(): lax.ppermute(to_first, 'slab', first_swap)  5.71 us
    ppermute x1, starting transfers between devices, per_device(): first_rows = lax.ppermute(rounded, 'slab', first_swap)  5.41 us
    ppermute x1, waiting for transfers between devices, per_device(): lax.ppermute(to_first, 'slab', first_swap)  5.21 us
    ppermute x1, waiting for transfers between devices, per_device(): first_rows = lax.ppermute(rounded, 'slab', first_swap)  4.33 us
  transfers between devices with their start and end apart: 36, of which 11 were waited for; matrix products, arithmetic and copies ran while one was open for 0% of the time, Pallas kernels for 27%

profile of v4, /device:TPU:22, one launch (start us, length us, event | category | flops | bytes accessed | tf_op | source)
XLA Modules:
  0.0 132.9 jit_solution(17744822045421189625)
XLA Ops:
  4.8 2.4 %collective-permute-start.1 = (bf16[64,4096]{1,0:T(8,128)(2,1)S(1)}, bf16[64,4096]{1,0:T(8,128)(2,1)S(1)}, u32[]{:S(2)}, u32[]{:S(2)}) collective-permute-start(bf16[64,4096]{1,0:T(8,128)(2,1)S(1)} %round_volume.1.refs_0_), channel_id=1, source_target_pairs={{0,2},{1,3},{2,4},{3,5},{4,6},{5,7},{6,0},{7,1},{8,10},{9,11},{10,... | collective-permute-start | bytes 1572872 | tf_op jit(solution)/shard_map/ppermute | solution.py:40
  9.2 3.1 %project.5.refs_2_.earlier.refs_4_ = f32[64,2048]{1,0:T(8,128)S(1)} custom-call(s32[1,256]{1,0:T(1,128)S(1)} %copy-done.5, s32[4]{0:T(128)S(1)} %pad_add_fusion.about, bf16[256,256,256]{2,1,0:T(8,128)(2,1)} %bitcast.14, bf16[64,4096]{1,0:T(8,128)(2,1)S(1)} %round_volume.1.refs_0_, bf16[64,4096]{1,0:T(8,128)(2,1)S(1)} %collective-permute-done.3.refs_1_), custom_call_target="tpu_custom_call" | custom-call | flops 1 | bytes 1 | tf_op jit(solution)/shard_map/project/pallas_call | solution.py:248
  12.3 7.2 %collective-permute-done.2.refs_1_ = bf16[64,4096]{1,0:T(8,128)(2,1)S(1)} collective-permute-done((bf16[64,4096]{1,0:T(8,128)(2,1)S(1)}, bf16[64,4096]{1,0:T(8,128)(2,1)S(1)}, u32[]{:S(2)}, u32[]{:S(2)}) %collective-permute-start.2) | collective-permute-done | bytes 524320 | tf_op jit(solution)/shard_map/ppermute | solution.py:40
  20.0 3.0 %collective-permute-start.7 = (bf16[64,2048]{1,0:T(8,128)(2,1)S(1)}, bf16[64,2048]{1,0:T(8,128)(2,1)S(1)}, u32[]{:S(2)}, u32[]{:S(2)}) collective-permute-start(bf16[64,2048]{1,0:T(8,128)(2,1)S(1)} %cut.2), channel_id=1, source_target_pairs={{0,2},{1,3},{2,4},{3,5},{4,6},{5,7},{6,0},{7,1},{8,10},{9,11},{10,... | collective-permute-start | bytes 786440 | tf_op jit(solution)/shard_map/ppermute | solution.py:40
  23.4 3.2 %collective-permute-start.4 = (bf16[64,4096]{1,0:T(8,128)(2,1)S(1)}, bf16[64,4096]{1,0:T(8,128)(2,1)S(1)}, u32[]{:S(2)}, u32[]{:S(2)}) collective-permute-start(bf16[64,4096]{1,0:T(8,128)(2,1)S(1)} %gate.9.refs_0_), channel_id=1, source_target_pairs={{0,2},{1,3},{2,4},{3,5},{4,6},{5,7},{6,0},{7,1},{8,10},{9,11},{10,... | collective-permute-start | bytes 1572872 | tf_op jit(solution)/shard_map/ppermute | solution.py:40
  26.6 4.4 %project.6.earlier.refs_3_ = f32[64,2048]{1,0:T(8,128)S(1)} custom-call(s32[1,256]{1,0:T(1,128)S(1)} %copy-done.6, s32[4]{0:T(128)S(1)} %pad_add_fusion.about, bf16[256,256,256]{2,1,0:T(8,128)(2,1)} %bitcast.15, bf16[64,4096]{1,0:T(8,128)(2,1)S(1)} %get-tuple-element.46.refs_1_.source.refs_0_, bf16[64,4096]{1,0:T(8,128)(2,1)S(1)} %collective-permute-done.9.refs_1_, ...), custom_call_target="tpu_custom_call" | custom-call | flops 1 | bytes 1 | tf_op jit(solution)/shard_map/project/pallas_call | solution.py:248
  31.0 2.5 %collective-permute-done.8.b = bf16[64,2048]{1,0:T(8,128)(2,1)S(1)} collective-permute-done((bf16[64,2048]{1,0:T(8,128)(2,1)S(1)}, bf16[64,2048]{1,0:T(8,128)(2,1)S(1)}, u32[]{:S(2)}, u32[]{:S(2)}) %collective-permute-start.8) | collective-permute-done | bytes 262176 | tf_op jit(solution)/shard_map/ppermute | solution.py:40
  35.1 3.7 %project.7.refs_2_.refs_3_ = f32[64,2048]{1,0:T(8,128)S(1)} custom-call(s32[1,256]{1,0:T(1,128)S(1)} %copy-done.6, s32[4]{0:T(128)S(1)} %pad_add_fusion.about, bf16[256,256,256]{2,1,0:T(8,128)(2,1)} %bitcast.16, bf16[64,4096]{1,0:T(8,128)(2,1)S(1)} %gate.9.refs_0_, bf16[64,4096]{1,0:T(8,128)(2,1)S(1)} %collective-permute-done.6.refs_1_, ...), custom_call_target="tpu_custom_call" | custom-call | flops 1 | bytes 1 | tf_op jit(solution)/shard_map/project/pallas_call | solution.py:248
  38.8 4.7 %collective-permute-done.5.refs_1_ = bf16[64,4096]{1,0:T(8,128)(2,1)S(1)} collective-permute-done((bf16[64,4096]{1,0:T(8,128)(2,1)S(1)}, bf16[64,4096]{1,0:T(8,128)(2,1)S(1)}, u32[]{:S(2)}, u32[]{:S(2)}) %collective-permute-start.5) | collective-permute-done | bytes 524320 | tf_op jit(solution)/shard_map/ppermute | solution.py:40
  44.0 3.7 %project.8.refs_1_.refs_4_ = f32[64,2048]{1,0:T(8,128)S(1)} custom-call(s32[1,256]{1,0:T(1,128)S(1)} %copy-done.6, s32[4]{0:T(128)S(1)} %pad_add_fusion.about, bf16[256,256,256]{2,1,0:T(8,128)(2,1)} %bitcast.17, bf16[64,4096]{1,0:T(8,128)(2,1)S(1)} %collective-permute-done.14.refs_0_, bf16[64,4096]{1,0:T(8,128)(2,1)S(1)} %get-tuple-element.48.refs_1_, ...), custom_call_target="tpu_custom_call" | custom-call | flops 1 | bytes 1 | tf_op jit(solution)/shard_map/project/pallas_call | solution.py:248
  50.0 4.7 %project.9 = (f32[16,2048]{1,0:T(8,128)S(1)}, f32[16,2048]{1,0:T(8,128)S(1)}, f32[16,2048]{1,0:T(8,128)S(1)}) custom-call(s32[1,256]{1,0:T(1,128)S(1)} %copy-done.6, s32[4]{0:T(128)S(1)} %pad_add_fusion.about, bf16[256,256,256]{2,1,0:T(8,128)(2,1)} %bitcast.18, bf16[64,4096]{1,0:T(8,128)(2,1)S(1)} %collective-permute-done.11.refs_0_, ...), custom_call_target="tpu_custom_call" | custom-call | flops 1 | bytes 1 | tf_op jit(solution)/shard_map/project/pallas_call | solution.py:248
  54.7 5.7 %collective-permute-start.16 = (f32[16,2048]{1,0:T(8,128)S(1)}, f32[16,2048]{1,0:T(8,128)S(1)}, u32[]{:S(2)}, u32[]{:S(2)}) collective-permute-start(f32[16,2048]{1,0:T(8,128)S(1)} %get-tuple-element.51), channel_id=1, source_target_pairs={{16,32},{32,16},{48,64},{64,48},{80,96},{96,80},{17,33},{33,17},{4... | collective-permute-start | bytes 393224 | tf_op jit(solution)/shard_map/ppermute | solution.py:469
  60.5 5.2 %collective-permute-done.16.b = f32[16,2048]{1,0:T(8,128)S(1)} collective-permute-done((f32[16,2048]{1,0:T(8,128)S(1)}, f32[16,2048]{1,0:T(8,128)S(1)}, u32[]{:S(2)}, u32[]{:S(2)}) %collective-permute-start.16) | collective-permute-done | bytes 131104 | tf_op jit(solution)/shard_map/ppermute | solution.py:469
  66.7 5.4 %collective-permute-start.18 = (bf16[16,2048]{1,0:T(8,128)(2,1)S(1)}, bf16[16,2048]{1,0:T(8,128)(2,1)S(1)}, u32[]{:S(2)}, u32[]{:S(2)}) collective-permute-start(bf16[16,2048]{1,0:T(8,128)(2,1)S(1)} %get-tuple-element.53), channel_id=1, source_target_pairs={{16,32},{32,16},{48,64},{64,48},{80,96},{96,80},{17,33},{33,17},{4... | collective-permute-start | bytes 196616 | tf_op jit(solution)/shard_map/ppermute | solution.py:472
  72.1 4.3 %collective-permute-done.18.refs_1_ = bf16[16,2048]{1,0:T(8,128)(2,1)S(1)} collective-permute-done((bf16[16,2048]{1,0:T(8,128)(2,1)S(1)}, bf16[16,2048]{1,0:T(8,128)(2,1)S(1)}, u32[]{:S(2)}, u32[]{:S(2)}) %collective-permute-start.18) | collective-permute-done | bytes 65568 | tf_op jit(solution)/shard_map/ppermute | solution.py:472
  76.5 4.8 %pull.6 = (bf16[64,4096]{1,0:T(8,128)(2,1)S(1)}, bf16[64,4096]{1,0:T(8,128)(2,1)S(1)}, bf16[64,4096]{1,0:T(8,128)(2,1)S(1)}, bf16[64,2048]{1,0:T(8,128)(2,1)S(1)}) custom-call(s32[1,256]{1,0:T(1,128)S(1)} %copy-done.6, s32[4]{0:T(128)S(1)} %pad_add_fusion.about, bf16[256,256,256]{2,1,0:T(8,128)(2,1)} %bitcast.19, bf16[32,64]{1,0:T(8,128)(2,1)S(1)} %bitcast.13, ...), custom_call_target="tpu_custom_call" | custom-call | flops 1 | bytes 1 | tf_op jit(solution)/shard_map/pull/pallas_call | solution.py:338
  81.9 4.5 %pull.7 = (f32[64,4096]{1,0:T(8,128)S(1)}, f32[64,4096]{1,0:T(8,128)S(1)}, f32[64,4096]{1,0:T(8,128)S(1)}) custom-call(s32[1,256]{1,0:T(1,128)S(1)} %copy-done.6, s32[4]{0:T(128)S(1)} %pad_add_fusion.about, bf16[256,256,256]{2,1,0:T(8,128)(2,1)} %bitcast.20, bf16[64,2048]{1,0:T(8,128)(2,1)S(1)} %get-tuple-element.55.refs_0_, ...), custom_call_target="tpu_custom_call" | custom-call | flops 1 | bytes 1 | tf_op jit(solution)/shard_map/pull/pallas_call | solution.py:338
  91.0 3.6 %pull.8 = (bf16[64,4096]{1,0:T(8,128)(2,1)S(1)}, bf16[64,4096]{1,0:T(8,128)(2,1)S(1)}) custom-call(s32[1,256]{1,0:T(1,128)S(1)} %copy-done.6, s32[4]{0:T(128)S(1)} %pad_add_fusion.about, bf16[256,256,256]{2,1,0:T(8,128)(2,1)} %bitcast.21, bf16[64,2048]{1,0:T(8,128)(2,1)S(1)} %get-tuple-element.55.refs_0_, bf16[64,4096]{1,0:T(8,128)(2,1)S(1)} %get-tuple-element.62.refs_1_), custom_call_target="tpu_custom_call" | custom-call | flops 1 | bytes 1 | tf_op jit(solution)/shard_map/pull/pallas_call | solution.py:338
  95.2 3.6 %pull.9 = (f32[64,4096]{1,0:T(8,128)S(1)}, f32[64,4096]{1,0:T(8,128)S(1)}) custom-call(s32[1,256]{1,0:T(1,128)S(1)} %copy-done.6, s32[4]{0:T(128)S(1)} %pad_add_fusion.about, bf16[256,256,256]{2,1,0:T(8,128)(2,1)} %bitcast.22, bf16[64,2048]{1,0:T(8,128)(2,1)S(1)} %get-tuple-element.55.refs_0_, bf16[64,4096]{1,0:T(8,128)(2,1)S(1)} %get-tuple-element.63.refs_1_), custom_call_target="tpu_custom_call" | custom-call | flops 1 | bytes 1 | tf_op jit(solution)/shard_map/pull/pallas_call | solution.py:338
  98.9 4.5 %pull.10 = (bf16[64,4096]{1,0:T(8,128)(2,1)S(1)}, bf16[64,4096]{1,0:T(8,128)(2,1)S(1)}, bf16[64,4096]{1,0:T(8,128)(2,1)S(1)}) custom-call(s32[1,256]{1,0:T(1,128)S(1)} %copy-done.6, s32[4]{0:T(128)S(1)} %pad_add_fusion.about, bf16[256,256,256]{2,1,0:T(8,128)(2,1)} %bitcast.23, bf16[64,2048]{1,0:T(8,128)(2,1)S(1)} %get-tuple-element.55.refs_0_, ...), custom_call_target="tpu_custom_call" | custom-call | flops 1 | bytes 1 | tf_op jit(solution)/shard_map/pull/pallas_call | solution.py:338
  104.6 3.2 %collective-permute-start.31 = (bf16[64,2048]{1,0:T(8,128)(2,1)S(1)}, bf16[64,2048]{1,0:T(8,128)(2,1)S(1)}, u32[]{:S(2)}, u32[]{:S(2)}) collective-permute-start(bf16[64,2048]{1,0:T(8,128)(2,1)S(1)} %get-tuple-element.75.refs_4_), channel_id=1, source_target_pairs={{0,2},{1,3},{2,4},{3,5},{4,6},{5,7},{6,0},{7,1},{8,10},{9,11},{10,... | collective-permute-start | bytes 786440 | tf_op jit(solution)/shard_map/ppermute | solution.py:40
  108.0 4.5 %pull.11 = (f32[64,4096]{1,0:T(8,128)S(1)}, f32[64,4096]{1,0:T(8,128)S(1)}, f32[64,4096]{1,0:T(8,128)S(1)}) custom-call(s32[1,256]{1,0:T(1,128)S(1)} %copy-done.6, s32[4]{0:T(128)S(1)} %pad_add_fusion.about, bf16[256,256,256]{2,1,0:T(8,128)(2,1)} %bitcast.24, bf16[64,2048]{1,0:T(8,128)(2,1)S(1)} %get-tuple-element.55.refs_0_, ...), custom_call_target="tpu_custom_call" | custom-call | flops 1 | bytes 1 | tf_op jit(solution)/shard_map/pull/pallas_call | solution.py:338
  117.5 9.9 %collective-permute-done.33.a = bf16[64,4096]{1,0:T(8,128)(2,1)S(1)} collective-permute-done((bf16[64,4096]{1,0:T(8,128)(2,1)S(1)}, bf16[64,4096]{1,0:T(8,128)(2,1)S(1)}, u32[]{:S(2)}, u32[]{:S(2)}) %collective-permute-start.33) | collective-permute-done | bytes 524320 | tf_op jit(solution)/shard_map/ppermute | solution.py:40
  128.2 3.2 %collective-permute-done.35.c = bf16[64,4096]{1,0:T(8,128)(2,1)S(1)} collective-permute-done((bf16[64,4096]{1,0:T(8,128)(2,1)S(1)}, bf16[64,4096]{1,0:T(8,128)(2,1)S(1)}, u32[]{:S(2)}, u32[]{:S(2)}) %collective-permute-start.35) | collective-permute-done | bytes 524320 | tf_op jit(solution)/shard_map/ppermute | solution.py:40
  (94 shorter events, 25.4 us)
Async XLA Ops:
  3.9 15.6 %collective-permute-start.2 = (bf16[64,4096]{1,0:T(8,128)(2,1)S(1)}, bf16[64,4096]{1,0:T(8,128)(2,1)S(1)}, u32[]{:S(2)}, u32[]{:S(2)}) collective-permute-start(bf16[64,4096]{1,0:T(8,128)(2,1)S(1)} %round_volume.1.refs_0_), channel_id=1, source_target_pairs={{0,6},{1,7},{2,0},{3,1},{4,2},{5,3},{6,4},{7,5},{8,14},{9,15},{10,... | collective-permute-start | bytes 1572872 | tf_op jit(solution)/shard_map/ppermute | solution.py:40
  4.8 14.7 %collective-permute-start.1 = (bf16[64,4096]{1,0:T(8,128)(2,1)S(1)}, bf16[64,4096]{1,0:T(8,128)(2,1)S(1)}, u32[]{:S(2)}, u32[]{:S(2)}) collective-permute-start(bf16[64,4096]{1,0:T(8,128)(2,1)S(1)} %round_volume.1.refs_0_), channel_id=1, source_target_pairs={{0,2},{1,3},{2,4},{3,5},{4,6},{5,7},{6,0},{7,1},{8,10},{9,11},{10,... | collective-permute-start | bytes 1572872 | tf_op jit(solution)/shard_map/ppermute | solution.py:40
  7.2 15.9 %collective-permute-start = (bf16[64,4096]{1,0:T(8,128)(2,1)S(1)}, bf16[64,4096]{1,0:T(8,128)(2,1)S(1)}, u32[]{:S(2)}, u32[]{:S(2)}) collective-permute-start(bf16[64,4096]{1,0:T(8,128)(2,1)S(1)} %round_volume.1.refs_0_), channel_id=1, source_target_pairs={{0,8},{1,9},{2,10},{3,11},{4,12},{5,13},{6,14},{7,15},{8,0},{9,1},... | collective-permute-start | bytes 1572872 | tf_op jit(solution)/shard_map/ppermute | solution.py:40
  20.0 11.0 %collective-permute-start.7 = (bf16[64,2048]{1,0:T(8,128)(2,1)S(1)}, bf16[64,2048]{1,0:T(8,128)(2,1)S(1)}, u32[]{:S(2)}, u32[]{:S(2)}) collective-permute-start(bf16[64,2048]{1,0:T(8,128)(2,1)S(1)} %cut.2), channel_id=1, source_target_pairs={{0,2},{1,3},{2,4},{3,5},{4,6},{5,7},{6,0},{7,1},{8,10},{9,11},{10,... | collective-permute-start | bytes 786440 | tf_op jit(solution)/shard_map/ppermute | solution.py:40
  23.1 10.5 %collective-permute-start.8 = (bf16[64,2048]{1,0:T(8,128)(2,1)S(1)}, bf16[64,2048]{1,0:T(8,128)(2,1)S(1)}, u32[]{:S(2)}, u32[]{:S(2)}) collective-permute-start(bf16[64,2048]{1,0:T(8,128)(2,1)S(1)} %cut.3), channel_id=1, source_target_pairs={{0,6},{1,7},{2,0},{3,1},{4,2},{5,3},{6,4},{7,5},{8,14},{9,15},{10,... | collective-permute-start | bytes 786440 | tf_op jit(solution)/shard_map/ppermute | solution.py:40
  23.2 11.9 %collective-permute-start.6 = (bf16[64,4096]{1,0:T(8,128)(2,1)S(1)}, bf16[64,4096]{1,0:T(8,128)(2,1)S(1)}, u32[]{:S(2)}, u32[]{:S(2)}) collective-permute-start(bf16[64,4096]{1,0:T(8,128)(2,1)S(1)} %gate.9.refs_0_), channel_id=1, source_target_pairs={{0,1},{1,0},{2,3},{3,2},{4,5},{5,4},{6,7},{7,6},{8,9},{9,8},{10,11... | collective-permute-start | bytes 1572872 | tf_op jit(solution)/shard_map/ppermute | solution.py:40
  23.3 20.2 %collective-permute-start.5 = (bf16[64,4096]{1,0:T(8,128)(2,1)S(1)}, bf16[64,4096]{1,0:T(8,128)(2,1)S(1)}, u32[]{:S(2)}, u32[]{:S(2)}) collective-permute-start(bf16[64,4096]{1,0:T(8,128)(2,1)S(1)} %gate.9.refs_0_), channel_id=1, source_target_pairs={{0,6},{1,7},{2,0},{3,1},{4,2},{5,3},{6,4},{7,5},{8,14},{9,15},{10,... | collective-permute-start | bytes 1572872 | tf_op jit(solution)/shard_map/ppermute | solution.py:40
  23.4 20.2 %collective-permute-start.4 = (bf16[64,4096]{1,0:T(8,128)(2,1)S(1)}, bf16[64,4096]{1,0:T(8,128)(2,1)S(1)}, u32[]{:S(2)}, u32[]{:S(2)}) collective-permute-start(bf16[64,4096]{1,0:T(8,128)(2,1)S(1)} %gate.9.refs_0_), channel_id=1, source_target_pairs={{0,2},{1,3},{2,4},{3,5},{4,6},{5,7},{6,0},{7,1},{8,10},{9,11},{10,... | collective-permute-start | bytes 1572872 | tf_op jit(solution)/shard_map/ppermute | solution.py:40
  33.6 10.4 %collective-permute-start.14 = (bf16[64,4096]{1,0:T(8,128)(2,1)S(1)}, bf16[64,4096]{1,0:T(8,128)(2,1)S(1)}, u32[]{:S(2)}, u32[]{:S(2)}) collective-permute-start(bf16[64,4096]{1,0:T(8,128)(2,1)S(1)} %join.1.refs_2_), channel_id=1, source_target_pairs={{0,1},{1,0},{2,3},{3,2},{4,5},{5,4},{6,7},{7,6},{8,9},{9,8},{10,11... | collective-permute-start | bytes 1572872 | tf_op jit(solution)/shard_map/ppermute | solution.py:40
  33.7 14.3 %collective-permute-start.13 = (bf16[64,4096]{1,0:T(8,128)(2,1)S(1)}, bf16[64,4096]{1,0:T(8,128)(2,1)S(1)}, u32[]{:S(2)}, u32[]{:S(2)}) collective-permute-start(bf16[64,4096]{1,0:T(8,128)(2,1)S(1)} %join.1.refs_2_), channel_id=1, source_target_pairs={{0,8},{1,9},{2,10},{3,11},{4,12},{5,13},{6,14},{7,15},{8,0},{9,1},... | collective-permute-start | bytes 1572872 | tf_op jit(solution)/shard_map/ppermute | solution.py:40
  54.7 11.0 %collective-permute-start.16 = (f32[16,2048]{1,0:T(8,128)S(1)}, f32[16,2048]{1,0:T(8,128)S(1)}, u32[]{:S(2)}, u32[]{:S(2)}) collective-permute-start(f32[16,2048]{1,0:T(8,128)S(1)} %get-tuple-element.51), channel_id=1, source_target_pairs={{16,32},{32,16},{48,64},{64,48},{80,96},{96,80},{17,33},{33,17},{4... | collective-permute-start | bytes 393224 | tf_op jit(solution)/shard_map/ppermute | solution.py:469
  66.7 9.8 %collective-permute-start.18 = (bf16[16,2048]{1,0:T(8,128)(2,1)S(1)}, bf16[16,2048]{1,0:T(8,128)(2,1)S(1)}, u32[]{:S(2)}, u32[]{:S(2)}) collective-permute-start(bf16[16,2048]{1,0:T(8,128)(2,1)S(1)} %get-tuple-element.53), channel_id=1, source_target_pairs={{16,32},{32,16},{48,64},{64,48},{80,96},{96,80},{17,33},{33,17},{4... | collective-permute-start | bytes 196616 | tf_op jit(solution)/shard_map/ppermute | solution.py:472
  86.7 16.7 %collective-permute-start.26 = (bf16[64,4096]{1,0:T(8,128)(2,1)S(1)}, bf16[64,4096]{1,0:T(8,128)(2,1)S(1)}, u32[]{:S(2)}, u32[]{:S(2)}) collective-permute-start(bf16[64,4096]{1,0:T(8,128)(2,1)S(1)} %get-tuple-element.66), channel_id=1, source_target_pairs={{0,2},{1,3},{2,4},{3,5},{4,6},{5,7},{6,0},{7,1},{8,10},{9,11},{10,... | collective-permute-start | bytes 1572872 | tf_op jit(solution)/shard_map/ppermute | solution.py:40
  87.0 16.6 %collective-permute-start.27 = (bf16[64,4096]{1,0:T(8,128)(2,1)S(1)}, bf16[64,4096]{1,0:T(8,128)(2,1)S(1)}, u32[]{:S(2)}, u32[]{:S(2)}) collective-permute-start(bf16[64,4096]{1,0:T(8,128)(2,1)S(1)} %get-tuple-element.67), channel_id=1, source_target_pairs={{0,6},{1,7},{2,0},{3,1},{4,2},{5,3},{6,4},{7,5},{8,14},{9,15},{10,... | collective-permute-start | bytes 1572872 | tf_op jit(solution)/shard_map/ppermute | solution.py:40
  88.8 15.2 %collective-permute-start.25 = (bf16[64,4096]{1,0:T(8,128)(2,1)S(1)}, bf16[64,4096]{1,0:T(8,128)(2,1)S(1)}, u32[]{:S(2)}, u32[]{:S(2)}) collective-permute-start(bf16[64,4096]{1,0:T(8,128)(2,1)S(1)} %get-tuple-element.62.refs_1_), channel_id=1, source_target_pairs={{0,8},{1,9},{2,10},{3,11},{4,12},{5,13},{6,14},{7,15},{8,0},{9,1},... | collective-permute-start | bytes 1572872 | tf_op jit(solution)/shard_map/ppermute | solution.py:40
  94.7 9.7 %collective-permute-start.24 = (bf16[64,4096]{1,0:T(8,128)(2,1)S(1)}, bf16[64,4096]{1,0:T(8,128)(2,1)S(1)}, u32[]{:S(2)}, u32[]{:S(2)}) collective-permute-start(bf16[64,4096]{1,0:T(8,128)(2,1)S(1)} %get-tuple-element.65), channel_id=1, source_target_pairs={{0,1},{1,0},{2,3},{3,2},{4,5},{5,4},{6,7},{7,6},{8,9},{9,8},{10,11... | collective-permute-start | bytes 1572872 | tf_op jit(solution)/shard_map/ppermute | solution.py:40
  103.4 11.5 %collective-permute-start.29 = (bf16[64,4096]{1,0:T(8,128)(2,1)S(1)}, bf16[64,4096]{1,0:T(8,128)(2,1)S(1)}, u32[]{:S(2)}, u32[]{:S(2)}) collective-permute-start(bf16[64,4096]{1,0:T(8,128)(2,1)S(1)} %get-tuple-element.77), channel_id=1, source_target_pairs={{0,1},{1,0},{2,3},{3,2},{4,5},{5,4},{6,7},{7,6},{8,9},{9,8},{10,11... | collective-permute-start | bytes 1572872 | tf_op jit(solution)/shard_map/ppermute | solution.py:40
  103.6 11.3 %collective-permute-start.30 = (bf16[64,4096]{1,0:T(8,128)(2,1)S(1)}, bf16[64,4096]{1,0:T(8,128)(2,1)S(1)}, u32[]{:S(2)}, u32[]{:S(2)}) collective-permute-start(bf16[64,4096]{1,0:T(8,128)(2,1)S(1)} %get-tuple-element.78), channel_id=1, source_target_pairs={{0,1},{1,0},{2,3},{3,2},{4,5},{5,4},{6,7},{7,6},{8,9},{9,8},{10,11... | collective-permute-start | bytes 1572872 | tf_op jit(solution)/shard_map/ppermute | solution.py:40
  104.0 10.9 %collective-permute-start.28 = (bf16[64,4096]{1,0:T(8,128)(2,1)S(1)}, bf16[64,4096]{1,0:T(8,128)(2,1)S(1)}, u32[]{:S(2)}, u32[]{:S(2)}) collective-permute-start(bf16[64,4096]{1,0:T(8,128)(2,1)S(1)} %get-tuple-element.69.refs_3_), channel_id=1, source_target_pairs={{0,1},{1,0},{2,3},{3,2},{4,5},{5,4},{6,7},{7,6},{8,9},{9,8},{10,11... | collective-permute-start | bytes 1572872 | tf_op jit(solution)/shard_map/ppermute | solution.py:40
  104.5 9.7 %collective-permute-start.32 = (bf16[64,2048]{1,0:T(8,128)(2,1)S(1)}, bf16[64,2048]{1,0:T(8,128)(2,1)S(1)}, u32[]{:S(2)}, u32[]{:S(2)}) collective-permute-start(bf16[64,2048]{1,0:T(8,128)(2,1)S(1)} %get-tuple-element.79), channel_id=1, source_target_pairs={{0,6},{1,7},{2,0},{3,1},{4,2},{5,3},{6,4},{7,5},{8,14},{9,15},{10,... | collective-permute-start | bytes 786440 | tf_op jit(solution)/shard_map/ppermute | solution.py:40
  104.6 10.3 %collective-permute-start.31 = (bf16[64,2048]{1,0:T(8,128)(2,1)S(1)}, bf16[64,2048]{1,0:T(8,128)(2,1)S(1)}, u32[]{:S(2)}, u32[]{:S(2)}) collective-permute-start(bf16[64,2048]{1,0:T(8,128)(2,1)S(1)} %get-tuple-element.75.refs_4_), channel_id=1, source_target_pairs={{0,2},{1,3},{2,4},{3,5},{4,6},{5,7},{6,0},{7,1},{8,10},{9,11},{10,... | collective-permute-start | bytes 786440 | tf_op jit(solution)/shard_map/ppermute | solution.py:40
  114.2 13.2 %collective-permute-start.33 = (bf16[64,4096]{1,0:T(8,128)(2,1)S(1)}, bf16[64,4096]{1,0:T(8,128)(2,1)S(1)}, u32[]{:S(2)}, u32[]{:S(2)}) collective-permute-start(bf16[64,4096]{1,0:T(8,128)(2,1)S(1)} %combine.6.refs_1_), channel_id=1, source_target_pairs={{0,8},{1,9},{2,10},{3,11},{4,12},{5,13},{6,14},{7,15},{8,0},{9,1},... | collective-permute-start | bytes 1572872 | tf_op jit(solution)/shard_map/ppermute | solution.py:40
  115.2 13.0 %collective-permute-start.34 = (bf16[64,4096]{1,0:T(8,128)(2,1)S(1)}, bf16[64,4096]{1,0:T(8,128)(2,1)S(1)}, u32[]{:S(2)}, u32[]{:S(2)}) collective-permute-start(bf16[64,4096]{1,0:T(8,128)(2,1)S(1)} %get-tuple-element.87), channel_id=1, source_target_pairs={{0,2},{1,3},{2,4},{3,5},{4,6},{5,7},{6,0},{7,1},{8,10},{9,11},{10,... | collective-permute-start | bytes 1572872 | tf_op jit(solution)/shard_map/ppermute | solution.py:40
  117.5 13.8 %collective-permute-start.35 = (bf16[64,4096]{1,0:T(8,128)(2,1)S(1)}, bf16[64,4096]{1,0:T(8,128)(2,1)S(1)}, u32[]{:S(2)}, u32[]{:S(2)}) collective-permute-start(bf16[64,4096]{1,0:T(8,128)(2,1)S(1)} %get-tuple-element.88), channel_id=1, source_target_pairs={{0,6},{1,7},{2,0},{3,1},{4,2},{5,3},{6,4},{7,5},{8,14},{9,15},{10,... | collective-permute-start | bytes 1572872 | tf_op jit(solution)/shard_map/ppermute | solution.py:40
  (20 other events, 203.7 us)

commit v5 on v4

--- a/solution.py
+++ b/solution.py
@@ -180,8 +180,11 @@
     n = len(shards)
     started = total is not None
     last = axial is not None
-    piece = 8
-    pieces = tiles // piece
+    pieces = [
+        (p, start, size)
+        for p in range(n)
+        for start, size in (((0, 4), (4, 4), (8, 8)) if p == 0 else ((0, 8), (8, 8)))
+    ]
 
     def body(blk, about, w, *refs):
         refs = list(refs)
@@ -193,23 +196,21 @@
         origins = [base_of(about, *places[p], tiles) for p in range(n)]
         copies = [
             pltpu.make_async_copy(
-                w.at[pl.ds(origins[p] + q * piece, piece)],
-                slots.at[pl.ds(p * tiles + q * piece, piece)],
-                sems.at[p * pieces + q],
+                w.at[pl.ds(origins[p] + start, size)],
+                slots.at[pl.ds(p * tiles + start, size)],
+                sems.at[k],
             )
-            for p in range(n)
-            for q in range(pieces)
+            for k, (p, start, size) in enumerate(pieces)
         ]
         for copy in copies:
             copy.start()
         acc[...] = before[...] if started else jnp.zeros(acc.shape, F32)
-        for p in range(n):
-            for q in range(pieces):
-                copies[p * pieces + q].wait()
-                for i in range(q * piece, (q + 1) * piece):
-                    at = pl.multiple_of(blk[0, origins[p] + i] * columns, columns)
-                    row = parts[p][:, i * width : (i + 1) * width]
-                    acc[:, pl.ds(at, columns)] += dot(row, slots[p * tiles + i])
+        for copy, (p, start, size) in zip(copies, pieces):
+            copy.wait()
+            for i in range(start, start + size):
+                at = pl.multiple_of(blk[0, origins[p] + i] * columns, columns)
+                row = parts[p][:, i * width : (i + 1) * width]
+                acc[:, pl.ds(at, columns)] += dot(row, slots[p * tiles + i])
         if last:
             placed = placing(about, ax).astype(BF16)
             high, low = split(acc[...])
@@ -234,7 +235,7 @@
         specs.append(VM)
     scratch = [
         pltpu.VMEM((n * tiles, width, columns), BF16),
-        pltpu.SemaphoreType.DMA((n * pieces,)),
+        pltpu.SemaphoreType.DMA((len(pieces),)),
     ]
     if last:
         args.append(axial)
@@ -295,8 +296,11 @@
     tiles = weights.shape[0] // (4 * NX)
     pixels = tiles * width
     n = len(places)
-    piece = 8
-    pieces = tiles // piece
+    pieces = [
+        (p, start, size)
+        for p in range(n)
+        for start, size in (((0, 4), (4, 4), (8, 8)) if p == 0 else ((0, 8), (8, 8)))
+    ]
 
     def body(blk, about, w, *refs):
         args = refs[: len(given)]
@@ -305,12 +309,11 @@
         origins = [base_of(about, *places[p], tiles) for p in range(n)]
         copies = [
             pltpu.make_async_copy(
-                w.at[pl.ds(origins[p] + q * piece, piece)],
-                slots.at[pl.ds(p * tiles + q * piece, piece)],
-                sems.at[p * pieces + q],
+                w.at[pl.ds(origins[p] + start, size)],
+                slots.at[pl.ds(p * tiles + start, size)],
+                sems.at[k],
             )
-            for p in range(n)
-            for q in range(pieces)
+            for k, (p, start, size) in enumerate(pieces)
         ]
         for copy in copies:
             copy.start()
@@ -319,18 +322,17 @@
             smear(about, args[0], args[1:], sm)
         else:
             sm = args[0]
-        for p in range(n):
-            for q in range(pieces):
-                copies[p * pieces + q].wait()
-                for i in range(q * piece, (q + 1) * piece):
-                    at = pl.multiple_of(blk[0, origins[p] + i] * columns, columns)
-                    value = lax.dot_general(
-                        sm[:, pl.ds(at, columns)],
-                        slots[p * tiles + i],
-                        NT,
-                        preferred_element_type=F32,
-                    )
-                    outs[p][:, i * width : (i + 1) * width] = value.astype(out_dtype)
+        for copy, (p, start, size) in zip(copies, pieces):
+            copy.wait()
+            for i in range(start, start + size):
+                at = pl.multiple_of(blk[0, origins[p] + i] * columns, columns)
+                value = lax.dot_general(
+                    sm[:, pl.ds(at, columns)],
+                    slots[p * tiles + i],
+                    NT,
+                    preferred_element_type=F32,
+                )
+                outs[p][:, i * width : (i + 1) * width] = value.astype(out_dtype)
 
     out_shape = [jax.ShapeDtypeStruct((planes, pixels), out_dtype)] * n
     if own:
@@ -342,7 +344,7 @@
         out_shape=out_shape,
         scratch_shapes=[
             pltpu.VMEM((n * tiles, width, columns), BF16),
-            pltpu.SemaphoreType.DMA((n * pieces,)),
+            pltpu.SemaphoreType.DMA((len(pieces),)),
         ],
         compiler_params=params(24),
         cost_estimate=cheap(),
@@ -504,7 +506,7 @@
     mine = back(owns(*offsets), smeared, after=[part])
     offsets = [(1, 0), (-1, 0), (0, 0)]
     part, last_swaps = swap_parts(offsets, [mine[0]])
-    from_over, from_left, from_right = gate([from_over, from_left, from_right], part)
+    from_left, from_right, from_over = gate([from_left, from_right, from_over], part)
     swaps = gate(swaps, from_over)
     half_up, half_down = combine([[whole(mine[0]), whole(swaps[0]), whole(from_over)]], pixels, 2)
     half_left = send(half_up, UP)

time: 133 us -> 133 us (level)
  no operation moved by 1% of the time
where the time goes in v5:
time: 133 us
  Pallas kernels  48.8 us (37%)
  waiting for transfers between devices  41.5 us (31%)
  starting transfers between devices  38.1 us (29%)
  between operations  2.33 us (2%)
  local copies, waits for them, and re-layouts  1.94 us (1%)
    ppermute x32, waiting for transfers between devices, send(): return lax.ppermute(array, 'view', pairs)  31.9 us
    ppermute x32, starting transfers between devices, send(): return lax.ppermute(array, 'view', pairs)  26.5 us
    pallas_call x6, Pallas kernels, pull(): pl.pallas_call(body, in_specs=[SM, SM, HBM] + [VM] * len(given) + [ANY] *...  25.3 us
    pallas_call x5, Pallas kernels, project(): pl.pallas_call(body, in_specs=specs, out_specs=out_specs, out_shape=out_s...  19.7 us
    ppermute x1, starting transfers between devices, per_device(): lax.ppermute(to_first, 'slab', first_swap)  5.7 us
    ppermute x1, starting transfers between devices, per_device(): first_rows = lax.ppermute(rounded, 'slab', first_swap)  5.41 us
    ppermute x1, waiting for transfers between devices, per_device(): lax.ppermute(to_first, 'slab', first_swap)  5.22 us
    ppermute x1, waiting for transfers between devices, per_device(): first_rows = lax.ppermute(rounded, 'slab', first_swap)  4.33 us
  transfers between devices with their start and end apart: 36, of which 11 were waited for; matrix products, arithmetic and copies ran while one was open for 0% of the time, Pallas kernels for 27%

profile of v5, /device:TPU:22, one launch (start us, length us, event | category | flops | bytes accessed | tf_op | source)
XLA Modules:
  0.0 132.7 jit_solution(5372779309423087777)
XLA Ops:
  4.8 2.4 %collective-permute-start.1 = (bf16[64,4096]{1,0:T(8,128)(2,1)S(1)}, bf16[64,4096]{1,0:T(8,128)(2,1)S(1)}, u32[]{:S(2)}, u32[]{:S(2)}) collective-permute-start(bf16[64,4096]{1,0:T(8,128)(2,1)S(1)} %round_volume.1.refs_0_), channel_id=1, source_target_pairs={{0,2},{1,3},{2,4},{3,5},{4,6},{5,7},{6,0},{7,1},{8,10},{9,11},{10,... | collective-permute-start | bytes 1572872 | tf_op jit(solution)/shard_map/ppermute | solution.py:40
  9.2 3.1 %project.5.refs_2_.earlier.refs_4_ = f32[64,2048]{1,0:T(8,128)S(1)} custom-call(s32[1,256]{1,0:T(1,128)S(1)} %copy-done.5, s32[4]{0:T(128)S(1)} %pad_add_fusion.about, bf16[256,256,256]{2,1,0:T(8,128)(2,1)} %bitcast.14, bf16[64,4096]{1,0:T(8,128)(2,1)S(1)} %round_volume.1.refs_0_, bf16[64,4096]{1,0:T(8,128)(2,1)S(1)} %collective-permute-done.3.refs_1_), custom_call_target="tpu_custom_call" | custom-call | flops 1 | bytes 1 | tf_op jit(solution)/shard_map/project/pallas_call | solution.py:249
  12.3 7.2 %collective-permute-done.2.refs_1_ = bf16[64,4096]{1,0:T(8,128)(2,1)S(1)} collective-permute-done((bf16[64,4096]{1,0:T(8,128)(2,1)S(1)}, bf16[64,4096]{1,0:T(8,128)(2,1)S(1)}, u32[]{:S(2)}, u32[]{:S(2)}) %collective-permute-start.2) | collective-permute-done | bytes 524320 | tf_op jit(solution)/shard_map/ppermute | solution.py:40
  20.0 3.0 %collective-permute-start.7 = (bf16[64,2048]{1,0:T(8,128)(2,1)S(1)}, bf16[64,2048]{1,0:T(8,128)(2,1)S(1)}, u32[]{:S(2)}, u32[]{:S(2)}) collective-permute-start(bf16[64,2048]{1,0:T(8,128)(2,1)S(1)} %cut.2), channel_id=1, source_target_pairs={{0,2},{1,3},{2,4},{3,5},{4,6},{5,7},{6,0},{7,1},{8,10},{9,11},{10,... | collective-permute-start | bytes 786440 | tf_op jit(solution)/shard_map/ppermute | solution.py:40
  23.4 3.2 %collective-permute-start.4 = (bf16[64,4096]{1,0:T(8,128)(2,1)S(1)}, bf16[64,4096]{1,0:T(8,128)(2,1)S(1)}, u32[]{:S(2)}, u32[]{:S(2)}) collective-permute-start(bf16[64,4096]{1,0:T(8,128)(2,1)S(1)} %gate.9.refs_0_), channel_id=1, source_target_pairs={{0,2},{1,3},{2,4},{3,5},{4,6},{5,7},{6,0},{7,1},{8,10},{9,11},{10,... | collective-permute-start | bytes 1572872 | tf_op jit(solution)/shard_map/ppermute | solution.py:40
  26.6 4.4 %project.6.earlier.refs_3_ = f32[64,2048]{1,0:T(8,128)S(1)} custom-call(s32[1,256]{1,0:T(1,128)S(1)} %copy-done.6, s32[4]{0:T(128)S(1)} %pad_add_fusion.about, bf16[256,256,256]{2,1,0:T(8,128)(2,1)} %bitcast.15, bf16[64,4096]{1,0:T(8,128)(2,1)S(1)} %get-tuple-element.46.refs_1_.source.refs_0_, bf16[64,4096]{1,0:T(8,128)(2,1)S(1)} %collective-permute-done.9.refs_1_, ...), custom_call_target="tpu_custom_call" | custom-call | flops 1 | bytes 1 | tf_op jit(solution)/shard_map/project/pallas_call | solution.py:249
  31.0 2.5 %collective-permute-done.8.b = bf16[64,2048]{1,0:T(8,128)(2,1)S(1)} collective-permute-done((bf16[64,2048]{1,0:T(8,128)(2,1)S(1)}, bf16[64,2048]{1,0:T(8,128)(2,1)S(1)}, u32[]{:S(2)}, u32[]{:S(2)}) %collective-permute-start.8) | collective-permute-done | bytes 262176 | tf_op jit(solution)/shard_map/ppermute | solution.py:40
  35.1 3.8 %project.7.refs_2_.refs_3_ = f32[64,2048]{1,0:T(8,128)S(1)} custom-call(s32[1,256]{1,0:T(1,128)S(1)} %copy-done.6, s32[4]{0:T(128)S(1)} %pad_add_fusion.about, bf16[256,256,256]{2,1,0:T(8,128)(2,1)} %bitcast.16, bf16[64,4096]{1,0:T(8,128)(2,1)S(1)} %gate.9.refs_0_, bf16[64,4096]{1,0:T(8,128)(2,1)S(1)} %collective-permute-done.6.refs_1_, ...), custom_call_target="tpu_custom_call" | custom-call | flops 1 | bytes 1 | tf_op jit(solution)/shard_map/project/pallas_call | solution.py:249
  38.8 4.7 %collective-permute-done.5.refs_1_ = bf16[64,4096]{1,0:T(8,128)(2,1)S(1)} collective-permute-done((bf16[64,4096]{1,0:T(8,128)(2,1)S(1)}, bf16[64,4096]{1,0:T(8,128)(2,1)S(1)}, u32[]{:S(2)}, u32[]{:S(2)}) %collective-permute-start.5) | collective-permute-done | bytes 524320 | tf_op jit(solution)/shard_map/ppermute | solution.py:40
  44.0 3.8 %project.8.refs_1_.refs_4_ = f32[64,2048]{1,0:T(8,128)S(1)} custom-call(s32[1,256]{1,0:T(1,128)S(1)} %copy-done.6, s32[4]{0:T(128)S(1)} %pad_add_fusion.about, bf16[256,256,256]{2,1,0:T(8,128)(2,1)} %bitcast.17, bf16[64,4096]{1,0:T(8,128)(2,1)S(1)} %collective-permute-done.14.refs_0_, bf16[64,4096]{1,0:T(8,128)(2,1)S(1)} %get-tuple-element.48.refs_1_, ...), custom_call_target="tpu_custom_call" | custom-call | flops 1 | bytes 1 | tf_op jit(solution)/shard_map/project/pallas_call | solution.py:249
  50.0 4.7 %project.9 = (f32[16,2048]{1,0:T(8,128)S(1)}, f32[16,2048]{1,0:T(8,128)S(1)}, f32[16,2048]{1,0:T(8,128)S(1)}) custom-call(s32[1,256]{1,0:T(1,128)S(1)} %copy-done.6, s32[4]{0:T(128)S(1)} %pad_add_fusion.about, bf16[256,256,256]{2,1,0:T(8,128)(2,1)} %bitcast.18, bf16[64,4096]{1,0:T(8,128)(2,1)S(1)} %collective-permute-done.11.refs_0_, ...), custom_call_target="tpu_custom_call" | custom-call | flops 1 | bytes 1 | tf_op jit(solution)/shard_map/project/pallas_call | solution.py:249
  54.7 5.7 %collective-permute-start.16 = (f32[16,2048]{1,0:T(8,128)S(1)}, f32[16,2048]{1,0:T(8,128)S(1)}, u32[]{:S(2)}, u32[]{:S(2)}) collective-permute-start(f32[16,2048]{1,0:T(8,128)S(1)} %get-tuple-element.51), channel_id=1, source_target_pairs={{16,32},{32,16},{48,64},{64,48},{80,96},{96,80},{17,33},{33,17},{4... | collective-permute-start | bytes 393224 | tf_op jit(solution)/shard_map/ppermute | solution.py:471
  60.5 5.2 %collective-permute-done.16.b = f32[16,2048]{1,0:T(8,128)S(1)} collective-permute-done((f32[16,2048]{1,0:T(8,128)S(1)}, f32[16,2048]{1,0:T(8,128)S(1)}, u32[]{:S(2)}, u32[]{:S(2)}) %collective-permute-start.16) | collective-permute-done | bytes 131104 | tf_op jit(solution)/shard_map/ppermute | solution.py:471
  66.7 5.4 %collective-permute-start.18 = (bf16[16,2048]{1,0:T(8,128)(2,1)S(1)}, bf16[16,2048]{1,0:T(8,128)(2,1)S(1)}, u32[]{:S(2)}, u32[]{:S(2)}) collective-permute-start(bf16[16,2048]{1,0:T(8,128)(2,1)S(1)} %get-tuple-element.53), channel_id=1, source_target_pairs={{16,32},{32,16},{48,64},{64,48},{80,96},{96,80},{17,33},{33,17},{4... | collective-permute-start | bytes 196616 | tf_op jit(solution)/shard_map/ppermute | solution.py:474
  72.2 4.3 %collective-permute-done.18.refs_1_ = bf16[16,2048]{1,0:T(8,128)(2,1)S(1)} collective-permute-done((bf16[16,2048]{1,0:T(8,128)(2,1)S(1)}, bf16[16,2048]{1,0:T(8,128)(2,1)S(1)}, u32[]{:S(2)}, u32[]{:S(2)}) %collective-permute-start.18) | collective-permute-done | bytes 65568 | tf_op jit(solution)/shard_map/ppermute | solution.py:474
  76.5 4.7 %pull.6 = (bf16[64,4096]{1,0:T(8,128)(2,1)S(1)}, bf16[64,4096]{1,0:T(8,128)(2,1)S(1)}, bf16[64,4096]{1,0:T(8,128)(2,1)S(1)}, bf16[64,2048]{1,0:T(8,128)(2,1)S(1)}) custom-call(s32[1,256]{1,0:T(1,128)S(1)} %copy-done.6, s32[4]{0:T(128)S(1)} %pad_add_fusion.about, bf16[256,256,256]{2,1,0:T(8,128)(2,1)} %bitcast.19, bf16[32,64]{1,0:T(8,128)(2,1)S(1)} %bitcast.13, ...), custom_call_target="tpu_custom_call" | custom-call | flops 1 | bytes 1 | tf_op jit(solution)/shard_map/pull/pallas_call | solution.py:340
  81.9 4.5 %pull.7 = (f32[64,4096]{1,0:T(8,128)S(1)}, f32[64,4096]{1,0:T(8,128)S(1)}, f32[64,4096]{1,0:T(8,128)S(1)}) custom-call(s32[1,256]{1,0:T(1,128)S(1)} %copy-done.6, s32[4]{0:T(128)S(1)} %pad_add_fusion.about, bf16[256,256,256]{2,1,0:T(8,128)(2,1)} %bitcast.20, bf16[64,2048]{1,0:T(8,128)(2,1)S(1)} %get-tuple-element.55.refs_0_, ...), custom_call_target="tpu_custom_call" | custom-call | flops 1 | bytes 1 | tf_op jit(solution)/shard_map/pull/pallas_call | solution.py:340
  91.0 3.6 %pull.8 = (bf16[64,4096]{1,0:T(8,128)(2,1)S(1)}, bf16[64,4096]{1,0:T(8,128)(2,1)S(1)}) custom-call(s32[1,256]{1,0:T(1,128)S(1)} %copy-done.6, s32[4]{0:T(128)S(1)} %pad_add_fusion.about, bf16[256,256,256]{2,1,0:T(8,128)(2,1)} %bitcast.21, bf16[64,2048]{1,0:T(8,128)(2,1)S(1)} %get-tuple-element.55.refs_0_, bf16[64,4096]{1,0:T(8,128)(2,1)S(1)} %get-tuple-element.62.refs_1_), custom_call_target="tpu_custom_call" | custom-call | flops 1 | bytes 1 | tf_op jit(solution)/shard_map/pull/pallas_call | solution.py:340
  95.1 3.6 %pull.9 = (f32[64,4096]{1,0:T(8,128)S(1)}, f32[64,4096]{1,0:T(8,128)S(1)}) custom-call(s32[1,256]{1,0:T(1,128)S(1)} %copy-done.6, s32[4]{0:T(128)S(1)} %pad_add_fusion.about, bf16[256,256,256]{2,1,0:T(8,128)(2,1)} %bitcast.22, bf16[64,2048]{1,0:T(8,128)(2,1)S(1)} %get-tuple-element.55.refs_0_, bf16[64,4096]{1,0:T(8,128)(2,1)S(1)} %get-tuple-element.63.refs_1_), custom_call_target="tpu_custom_call" | custom-call | flops 1 | bytes 1 | tf_op jit(solution)/shard_map/pull/pallas_call | solution.py:340
  98.7 4.5 %pull.10 = (bf16[64,4096]{1,0:T(8,128)(2,1)S(1)}, bf16[64,4096]{1,0:T(8,128)(2,1)S(1)}, bf16[64,4096]{1,0:T(8,128)(2,1)S(1)}) custom-call(s32[1,256]{1,0:T(1,128)S(1)} %copy-done.6, s32[4]{0:T(128)S(1)} %pad_add_fusion.about, bf16[256,256,256]{2,1,0:T(8,128)(2,1)} %bitcast.23, bf16[64,2048]{1,0:T(8,128)(2,1)S(1)} %get-tuple-element.55.refs_0_, ...), custom_call_target="tpu_custom_call" | custom-call | flops 1 | bytes 1 | tf_op jit(solution)/shard_map/pull/pallas_call | solution.py:340
  104.4 3.2 %collective-permute-start.31 = (bf16[64,2048]{1,0:T(8,128)(2,1)S(1)}, bf16[64,2048]{1,0:T(8,128)(2,1)S(1)}, u32[]{:S(2)}, u32[]{:S(2)}) collective-permute-start(bf16[64,2048]{1,0:T(8,128)(2,1)S(1)} %get-tuple-element.75.refs_4_), channel_id=1, source_target_pairs={{0,2},{1,3},{2,4},{3,5},{4,6},{5,7},{6,0},{7,1},{8,10},{9,11},{10,... | collective-permute-start | bytes 786440 | tf_op jit(solution)/shard_map/ppermute | solution.py:40
  107.9 4.5 %pull.11 = (f32[64,4096]{1,0:T(8,128)S(1)}, f32[64,4096]{1,0:T(8,128)S(1)}, f32[64,4096]{1,0:T(8,128)S(1)}) custom-call(s32[1,256]{1,0:T(1,128)S(1)} %copy-done.6, s32[4]{0:T(128)S(1)} %pad_add_fusion.about, bf16[256,256,256]{2,1,0:T(8,128)(2,1)} %bitcast.24, bf16[64,2048]{1,0:T(8,128)(2,1)S(1)} %get-tuple-element.55.refs_0_, ...), custom_call_target="tpu_custom_call" | custom-call | flops 1 | bytes 1 | tf_op jit(solution)/shard_map/pull/pallas_call | solution.py:340
  117.3 9.9 %collective-permute-done.33.a = bf16[64,4096]{1,0:T(8,128)(2,1)S(1)} collective-permute-done((bf16[64,4096]{1,0:T(8,128)(2,1)S(1)}, bf16[64,4096]{1,0:T(8,128)(2,1)S(1)}, u32[]{:S(2)}, u32[]{:S(2)}) %collective-permute-start.33) | collective-permute-done | bytes 524320 | tf_op jit(solution)/shard_map/ppermute | solution.py:40
  128.1 3.0 %collective-permute-done.35.c = bf16[64,4096]{1,0:T(8,128)(2,1)S(1)} collective-permute-done((bf16[64,4096]{1,0:T(8,128)(2,1)S(1)}, bf16[64,4096]{1,0:T(8,128)(2,1)S(1)}, u32[]{:S(2)}, u32[]{:S(2)}) %collective-permute-start.35) | collective-permute-done | bytes 524320 | tf_op jit(solution)/shard_map/ppermute | solution.py:40
  (94 shorter events, 25.6 us)
Async XLA Ops:
  3.9 15.6 %collective-permute-start.2 = (bf16[64,4096]{1,0:T(8,128)(2,1)S(1)}, bf16[64,4096]{1,0:T(8,128)(2,1)S(1)}, u32[]{:S(2)}, u32[]{:S(2)}) collective-permute-start(bf16[64,4096]{1,0:T(8,128)(2,1)S(1)} %round_volume.1.refs_0_), channel_id=1, source_target_pairs={{0,6},{1,7},{2,0},{3,1},{4,2},{5,3},{6,4},{7,5},{8,14},{9,15},{10,... | collective-permute-start | bytes 1572872 | tf_op jit(solution)/shard_map/ppermute | solution.py:40
  4.8 14.7 %collective-permute-start.1 = (bf16[64,4096]{1,0:T(8,128)(2,1)S(1)}, bf16[64,4096]{1,0:T(8,128)(2,1)S(1)}, u32[]{:S(2)}, u32[]{:S(2)}) collective-permute-start(bf16[64,4096]{1,0:T(8,128)(2,1)S(1)} %round_volume.1.refs_0_), channel_id=1, source_target_pairs={{0,2},{1,3},{2,4},{3,5},{4,6},{5,7},{6,0},{7,1},{8,10},{9,11},{10,... | collective-permute-start | bytes 1572872 | tf_op jit(solution)/shard_map/ppermute | solution.py:40
  7.2 15.9 %collective-permute-start = (bf16[64,4096]{1,0:T(8,128)(2,1)S(1)}, bf16[64,4096]{1,0:T(8,128)(2,1)S(1)}, u32[]{:S(2)}, u32[]{:S(2)}) collective-permute-start(bf16[64,4096]{1,0:T(8,128)(2,1)S(1)} %round_volume.1.refs_0_), channel_id=1, source_target_pairs={{0,8},{1,9},{2,10},{3,11},{4,12},{5,13},{6,14},{7,15},{8,0},{9,1},... | collective-permute-start | bytes 1572872 | tf_op jit(solution)/shard_map/ppermute | solution.py:40
  20.0 11.0 %collective-permute-start.7 = (bf16[64,2048]{1,0:T(8,128)(2,1)S(1)}, bf16[64,2048]{1,0:T(8,128)(2,1)S(1)}, u32[]{:S(2)}, u32[]{:S(2)}) collective-permute-start(bf16[64,2048]{1,0:T(8,128)(2,1)S(1)} %cut.2), channel_id=1, source_target_pairs={{0,2},{1,3},{2,4},{3,5},{4,6},{5,7},{6,0},{7,1},{8,10},{9,11},{10,... | collective-permute-start | bytes 786440 | tf_op jit(solution)/shard_map/ppermute | solution.py:40
  23.1 10.5 %collective-permute-start.8 = (bf16[64,2048]{1,0:T(8,128)(2,1)S(1)}, bf16[64,2048]{1,0:T(8,128)(2,1)S(1)}, u32[]{:S(2)}, u32[]{:S(2)}) collective-permute-start(bf16[64,2048]{1,0:T(8,128)(2,1)S(1)} %cut.3), channel_id=1, source_target_pairs={{0,6},{1,7},{2,0},{3,1},{4,2},{5,3},{6,4},{7,5},{8,14},{9,15},{10,... | collective-permute-start | bytes 786440 | tf_op jit(solution)/shard_map/ppermute | solution.py:40
  23.2 11.9 %collective-permute-start.6 = (bf16[64,4096]{1,0:T(8,128)(2,1)S(1)}, bf16[64,4096]{1,0:T(8,128)(2,1)S(1)}, u32[]{:S(2)}, u32[]{:S(2)}) collective-permute-start(bf16[64,4096]{1,0:T(8,128)(2,1)S(1)} %gate.9.refs_0_), channel_id=1, source_target_pairs={{0,1},{1,0},{2,3},{3,2},{4,5},{5,4},{6,7},{7,6},{8,9},{9,8},{10,11... | collective-permute-start | bytes 1572872 | tf_op jit(solution)/shard_map/ppermute | solution.py:40
  23.3 20.2 %collective-permute-start.5 = (bf16[64,4096]{1,0:T(8,128)(2,1)S(1)}, bf16[64,4096]{1,0:T(8,128)(2,1)S(1)}, u32[]{:S(2)}, u32[]{:S(2)}) collective-permute-start(bf16[64,4096]{1,0:T(8,128)(2,1)S(1)} %gate.9.refs_0_), channel_id=1, source_target_pairs={{0,6},{1,7},{2,0},{3,1},{4,2},{5,3},{6,4},{7,5},{8,14},{9,15},{10,... | collective-permute-start | bytes 1572872 | tf_op jit(solution)/shard_map/ppermute | solution.py:40
  23.4 20.2 %collective-permute-start.4 = (bf16[64,4096]{1,0:T(8,128)(2,1)S(1)}, bf16[64,4096]{1,0:T(8,128)(2,1)S(1)}, u32[]{:S(2)}, u32[]{:S(2)}) collective-permute-start(bf16[64,4096]{1,0:T(8,128)(2,1)S(1)} %gate.9.refs_0_), channel_id=1, source_target_pairs={{0,2},{1,3},{2,4},{3,5},{4,6},{5,7},{6,0},{7,1},{8,10},{9,11},{10,... | collective-permute-start | bytes 1572872 | tf_op jit(solution)/shard_map/ppermute | solution.py:40
  33.6 10.4 %collective-permute-start.14 = (bf16[64,4096]{1,0:T(8,128)(2,1)S(1)}, bf16[64,4096]{1,0:T(8,128)(2,1)S(1)}, u32[]{:S(2)}, u32[]{:S(2)}) collective-permute-start(bf16[64,4096]{1,0:T(8,128)(2,1)S(1)} %join.1.refs_2_), channel_id=1, source_target_pairs={{0,1},{1,0},{2,3},{3,2},{4,5},{5,4},{6,7},{7,6},{8,9},{9,8},{10,11... | collective-permute-start | bytes 1572872 | tf_op jit(solution)/shard_map/ppermute | solution.py:40
  33.7 14.3 %collective-permute-start.13 = (bf16[64,4096]{1,0:T(8,128)(2,1)S(1)}, bf16[64,4096]{1,0:T(8,128)(2,1)S(1)}, u32[]{:S(2)}, u32[]{:S(2)}) collective-permute-start(bf16[64,4096]{1,0:T(8,128)(2,1)S(1)} %join.1.refs_2_), channel_id=1, source_target_pairs={{0,8},{1,9},{2,10},{3,11},{4,12},{5,13},{6,14},{7,15},{8,0},{9,1},... | collective-permute-start | bytes 1572872 | tf_op jit(solution)/shard_map/ppermute | solution.py:40
  54.7 11.0 %collective-permute-start.16 = (f32[16,2048]{1,0:T(8,128)S(1)}, f32[16,2048]{1,0:T(8,128)S(1)}, u32[]{:S(2)}, u32[]{:S(2)}) collective-permute-start(f32[16,2048]{1,0:T(8,128)S(1)} %get-tuple-element.51), channel_id=1, source_target_pairs={{16,32},{32,16},{48,64},{64,48},{80,96},{96,80},{17,33},{33,17},{4... | collective-permute-start | bytes 393224 | tf_op jit(solution)/shard_map/ppermute | solution.py:471
  66.7 9.8 %collective-permute-start.18 = (bf16[16,2048]{1,0:T(8,128)(2,1)S(1)}, bf16[16,2048]{1,0:T(8,128)(2,1)S(1)}, u32[]{:S(2)}, u32[]{:S(2)}) collective-permute-start(bf16[16,2048]{1,0:T(8,128)(2,1)S(1)} %get-tuple-element.53), channel_id=1, source_target_pairs={{16,32},{32,16},{48,64},{64,48},{80,96},{96,80},{17,33},{33,17},{4... | collective-permute-start | bytes 196616 | tf_op jit(solution)/shard_map/ppermute | solution.py:474
  86.7 16.6 %collective-permute-start.25 = (bf16[64,4096]{1,0:T(8,128)(2,1)S(1)}, bf16[64,4096]{1,0:T(8,128)(2,1)S(1)}, u32[]{:S(2)}, u32[]{:S(2)}) collective-permute-start(bf16[64,4096]{1,0:T(8,128)(2,1)S(1)} %get-tuple-element.66), channel_id=1, source_target_pairs={{0,2},{1,3},{2,4},{3,5},{4,6},{5,7},{6,0},{7,1},{8,10},{9,11},{10,... | collective-permute-start | bytes 1572872 | tf_op jit(solution)/shard_map/ppermute | solution.py:40
  86.9 16.5 %collective-permute-start.26 = (bf16[64,4096]{1,0:T(8,128)(2,1)S(1)}, bf16[64,4096]{1,0:T(8,128)(2,1)S(1)}, u32[]{:S(2)}, u32[]{:S(2)}) collective-permute-start(bf16[64,4096]{1,0:T(8,128)(2,1)S(1)} %get-tuple-element.67), channel_id=1, source_target_pairs={{0,6},{1,7},{2,0},{3,1},{4,2},{5,3},{6,4},{7,5},{8,14},{9,15},{10,... | collective-permute-start | bytes 1572872 | tf_op jit(solution)/shard_map/ppermute | solution.py:40
  88.8 15.1 %collective-permute-start.27 = (bf16[64,4096]{1,0:T(8,128)(2,1)S(1)}, bf16[64,4096]{1,0:T(8,128)(2,1)S(1)}, u32[]{:S(2)}, u32[]{:S(2)}) collective-permute-start(bf16[64,4096]{1,0:T(8,128)(2,1)S(1)} %get-tuple-element.62.refs_1_), channel_id=1, source_target_pairs={{0,8},{1,9},{2,10},{3,11},{4,12},{5,13},{6,14},{7,15},{8,0},{9,1},... | collective-permute-start | bytes 1572872 | tf_op jit(solution)/shard_map/ppermute | solution.py:40
  94.5 9.6 %collective-permute-start.24 = (bf16[64,4096]{1,0:T(8,128)(2,1)S(1)}, bf16[64,4096]{1,0:T(8,128)(2,1)S(1)}, u32[]{:S(2)}, u32[]{:S(2)}) collective-permute-start(bf16[64,4096]{1,0:T(8,128)(2,1)S(1)} %get-tuple-element.65), channel_id=1, source_target_pairs={{0,1},{1,0},{2,3},{3,2},{4,5},{5,4},{6,7},{7,6},{8,9},{9,8},{10,11... | collective-permute-start | bytes 1572872 | tf_op jit(solution)/shard_map/ppermute | solution.py:40
  103.2 11.6 %collective-permute-start.29 = (bf16[64,4096]{1,0:T(8,128)(2,1)S(1)}, bf16[64,4096]{1,0:T(8,128)(2,1)S(1)}, u32[]{:S(2)}, u32[]{:S(2)}) collective-permute-start(bf16[64,4096]{1,0:T(8,128)(2,1)S(1)} %get-tuple-element.77), channel_id=1, source_target_pairs={{0,1},{1,0},{2,3},{3,2},{4,5},{5,4},{6,7},{7,6},{8,9},{9,8},{10,11... | collective-permute-start | bytes 1572872 | tf_op jit(solution)/shard_map/ppermute | solution.py:40
  103.4 11.5 %collective-permute-start.30 = (bf16[64,4096]{1,0:T(8,128)(2,1)S(1)}, bf16[64,4096]{1,0:T(8,128)(2,1)S(1)}, u32[]{:S(2)}, u32[]{:S(2)}) collective-permute-start(bf16[64,4096]{1,0:T(8,128)(2,1)S(1)} %get-tuple-element.78), channel_id=1, source_target_pairs={{0,1},{1,0},{2,3},{3,2},{4,5},{5,4},{6,7},{7,6},{8,9},{9,8},{10,11... | collective-permute-start | bytes 1572872 | tf_op jit(solution)/shard_map/ppermute | solution.py:40
  103.8 11.0 %collective-permute-start.28 = (bf16[64,4096]{1,0:T(8,128)(2,1)S(1)}, bf16[64,4096]{1,0:T(8,128)(2,1)S(1)}, u32[]{:S(2)}, u32[]{:S(2)}) collective-permute-start(bf16[64,4096]{1,0:T(8,128)(2,1)S(1)} %get-tuple-element.69.refs_3_), channel_id=1, source_target_pairs={{0,1},{1,0},{2,3},{3,2},{4,5},{5,4},{6,7},{7,6},{8,9},{9,8},{10,11... | collective-permute-start | bytes 1572872 | tf_op jit(solution)/shard_map/ppermute | solution.py:40
  104.3 9.7 %collective-permute-start.32 = (bf16[64,2048]{1,0:T(8,128)(2,1)S(1)}, bf16[64,2048]{1,0:T(8,128)(2,1)S(1)}, u32[]{:S(2)}, u32[]{:S(2)}) collective-permute-start(bf16[64,2048]{1,0:T(8,128)(2,1)S(1)} %get-tuple-element.79), channel_id=1, source_target_pairs={{0,6},{1,7},{2,0},{3,1},{4,2},{5,3},{6,4},{7,5},{8,14},{9,15},{10,... | collective-permute-start | bytes 786440 | tf_op jit(solution)/shard_map/ppermute | solution.py:40
  104.4 10.4 %collective-permute-start.31 = (bf16[64,2048]{1,0:T(8,128)(2,1)S(1)}, bf16[64,2048]{1,0:T(8,128)(2,1)S(1)}, u32[]{:S(2)}, u32[]{:S(2)}) collective-permute-start(bf16[64,2048]{1,0:T(8,128)(2,1)S(1)} %get-tuple-element.75.refs_4_), channel_id=1, source_target_pairs={{0,2},{1,3},{2,4},{3,5},{4,6},{5,7},{6,0},{7,1},{8,10},{9,11},{10,... | collective-permute-start | bytes 786440 | tf_op jit(solution)/shard_map/ppermute | solution.py:40
  114.0 13.2 %collective-permute-start.33 = (bf16[64,4096]{1,0:T(8,128)(2,1)S(1)}, bf16[64,4096]{1,0:T(8,128)(2,1)S(1)}, u32[]{:S(2)}, u32[]{:S(2)}) collective-permute-start(bf16[64,4096]{1,0:T(8,128)(2,1)S(1)} %combine.6.refs_1_), channel_id=1, source_target_pairs={{0,8},{1,9},{2,10},{3,11},{4,12},{5,13},{6,14},{7,15},{8,0},{9,1},... | collective-permute-start | bytes 1572872 | tf_op jit(solution)/shard_map/ppermute | solution.py:40
  115.1 13.0 %collective-permute-start.34 = (bf16[64,4096]{1,0:T(8,128)(2,1)S(1)}, bf16[64,4096]{1,0:T(8,128)(2,1)S(1)}, u32[]{:S(2)}, u32[]{:S(2)}) collective-permute-start(bf16[64,4096]{1,0:T(8,128)(2,1)S(1)} %get-tuple-element.87), channel_id=1, source_target_pairs={{0,2},{1,3},{2,4},{3,5},{4,6},{5,7},{6,0},{7,1},{8,10},{9,11},{10,... | collective-permute-start | bytes 1572872 | tf_op jit(solution)/shard_map/ppermute | solution.py:40
  117.3 13.8 %collective-permute-start.35 = (bf16[64,4096]{1,0:T(8,128)(2,1)S(1)}, bf16[64,4096]{1,0:T(8,128)(2,1)S(1)}, u32[]{:S(2)}, u32[]{:S(2)}) collective-permute-start(bf16[64,4096]{1,0:T(8,128)(2,1)S(1)} %get-tuple-element.88), channel_id=1, source_target_pairs={{0,6},{1,7},{2,0},{3,1},{4,2},{5,3},{6,4},{7,5},{8,14},{9,15},{10,... | collective-permute-start | bytes 1572872 | tf_op jit(solution)/shard_map/ppermute | solution.py:40
  (20 other events, 203.5 us)
